TPU v7x, 128 devices: a whole 4x4x4 slice. The times are simulated.
128 devices in a mesh: section: 2 (over y_hi), dp: 4 (over z), shard: 16 (over y_lo, x, core).
Axes of the slice: x: 4, y: 4 (y_hi: 2, y_lo: 2; y = y_hi * 2 + y_lo), z: 4, core: 2. Of those that a mesh axis runs over, the one named last changes fastest.
Arguments:
- ends: bfloat16 [2, 12288, 1024], P('section', ('dp', 'shard')), may hold values from -6 to 6
- segment_ids: int32 [12288], P(('dp', 'shard')), may hold values from 0 to 24, as said below
- token_mask: int32 [12288], P(('dp', 'shard')), may hold values from 0 to 1, as said below
- ln1_gain: bfloat16 [2, 1024], P('section', 'shard'), may hold values from 0.5 to 1.5
- ln1_bias: bfloat16 [2, 1024], P('section', 'shard'), may hold values from -2 to 2
- w_qkv: bfloat16 [2, 1024, 3072], P('section', 'shard'), may hold values from -0.1875 to 0.1875
- b_query: bfloat16 [2, 1024], P('section', 'shard'), may hold values from -3 to 3
- b_value: bfloat16 [2, 1024], P('section', 'shard'), may hold values from -3 to 3
- w_out: bfloat16 [2, 1024, 1024], P('section', 'shard'), may hold values from -0.75 to 0.75
- b_out: bfloat16 [2, 1024], P('section', 'shard'), may hold values from -3 to 3
- ln2_gain: bfloat16 [2, 1024], P('section', 'shard'), may hold values from 0.5 to 1.5
- ln2_bias: bfloat16 [2, 1024], P('section', 'shard'), may hold values from -2 to 2
- w_up: bfloat16 [2, 1024, 4096], P('section', 'shard'), may hold values from -0.1875 to 0.1875
- b_up: bfloat16 [2, 4096], P('section', 'shard'), may hold values from -3 to 3
- w_down: bfloat16 [2, 4096, 1024], P('section', 'shard'), may hold values from -0.1875 to 0.1875
- b_down: bfloat16 [2, 1024], P('section', 'shard'), may hold values from -3 to 3
Outputs:
- section_out: bfloat16 [2, 12288, 1024], P('section', ('dp', 'shard'))
- section_grad: bfloat16 [2, 12288, 1024], P('section', ('dp', 'shard'))
- grad_ln1_gain: float32 [2, 1024], P('section', 'shard')
- grad_ln1_bias: float32 [2, 1024], P('section', 'shard')
- grad_w_qkv: float32 [2, 1024, 3072], P('section', 'shard')
- grad_b_query: float32 [2, 1024], P('section', 'shard')
- grad_b_value: float32 [2, 1024], P('section', 'shard')
- grad_w_out: float32 [2, 1024, 1024], P('section', 'shard')
- grad_b_out: float32 [2, 1024], P('section', 'shard')
- grad_ln2_gain: float32 [2, 1024], P('section', 'shard')
- grad_ln2_bias: float32 [2, 1024], P('section', 'shard')
- grad_w_up: float32 [2, 1024, 4096], P('section', 'shard')
- grad_b_up: float32 [2, 4096], P('section', 'shard')
- grad_w_down: float32 [2, 4096, 1024], P('section', 'shard')
- grad_b_down: float32 [2, 1024], P('section', 'shard')
Inputs may be any that keep to these rules, and one draw needn't show every extreme that they name: `segment_ids`: within each slot of 96 rows the ids start at 0 and never fall; a sequence never crosses a slot and starts at a row whose place in the slot is a multiple of 4; only the padding run that ends a slot may start elsewhere; the padding rows that end a slot share the id after the slot's last sequence. Groups along dp carry different amounts of padding, at most 48 rows a slot. `token_mask`: 1 on rows of sequences and 0 on the padding rows at the end of a slot.
All inputs are finite; a program needn't handle non-finite values.
Results may differ from a plain program's by a relative error of at most 0.025.
Values may be sent and summed in bfloat16 or wider, within the bound.
A program may use at most 384 MiB of HBM per device.

v0:
```python
import functools
import math

import jax
import jax.numpy as jnp
from jax import lax
from jax.sharding import PartitionSpec as P

HEADS = 16
SLOT = 96
MICRO = 2


norm_eps = 1e-05
masked_score = -1e30


def sent_together(arrays, axis, dim, along):
    widths = [math.prod(a.shape[along:]) for a in arrays]
    both = jnp.concatenate(
        [a.reshape(*a.shape[:along], w) for a, w in zip(arrays, widths)], axis=along
    )
    filled = lax.all_gather(both, axis, axis=dim, tiled=True)
    pieces = jnp.split(filled, [sum(widths[:k]) for k in range(1, len(widths))], axis=along)
    return tuple(
        (b.reshape(*filled.shape[:along], *a.shape[along:]) for a, b in zip(arrays, pieces))
    )


def shifted(value, axis, steps):
    count = lax.axis_size(axis)
    leading, last = (max(0, -steps), min(count, count - steps))
    return lax.ppermute(value, axis, [(source, source + steps) for source in range(leading, last)])


def in_one_piece(arrays, axis, dim, along):
    widths = [math.prod(a.shape[along:]) for a in arrays]
    both = jnp.concatenate(
        [a.reshape(*a.shape[:along], w) for a, w in zip(arrays, widths)], axis=along
    )
    filled = lax.psum_scatter(both, axis, scatter_dimension=dim, tiled=True)
    pieces = jnp.split(filled, [sum(widths[:k]) for k in range(1, len(widths))], axis=along)
    return tuple(
        (b.reshape(*filled.shape[:along], *a.shape[along:]) for a, b in zip(arrays, pieces))
    )


def normalize(values, norm_gain, norm_bias):
    row_mean = jnp.mean(values, axis=-1, keepdims=True)
    centered = values - row_mean
    variance = jnp.mean(centered * centered, axis=-1, keepdims=True)
    return centered * lax.rsqrt(variance + norm_eps) * norm_gain + norm_bias


def dot_rows(left, right):
    return lax.dot_general(
        left, right, (((0,), (0,)), ((), ())), preferred_element_type=jnp.float32
    )


def dot_back(left, right):
    return lax.dot_general(
        left, right, (((1,), (1,)), ((), ())), preferred_element_type=jnp.float32
    )


def split_heads(values):
    return values.reshape(values.shape[0], HEADS, values.shape[1] // HEADS)


def head_scores(queries, keys_part, segment):
    score_scale = (queries.shape[1] // HEADS) ** (-0.5)
    positions = jnp.arange(segment.shape[0])
    slot_of = positions // SLOT
    allowed = (
        (segment[:, None] == segment[None, :])
        & (positions[None, :] <= positions[:, None])
        & (slot_of[:, None] == slot_of[None, :])
    )
    raw_scores = (
        jnp.einsum(
            "qhd,khd->hqk",
            split_heads(queries),
            split_heads(keys_part),
            preferred_element_type=jnp.float32,
        )
        * score_scale
    )
    return jnp.where(allowed[None], raw_scores, masked_score)


def forward_slot(rows_in, segment, gathered):
    (
        gain_one,
        bias_one,
        w_joint,
        bias_query,
        bias_value,
        w_mix,
        bias_mix,
        gain_two,
        bias_two,
        w_grow,
        bias_grow,
        w_shrink,
        bias_shrink,
    ) = gathered
    model_width = rows_in.shape[1]
    inputs = rows_in.astype(jnp.float32)
    normed = normalize(inputs, gain_one.astype(jnp.float32), bias_one.astype(jnp.float32)).astype(
        jnp.bfloat16
    )
    projected = jnp.dot(normed, w_joint, preferred_element_type=jnp.float32)
    queries = (projected[:, :model_width] + bias_query.astype(jnp.float32)).astype(jnp.bfloat16)
    keys_part = projected[:, model_width : 2 * model_width].astype(jnp.bfloat16)
    values_part = (projected[:, 2 * model_width :] + bias_value.astype(jnp.float32)).astype(
        jnp.bfloat16
    )
    scores = head_scores(queries, keys_part, segment)
    row_top = jnp.max(scores, axis=-1, keepdims=True)
    exponent = jnp.exp(scores - row_top)
    row_total = jnp.sum(exponent, axis=-1, keepdims=True)
    attn_probs = exponent / row_total
    row_lse = row_top + jnp.log(row_total)
    attended = (
        jnp.einsum(
            "hqk,khd->qhd",
            attn_probs.astype(jnp.bfloat16),
            split_heads(values_part),
            preferred_element_type=jnp.float32,
        )
        .reshape(rows_in.shape)
        .astype(jnp.bfloat16)
    )
    branch = jnp.dot(attended, w_mix, preferred_element_type=jnp.float32) + bias_mix.astype(
        jnp.float32
    )
    middle = inputs + branch
    second = normalize(middle, gain_two.astype(jnp.float32), bias_two.astype(jnp.float32)).astype(
        jnp.bfloat16
    )
    before = jnp.dot(second, w_grow, preferred_element_type=jnp.float32) + bias_grow.astype(
        jnp.float32
    )
    hidden = jax.nn.gelu(before, approximate=True).astype(jnp.bfloat16)
    update = jnp.dot(hidden, w_shrink, preferred_element_type=jnp.float32) + bias_shrink.astype(
        jnp.float32
    )
    joined = jnp.concatenate([queries, keys_part, values_part], axis=1)
    record = (rows_in, joined, row_lse, attended, middle, second, before, hidden)
    return ((middle + update).astype(jnp.bfloat16), record)


def forward_skip(rows_in, segment, gathered):
    slot_rows, model_width = rows_in.shape
    hidden_width = gathered[9].shape[1]
    record = (
        jnp.zeros((slot_rows, model_width), jnp.bfloat16),
        jnp.zeros((slot_rows, 3 * model_width), jnp.bfloat16),
        jnp.zeros((HEADS, slot_rows, 1), jnp.float32),
        jnp.zeros((slot_rows, model_width), jnp.bfloat16),
        jnp.zeros((slot_rows, model_width), jnp.float32),
        jnp.zeros((slot_rows, model_width), jnp.bfloat16),
        jnp.zeros((slot_rows, hidden_width), jnp.float32),
        jnp.zeros((slot_rows, hidden_width), jnp.bfloat16),
    )
    return (jnp.zeros((slot_rows, model_width), jnp.bfloat16), record)


def backward_slot(grad_out, record, segment, gathered):
    (
        gain_one,
        bias_one,
        w_joint,
        bias_query,
        bias_value,
        w_mix,
        bias_mix,
        gain_two,
        bias_two,
        w_grow,
        bias_grow,
        w_shrink,
        bias_shrink,
    ) = gathered
    rows_in, joined, row_lse, attended, middle, second, before, hidden = record
    model_width = rows_in.shape[1]
    grad_update = grad_out.astype(jnp.bfloat16)
    grad_bias_shrink = jnp.sum(grad_update.astype(jnp.float32), axis=0)
    grad_w_shrink = dot_rows(hidden, grad_update)
    grad_hidden = dot_back(grad_update, w_shrink)
    _, gelu_pull = jax.vjp(functools.partial(jax.nn.gelu, approximate=True), before)
    grad_before = gelu_pull(grad_hidden)[0].astype(jnp.bfloat16)
    grad_bias_grow = jnp.sum(grad_before.astype(jnp.float32), axis=0)
    grad_w_grow = dot_rows(second, grad_before)
    grad_second = dot_back(grad_before, w_grow)
    _, second_pull = jax.vjp(
        normalize, middle, gain_two.astype(jnp.float32), bias_two.astype(jnp.float32)
    )
    grad_mid_norm, grad_gain_two, grad_bias_two = second_pull(grad_second)
    grad_middle = grad_out + grad_mid_norm
    grad_branch = grad_middle.astype(jnp.bfloat16)
    grad_bias_mix = jnp.sum(grad_branch.astype(jnp.float32), axis=0)
    grad_w_mix = dot_rows(attended, grad_branch)
    grad_attended = dot_back(grad_branch, w_mix).astype(jnp.bfloat16)
    queries = joined[:, :model_width]
    keys_part = joined[:, model_width : 2 * model_width]
    values_part = joined[:, 2 * model_width :]
    score_scale = (model_width // HEADS) ** (-0.5)
    attn_probs = jnp.exp(head_scores(queries, keys_part, segment) - row_lse)
    grad_heads = split_heads(grad_attended)
    grad_probs = jnp.einsum(
        "qhd,khd->hqk", grad_heads, split_heads(values_part), preferred_element_type=jnp.float32
    )
    row_delta = jnp.sum(attn_probs * grad_probs, axis=-1, keepdims=True)
    grad_scores = (attn_probs * (grad_probs - row_delta)).astype(jnp.bfloat16)
    grad_query = (
        jnp.einsum(
            "hqk,khd->qhd", grad_scores, split_heads(keys_part), preferred_element_type=jnp.float32
        )
        * score_scale
    )
    grad_key = (
        jnp.einsum(
            "hqk,qhd->khd", grad_scores, split_heads(queries), preferred_element_type=jnp.float32
        )
        * score_scale
    )
    grad_value = jnp.einsum(
        "hqk,qhd->khd",
        attn_probs.astype(jnp.bfloat16),
        grad_heads,
        preferred_element_type=jnp.float32,
    )
    grad_joined = jnp.concatenate(
        [v.reshape(rows_in.shape) for v in (grad_query, grad_key, grad_value)], axis=1
    ).astype(jnp.bfloat16)
    grad_bias_query = jnp.sum(grad_joined[:, :model_width].astype(jnp.float32), axis=0)
    grad_bias_value = jnp.sum(grad_joined[:, 2 * model_width :].astype(jnp.float32), axis=0)
    inputs = rows_in.astype(jnp.float32)
    normed_full, first_pull = jax.vjp(
        normalize, inputs, gain_one.astype(jnp.float32), bias_one.astype(jnp.float32)
    )
    grad_w_joint = dot_rows(normed_full.astype(jnp.bfloat16), grad_joined)
    grad_normed = dot_back(grad_joined, w_joint)
    grad_in_norm, grad_gain_one, grad_bias_one = first_pull(grad_normed)
    grad_in = grad_middle + grad_in_norm
    grad_terms = (
        grad_gain_one,
        grad_bias_one,
        grad_w_joint,
        grad_bias_query,
        grad_bias_value,
        grad_w_mix,
        grad_bias_mix,
        grad_gain_two,
        grad_bias_two,
        grad_w_grow,
        grad_bias_grow,
        grad_w_shrink,
        grad_bias_shrink,
    )
    return (grad_in, grad_terms)


def backward_skip(grad_out, record, segment, gathered):
    return (
        jnp.zeros(grad_out.shape, jnp.float32),
        jax.tree.map(lambda v: jnp.zeros(v.shape, jnp.float32), gathered),
    )


def on_device(
    ends,
    segment_ids,
    token_mask,
    ln1_gain,
    ln1_bias,
    w_qkv,
    b_query,
    b_value,
    w_out,
    b_out,
    ln2_gain,
    ln2_bias,
    w_up,
    b_up,
    w_down,
    b_down,
):
    fetched = (
        *sent_together(
            (ln1_gain, ln1_bias, w_qkv, b_query, b_value, w_out, b_out, ln2_gain, ln2_bias, w_up),
            "shard",
            1,
            2,
        ),
        *sent_together((b_up, w_down), "shard", 1, 2),
        lax.all_gather(b_down, "shard", axis=1, tiled=True),
    )
    gathered = tuple((v[0] for v in fetched))
    section_index = lax.axis_index("section")
    first_section = section_index == 0
    tok_rows, model_width = (ends.shape[1], ends.shape[2])
    slot_rows = tok_rows // MICRO
    local_rows = ends[0].reshape(MICRO, slot_rows, model_width)
    seg_rows = segment_ids.reshape(MICRO, slot_rows)
    arrived = jnp.zeros((slot_rows, model_width), jnp.bfloat16)
    produced_all = []
    records = []
    for tick_index in range(MICRO + 1):
        own_micro = min(tick_index, MICRO - 1)
        prior_micro = max(tick_index - 1, 0)
        rows_now = jnp.where(first_section, local_rows[own_micro], arrived)
        seg_now = jnp.where(first_section, seg_rows[own_micro], seg_rows[prior_micro])
        active = jnp.where(first_section, tick_index < MICRO, tick_index >= 1)
        produced, record = lax.cond(active, forward_slot, forward_skip, rows_now, seg_now, gathered)
        produced_all.append(produced)
        records.append(record)
        if tick_index < MICRO:
            arrived = shifted(produced, "section", 1)
    section_out = lax.dynamic_slice_in_dim(jnp.stack(produced_all), section_index, MICRO, 0)
    section_out = section_out.reshape(tok_rows, model_width)[None]
    refetched = (
        *sent_together(
            (ln1_gain, ln1_bias, w_qkv, b_query, b_value, w_out, b_out, ln2_gain, ln2_bias, w_up),
            "shard",
            1,
            2,
        ),
        *sent_together((b_up, w_down), "shard", 1, 2),
        lax.all_gather(b_down, "shard", axis=1, tiled=True),
    )
    backward_weights = tuple((v[0] for v in refetched))
    stacked_records = jax.tree.map(lambda *v: jnp.stack(v), *records)
    cot_rows = local_rows.astype(jnp.float32) * token_mask.reshape(MICRO, slot_rows)[
        :, :, None
    ].astype(jnp.float32)
    incoming = jnp.zeros((slot_rows, model_width), jnp.bfloat16)
    totals = jax.tree.map(lambda v: jnp.zeros(v.shape, jnp.float32), backward_weights)
    back_all = []
    for tick_index in range(MICRO + 1):
        own_micro = min(tick_index, MICRO - 1)
        prior_micro = max(tick_index - 1, 0)
        grad_now = jnp.where(first_section, incoming.astype(jnp.float32), cot_rows[own_micro])
        seg_now = jnp.where(first_section, seg_rows[prior_micro], seg_rows[own_micro])
        record_tick = jnp.where(first_section, prior_micro, min(tick_index + 1, MICRO))
        record = jax.tree.map(lambda v: v[record_tick], stacked_records)
        active = jnp.where(first_section, tick_index >= 1, tick_index < MICRO)
        grad_in, grad_terms = lax.cond(
            active, backward_slot, backward_skip, grad_now, record, seg_now, backward_weights
        )
        totals = jax.tree.map(jnp.add, totals, grad_terms)
        sent_grad = grad_in.astype(jnp.bfloat16)
        back_all.append(sent_grad)
        if tick_index < MICRO:
            incoming = shifted(sent_grad, "section", -1)
    section_grad = lax.dynamic_slice_in_dim(jnp.stack(back_all), 1 - section_index, MICRO, 0)
    section_grad = section_grad.reshape(tok_rows, model_width)[None]
    shard_sums = (
        lax.psum_scatter(
            totals[0].astype(jnp.bfloat16), "shard", scatter_dimension=0, tiled=True
        ).astype(jnp.float32),
        *tuple(
            (
                part.astype(jnp.float32)
                for part in in_one_piece(
                    (
                        totals[1].astype(jnp.bfloat16),
                        totals[2].astype(jnp.bfloat16),
                        totals[3].astype(jnp.bfloat16),
                        totals[4].astype(jnp.bfloat16),
                        totals[5].astype(jnp.bfloat16),
                        totals[6].astype(jnp.bfloat16),
                        totals[7].astype(jnp.bfloat16),
                        totals[8].astype(jnp.bfloat16),
                        totals[9].astype(jnp.bfloat16),
                    ),
                    "shard",
                    0,
                    1,
                )
            )
        ),
        *tuple(
            (
                part.astype(jnp.float32)
                for part in in_one_piece(
                    (totals[10].astype(jnp.bfloat16), totals[11].astype(jnp.bfloat16)),
                    "shard",
                    0,
                    1,
                )
            )
        ),
        lax.psum_scatter(
            totals[12].astype(jnp.bfloat16), "shard", scatter_dimension=0, tiled=True
        ).astype(jnp.float32),
    )
    finals = (
        lax.psum(shard_sums[0].astype(jnp.bfloat16), "dp").astype(jnp.float32),
        lax.psum(shard_sums[1].astype(jnp.bfloat16), "dp").astype(jnp.float32),
        lax.psum(shard_sums[2].astype(jnp.bfloat16), "dp").astype(jnp.float32),
        lax.psum(shard_sums[3].astype(jnp.bfloat16), "dp").astype(jnp.float32),
        lax.psum(shard_sums[4].astype(jnp.bfloat16), "dp").astype(jnp.float32),
        lax.psum(shard_sums[5].astype(jnp.bfloat16), "dp").astype(jnp.float32),
        lax.psum(shard_sums[6].astype(jnp.bfloat16), "dp").astype(jnp.float32),
        lax.psum(shard_sums[7].astype(jnp.bfloat16), "dp").astype(jnp.float32),
        lax.psum(shard_sums[8].astype(jnp.bfloat16), "dp").astype(jnp.float32),
        lax.psum(shard_sums[9].astype(jnp.bfloat16), "dp").astype(jnp.float32),
        lax.psum(shard_sums[10].astype(jnp.bfloat16), "dp").astype(jnp.float32),
        lax.psum(shard_sums[11].astype(jnp.bfloat16), "dp").astype(jnp.float32),
        lax.psum(shard_sums[12].astype(jnp.bfloat16), "dp").astype(jnp.float32),
    )
    outputs = [v[None] for v in finals]
    return (
        section_out,
        section_grad,
        outputs[0],
        outputs[1],
        outputs[2],
        outputs[3],
        outputs[4],
        outputs[5],
        outputs[6],
        outputs[7],
        outputs[8],
        outputs[9],
        outputs[10],
        outputs[11],
        outputs[12],
    )


def solution(mesh):
    in_specs = (
        P("section", ("dp", "shard"), None),
        P(("dp", "shard")),
        P(("dp", "shard")),
        P("section", "shard"),
        P("section", "shard"),
        P("section", "shard", None),
        P("section", "shard"),
        P("section", "shard"),
        P("section", "shard", None),
        P("section", "shard"),
        P("section", "shard"),
        P("section", "shard"),
        P("section", "shard", None),
        P("section", "shard"),
        P("section", "shard", None),
        P("section", "shard"),
    )
    out_specs = (
        P("section", ("dp", "shard"), None),
        P("section", ("dp", "shard"), None),
        P("section", "shard"),
        P("section", "shard"),
        P("section", "shard", None),
        P("section", "shard"),
        P("section", "shard"),
        P("section", "shard", None),
        P("section", "shard"),
        P("section", "shard"),
        P("section", "shard"),
        P("section", "shard", None),
        P("section", "shard"),
        P("section", "shard", None),
        P("section", "shard"),
    )
    return jax.shard_map(
        on_device, mesh=mesh, in_specs=in_specs, out_specs=out_specs, check_vma=False
    )
```

profile of v0, /device:TPU:0, one launch (start us, length us, event | category | flops | bytes accessed | tf_op | source)
XLA Modules:
  0.0 784.5 jit_solution(9688213848455728598)
XLA Ops:
  15.6 31.1 %all-reduce = bf16[1024]{0:T(1024)(128)(2,1)S(1)} all-reduce(bf16[1024]{0:T(1024)(128)(2,1)S(1)} %dynamic-update-slice), channel_id=1, replica_groups=mesh['section'=2,'dp'=4,'shard'=16] {'shard'}, use_global_device_ids=true, to_apply=%add | all-reduce | flops 1024 | bytes 4096 | tf_op jit(solution)/shard_map/squeeze | solution.py:301
  51.0 19.3 %all-gather.5.cloned.1.call-done = bf16[1,4096,1025]{2,1,0:T(8,128)(2,1)} async-done(((bf16[1,256,1025]{2,1,0:T(8,128)(2,1)}), bf16[1,4096,1025]{2,1,0:T(8,128)(2,1)}) %all-gather.5.cloned.1.call-update) | async-done | bytes 8396816 | tf_op jit(solution)/shard_map/all_gather | solution.py:23
  71.9 12.4 %slice_bitcast_fusion = bf16[4096,1024]{1,0:T(8,128)(2,1)} fusion(bf16[1,4096,1025]{2,1,0:T(8,128)(2,1)} %all-gather.5.cloned.1.call-done), kind=kLoop, calls=%fused_computation.317 | loop fusion | bytes 16777216 | tf_op jit(solution)/shard_map/squeeze | solution.py:301
  84.3 81.4 %all-gather.3.cloned.1.call-done = bf16[1,1024,8199]{2,1,0:T(8,128)(2,1)} async-done(((bf16[1,64,8199]{2,1,0:T(8,128)(2,1)}), bf16[1,1024,8199]{2,1,0:T(8,128)(2,1)}) %all-gather.3.cloned.1.call-update) | async-done | bytes 16791568 | tf_op jit(solution)/shard_map/all_gather | solution.py:23
  168.4 8.7 %slice_bitcast_fusion.2 = bf16[1024,3072]{1,0:T(8,128)(2,1)} fusion(bf16[1,1024,8199]{2,1,0:T(8,128)(2,1)} %all-gather.3.cloned.1.call-done), kind=kLoop, calls=%fused_computation.319 | loop fusion | bytes 12582912 | tf_op jit(solution)/shard_map/squeeze | solution.py:301
  179.7 11.9 %slice_bitcast_fusion.1 = bf16[1024,4096]{1,0:T(8,128)(2,1)} fusion(bf16[1,1024,8199]{2,1,0:T(8,128)(2,1)} %all-gather.3.cloned.1.call-done), kind=kLoop, calls=%fused_computation.318 | loop fusion | bytes 16777216 | tf_op jit(solution)/shard_map/squeeze | solution.py:301
  191.7 29.6 %conditional.4 = (bf16[96,1024]{1,0:T(8,128)(2,1)}, bf16[1,96,1024]{2,1,0:T(8,128)(2,1)}, bf16[1,96,1024]{2,1,0:T(8,128)(2,1)S(1)}, bf16[1,96,3072]{2,1,0:T(8,12...) conditional(s32[]{:T(128)} %convert_element_type.618, () %tuple.97, ...), branch_computations={%region_0.1_spmd, %region_1.8_spmd} | conditional | flops 2467881216 | bytes 74329032 | solution.py:317
  192.1 4.0 fusion.22
  205.0 6.3 convolution_add_fusion
  211.3 3.9 fusion.11
  229.0 5.0 fusion.245
  239.9 2.9 fusion.296
  243.8 6.3 convolution_add_fusion.6
  251.6 3.3 fusion.211
  254.9 5.8 collective-permute-start.1
  261.5 3.2 collective-permute-done.1
  264.8 4.1 conditional.5
  280.0 4.6 pad_maximum_fusion.7
  290.0 36.8 %conditional.6 = (f32[1024]{0:T(1024)S(1)}, f32[1024]{0:T(1024)S(1)}, f32[1024,3072]{1,0:T(8,128)}, f32[1024]{0:T(1024)S(1)}, f32[1024]{0:T(1024)S(1)}, /*index=...) conditional(s32[]{:T(128)} %convert_element_type.639, ...), branch_computations={%region_22.23_spmd, %region_23.42_spmd} | conditional | flops 4947333120 | bytes 162286016 | solution.py:350
  290.0 6.1 broadcast.1163
  297.8 7.8 broadcast.1165
  310.1 7.8 broadcast.1167.clone
  330.5 57.7 %collective-permute-done.2 = bf16[96,1024]{1,0:T(8,128)(2,1)S(1)} collective-permute-done((bf16[96,1024]{1,0:T(8,128)(2,1)}, bf16[96,1024]{1,0:T(8,128)(2,1)S(1)}, u32[]{:S(2)}, u32[]{:S(2)}) %collective-permute-start.2) | collective-permute-done | bytes 196640 | tf_op jit(solution)/shard_map/ppermute | solution.py:33
  388.9 9.0 %convert_reduce_fusion.14 = (f32[4096]{0:T(1024)}, bf16[96,4096]{1,0:T(8,128)(2,1)S(1)}) fusion(f32[3,96,4096]{2,1,0:T(8,128)} %pad_maximum_fusion.7, s32[]{:T(128)S(6)} %select_n.230, bf16[96,1024]{1,0:T(8,128)(2,1)S(1)} %get-tuple-element.1016, bf16[1,4096,1025]{2,1,0:T(8,128)(2,1)} %all-gather.5.cloned.1.call-done), kind=kOutput, calls=%fused_computation.347 | convolution fusion | flops 813953024 | bytes 10960900 | tf_op jit(solution)/shard_map/cond/branch_1_fun/dot_general | solution.py:62
  398.0 7.8 multiply_reduce_fusion.11
  406.8 2.8 convolution_convert_fusion.8
  411.7 7.0 fusion.232
  423.1 9.3 %fusion.212 = f32[4096,1024]{0,1:T(8,128)} fusion(bf16[96,1024]{1,0:T(8,128)(2,1)S(1)} %copy-done.63, bf16[3,96,4096]{2,1,0:T(8,128)(2,1)} %pad_maximum_fusion.8, s32[]{:T(128)S(6)} %select_n.230), kind=kOutput, calls=%fused_computation.370 | convolution fusion | flops 805306368 | bytes 17760260 | tf_op jit(solution)/shard_map/cond/branch_1_fun/dot_general | solution.py:56
  433.2 56.3 %conditional.7 = (f32[1024]{0:T(1024)S(1)}, f32[1024]{0:T(1024)S(1)}, f32[1024,3072]{1,0:T(8,128)}, f32[1024]{0:T(1024)S(1)}, f32[1024]{0:T(1024)S(1)}, /*index=...) conditional(s32[]{:T(128)} %convert_element_type.618, ...), branch_computations={%region_51.52_spmd, %region_52.71_spmd} | conditional | flops 4947529728 | bytes 162876336 | solution.py:350
  437.8 7.9 %convert_reduce_fusion.8 = (f32[4096]{0:T(1024)}, bf16[96,4096]{1,0:T(8,128)(2,1)S(1)}) fusion(f32[3,96,4096]{2,1,0:T(8,128)} %get-tuple-element.596, s32[]{:T(128)S(6)} %select_n.203, bf16[4096,1024]{1,0:T(8,128)(2,1)} %get-tuple-element.595, f32[96,1024]{1,0:T(8,128)S(1)} %get-tuple-element.1008), kind=kOutput, calls=%fused_computation.225 | convolution fusion | flops 814051328 | bytes 11157508 | tf_op jit(solution)/shard_map/cond/branch_1_fun/dot_general | solution.py:62
  445.6 3.4 multiply_reduce_fusion.7
  451.7 4.6 copy.173
  460.4 3.1 fusion.152
  465.3 7.5 fusion.154
  473.7 9.1 %fusion.158 = f32[1024,4096]{1,0:T(8,128)} fusion(bf16[96,4096]{1,0:T(8,128)(2,1)S(1)} %copy-done.31, bf16[3,96,1024]{2,1,0:T(8,128)(2,1)} %get-tuple-element.605, s32[]{:T(128)S(6)} %select_n.203), kind=kOutput, calls=%fused_computation.274 | convolution fusion | flops 805306368 | bytes 17760260 | tf_op jit(solution)/shard_map/cond/branch_1_fun/dot_general | solution.py:56
  485.8 3.5 fusion.138
  491.0 15.3 %add_convert_fusion.6 = bf16[4096,1024]{0,1:T(8,128)(2,1)} fusion(f32[4096,1024]{0,1:T(8,128)S(1)} %get-tuple-element.942, f32[4096,1024]{0,1:T(8,128)} %get-tuple-element.940, f32[4096,1024]{0,1:T(8,128)} %fusion.212), kind=kLoop, calls=%fused_computation.313 | loop fusion | flops 12582912 | bytes 58720256 | tf_op jit(solution)/shard_map/convert_element_type | solution.py:389
  506.3 9.5 %pad_maximum_fusion.6 = bf16[4096,1025]{0,1:T(8,128)(2,1)} fusion(bf16[4096,1024]{0,1:T(8,128)(2,1)} %add_convert_fusion.6, bf16[4096,1]{0,1:T(2,128)(2,1)S(1)} %reshape.1260), kind=kLoop, calls=%fused_computation.316 | loop fusion | flops 16793600 | bytes 16793600 | tf_op jit(solution)/shard_map/concatenate | solution.py:38
  518.9 7.6 fusion.241
  526.5 9.4 %fusion.247 = f32[1024,4096]{1,0:T(8,128)} fusion(bf16[96,4096]{1,0:T(8,128)(2,1)S(1)} %copy-done.65, bf16[3,96,1024]{2,1,0:T(8,128)(2,1)} %pad_maximum_fusion.15, s32[]{:T(128)S(6)} %select_n.230), kind=kOutput, calls=%fused_computation.453 | convolution fusion | flops 805306368 | bytes 17760260 | tf_op jit(solution)/shard_map/cond/branch_1_fun/dot_general | solution.py:56
  536.6 4.9 add_convert_fusion.9
  541.5 2.9 copy.179
  545.9 17.0 %add_convert_fusion.8 = bf16[1024,3072]{1,0:T(8,128)(2,1)} fusion(f32[1024,3072]{1,0:T(8,128)} %get-tuple-element.697, f32[1024,3072]{1,0:T(8,128)} %get-tuple-element.696, f32[1024,3072]{1,0:T(8,128)} %fusion.241), kind=kLoop, calls=%fused_computation.315 | loop fusion | flops 9437184 | bytes 44040192 | tf_op jit(solution)/shard_map/convert_element_type | solution.py:370
  565.8 15.8 %add_convert_fusion.7 = bf16[1024,4096]{1,0:T(8,128)(2,1)} fusion(f32[1024,4096]{1,0:T(8,128)} %get-tuple-element.711, f32[1024,4096]{1,0:T(8,128)} %get-tuple-element.710, f32[1024,4096]{1,0:T(8,128)S(1)} %bitcast.490), kind=kLoop, calls=%fused_computation.314 | loop fusion | flops 12582912 | bytes 58720256 | tf_op jit(solution)/shard_map/convert_element_type | solution.py:377
  581.6 34.7 %concatenate.46 = bf16[1024,8198]{1,0:T(8,128)(2,1)} concatenate(bf16[1024,1]{1,0:T(8,128)(2,1)S(1)} %reshape.1276, bf16[1024,3072]{1,0:T(8,128)(2,1)} %add_convert_fusion.8, bf16[1024,1]{1,0:T(8,128)(2,1)S(1)} %reshape.1277, bf16[1024,1]{1,0:T(8,128)(2,1)S(1)} %reshape.1278, bf16[1024,1024]{1,0:T(8,128)(2,1)S(1)} %copy.179, bf16[1024,1]{1,0:T(8,128)(2,1)S(1)} %reshape.1279, ...), dimensions={1} | concatenate | bytes 33579008 | tf_op jit(solution)/shard_map/concatenate | solution.py:38
  618.4 97.2 %reduce-scatter.3.cloned.1.call-done = bf16[64,8198]{1,0:T(8,128)(2,1)} async-done(((bf16[1024,8198]{1,0:T(8,128)(2,1)}), bf16[64,8198]{1,0:T(8,128)(2,1)}) %reduce-scatter.3.cloned.1.call-update) | async-done | bytes 1049360 | tf_op jit(solution)/shard_map/reduce_scatter | solution.py:41
  724.1 28.5 %all-reduce.3 = (bf16[1024]{0:T(1024)(128)(2,1)S(1)}, bf16[1024]{0:T(1024)(128)(2,1)S(1)}) all-reduce(bf16[1024]{0:T(1024)(128)(2,1)S(1)} %add_convert_fusion.20, bf16[1024]{0:T(1024)(128)(2,1)S(1)} %add_convert_fusion.13), channel_id=2, replica_groups=mesh['section'=2,'dp'=4,'shard'=16] {'shard'}, use_global_device_ids=true, to_apply=%region_72.73.clone | all-reduce | flops 2048 | bytes 8192
  755.5 10.9 %all-reduce.4 = (bf16[1,64]{1,0:T(2,128)(2,1)S(1)}, bf16[1,64]{1,0:T(2,128)(2,1)S(1)}, bf16[1,64]{1,0:T(2,128)(2,1)S(1)}, bf16[1,64]{1,0:T(2,128)(2,1)S(1)}, bf1...) all-reduce(bf16[1,64]{1,0:T(2,128)(2,1)S(1)} %dynamic-slice_bitcast, ...), channel_id=1, replica_groups=mesh['section'=2,'dp'=4,'shard'=16] {'dp'}, use_global_device_ids=true, to_apply=%region_73.74 | all-reduce | flops 768 | bytes 3072 | tf_op jit(solution)/shard_map/psum | solution.py:401
  (570 shorter events, 139.3 us)
Async XLA Ops:
  7.3 63.0 %all-gather.5.cloned.1.call-start = ((), (), s32[]{:S(2)}) async-start(), calls=%async_computation.3 | async-start | bytes 10027008 | tf_op jit(solution)/shard_map/all_gather | solution.py:23
  10.4 155.3 %all-gather.3.cloned.1.call-start = ((), (), s32[]{:S(2)}) async-start(), calls=%async_computation.2 | async-start | bytes 18104320 | tf_op jit(solution)/shard_map/all_gather | solution.py:23
  11.3 36.0 %copy-start.163 = (s32[192]{0:T(256)S(1)}, s32[192]{0:T(256)}, u32[]{:S(2)}) copy-start(s32[192]{0:T(256)} %param.26) | copy-start | bytes 2308
  11.3 36.6 %copy-start.162 = (s32[192]{0:T(256)S(1)}, s32[192]{0:T(256)}, u32[]{:S(2)}) copy-start(s32[192]{0:T(256)} %param.25) | copy-start | bytes 2308
  11.3 37.2 %copy-start.37 = (bf16[1,192,1024]{2,1,0:T(8,128)(2,1)S(1)}, bf16[1,192,1024]{2,1,0:T(8,128)(2,1)}, u32[]{:S(2)}) copy-start(bf16[1,192,1024]{2,1,0:T(8,128)(2,1)} %param.24) | copy-start | bytes 1179652
  14.0 602.4 %reduce-scatter.5.cloned.1.call-start = ((), (), s32[]{:S(2)}) async-start(), calls=%async_computation.5 | async-start | bytes 8982528 | tf_op jit(solution)/shard_map/reduce_scatter | solution.py:41
  48.5 143.2 %copy-start.147 = (s32[96]{0:T(128)}, s32[96]{0:T(128)S(1)}, u32[]{:S(2)}) copy-start(s32[96]{0:T(128)S(1)} %get-tuple-element.1064) | copy-start | bytes 1156
  168.3 23.3 %copy-start.110 = (bf16[1024]{0:T(1024)(128)(2,1)}, bf16[1024]{0:T(1024)(128)(2,1)S(1)}, u32[]{:S(2)}) copy-start(bf16[1024]{0:T(1024)(128)(2,1)S(1)} %get-tuple-element.963) | copy-start | bytes 6148
  168.4 56.7 %copy-start.106 = (bf16[1024]{0:T(1024)(128)(2,1)}, bf16[1024]{0:T(1024)(128)(2,1)S(1)}, u32[]{:S(2)}) copy-start(bf16[1024]{0:T(1024)(128)(2,1)S(1)} %get-tuple-element.961) | copy-start | bytes 6148
  168.4 57.3 %copy-start.108 = (bf16[1024]{0:T(1024)(128)(2,1)}, bf16[1024]{0:T(1024)(128)(2,1)S(1)}, u32[]{:S(2)}) copy-start(bf16[1024]{0:T(1024)(128)(2,1)S(1)} %get-tuple-element.962) | copy-start | bytes 6148
  168.4 57.9 %copy-start.104 = (bf16[1024]{0:T(1024)(128)(2,1)}, bf16[1024]{0:T(1024)(128)(2,1)S(1)}, u32[]{:S(2)}) copy-start(bf16[1024]{0:T(1024)(128)(2,1)S(1)} %get-tuple-element.959) | copy-start | bytes 6148
  168.4 121.0 %copy-start.95 = (bf16[1024]{0:T(1024)(128)(2,1)}, bf16[1024]{0:T(1024)(128)(2,1)S(1)}, u32[]{:S(2)}) copy-start(bf16[1024]{0:T(1024)(128)(2,1)S(1)} %get-tuple-element.965) | copy-start | bytes 6148
  179.7 109.6 %copy-start = (bf16[1024,1024]{1,0:T(8,128)(2,1)}, bf16[1024,1024]{1,0:T(8,128)(2,1)S(1)}, u32[]{:S(2)}) copy-start(bf16[1024,1024]{1,0:T(8,128)(2,1)S(1)} %slice_bitcast_fusion.3) | copy-start | bytes 6291460
  191.8 12.3 %copy-start.17 = (bf16[1,96,1024]{2,1,0:T(8,128)(2,1)}, bf16[1,96,1024]{2,1,0:T(8,128)(2,1)S(1)}, u32[]{:S(2)}) copy-start(bf16[1,96,1024]{2,1,0:T(8,128)(2,1)S(1)} %get-tuple-element.1096) | copy-start | bytes 589828 | tf_op jit(solution)/shard_map/cond
  204.7 13.0 %copy-start.5 = (f32[96,1024]{1,0:T(8,128)}, f32[96,1024]{1,0:T(8,128)S(1)}, u32[]{:S(2)}) copy-start(f32[96,1024]{1,0:T(8,128)S(1)} %get-tuple-element.1026) | copy-start | bytes 1179652 | tf_op jit(solution)/shard_map/cond
  221.3 12.8 %copy-start.33 = (bf16[1,96,4096]{2,1,0:T(8,128)(2,1)}, bf16[1,96,4096]{2,1,0:T(8,128)(2,1)S(1)}, u32[]{:S(2)}) copy-start(bf16[1,96,4096]{2,1,0:T(8,128)(2,1)S(1)} %get-tuple-element.687) | copy-start | bytes 2359300
  221.3 12.8 %copy-start.101 = (f32[1,16,96,1]{2,1,3,0:T(8,128)}, f32[1,16,96,1]{2,1,3,0:T(8,128)S(1)}, u32[]{:S(2)}) copy-start(f32[1,16,96,1]{2,1,3,0:T(8,128)S(1)} %get-tuple-element.677) | copy-start | bytes 18436
  221.3 6.4 collective-permute-start
  226.3 17.5 %copy-start.98 = (f32[1024]{0:T(1024)}, f32[1024]{0:T(1024)S(1)}, u32[]{:S(2)}) copy-start(f32[1024]{0:T(1024)S(1)} %convert_element_type.632) | copy-start | bytes 12292
  237.5 14.0 %slice-start.12 = ((s8[9437184]{0:T(1024)(128)(4,1)}), s8[4194304]{0:T(1024)(128)(4,1)S(1)}, s32[]{:S(2)}) async-start(s8[9437184]{0:T(1024)(128)(4,1)} %bitcast.497), calls=%async_computation.19 | async-start | bytes 8388608
  239.9 11.7 %slice-start.13 = ((s8[9437184]{0:T(1024)(128)(4,1)}), s8[4194304]{0:T(1024)(128)(4,1)S(1)}, s32[]{:S(2)}) async-start(s8[9437184]{0:T(1024)(128)(4,1)} %bitcast.497), calls=%async_computation.20 | async-start | bytes 8388608
  251.6 13.2 %copy-start.105 = (bf16[1024]{0:T(1024)(128)(2,1)S(1)}, bf16[1024]{0:T(1024)(128)(2,1)}, u32[]{:S(2)}) copy-start(bf16[1024]{0:T(1024)(128)(2,1)} %copy-done.104) | copy-start | bytes 6148
  251.6 13.2 %copy-start.107 = (bf16[1024]{0:T(1024)(128)(2,1)S(1)}, bf16[1024]{0:T(1024)(128)(2,1)}, u32[]{:S(2)}) copy-start(bf16[1024]{0:T(1024)(128)(2,1)} %copy-done.106) | copy-start | bytes 6148
  251.6 13.2 %copy-start.109 = (bf16[1024]{0:T(1024)(128)(2,1)S(1)}, bf16[1024]{0:T(1024)(128)(2,1)}, u32[]{:S(2)}) copy-start(bf16[1024]{0:T(1024)(128)(2,1)} %copy-done.108) | copy-start | bytes 6148
  251.6 13.2 %copy-start.111 = (bf16[1024]{0:T(1024)(128)(2,1)S(1)}, bf16[1024]{0:T(1024)(128)(2,1)}, u32[]{:S(2)}) copy-start(bf16[1024]{0:T(1024)(128)(2,1)} %copy-done.110) | copy-start | bytes 6148
  251.6 13.2 %copy-start.145 = (s32[96]{0:T(128)S(1)}, s32[96]{0:T(128)}, u32[]{:S(2)}) copy-start(s32[96]{0:T(128)} %get-tuple-element.1063) | copy-start | bytes 1156
  254.9 9.9 %collective-permute-start.1 = (bf16[96,1024]{1,0:T(8,128)(2,1)S(1)}, bf16[96,1024]{1,0:T(8,128)(2,1)S(1)}, u32[]{:S(2)}, u32[]{:S(2)}) collective-permute-start(bf16[96,1024]{1,0:T(8,128)(2,1)S(1)} %fusion.211), channel_id=1, source_target_pairs={{0,64},{1,65},{2,66},{3,67},{4,68},{5,69},{6,70},{7,71},{8,72},{9,... | collective-permute-start | bytes 589832 | tf_op jit(solution)/shard_map/ppermute | solution.py:33
  326.8 62.1 %copy-start.117 = (f32[1024]{0:T(1024)}, f32[1024]{0:T(1024)S(1)}, u32[]{:S(2)}) copy-start(f32[1024]{0:T(1024)S(1)} %get-tuple-element.692) | copy-start | bytes 12292
  326.8 61.4 %copy-start.8 = (f32[2,96,1024]{2,1,0:T(8,128)S(1)}, f32[2,96,1024]{2,1,0:T(8,128)}, u32[]{:S(2)}) copy-start(f32[2,96,1024]{2,1,0:T(8,128)} %copy-done.7) | copy-start | bytes 2359300
  326.8 61.4 %collective-permute-start.2 = (bf16[96,1024]{1,0:T(8,128)(2,1)}, bf16[96,1024]{1,0:T(8,128)(2,1)S(1)}, u32[]{:S(2)}, u32[]{:S(2)}) collective-permute-start(bf16[96,1024]{1,0:T(8,128)(2,1)} %get-tuple-element.690), channel_id=1, source_target_pairs={{64,0},{65,1},{66,2},{67,3},{68,4},{69,5},{70,6},{71,7},{72,8},{73... | collective-permute-start | bytes 589832 | tf_op jit(solution)/shard_map/ppermute | solution.py:33
  406.8 13.7 %copy-start.24 = (f32[96,1024]{1,0:T(8,128)}, f32[96,1024]{1,0:T(8,128)S(1)}, u32[]{:S(2)}) copy-start(f32[96,1024]{1,0:T(8,128)S(1)} %get-tuple-element.1014) | copy-start | bytes 1179652
  418.7 13.7 %copy-start.149 = (f32[96]{0:T(128)}, f32[96]{0:T(128)S(1)}, u32[]{:S(2)}) copy-start(f32[96]{0:T(128)S(1)} %get-tuple-element.1069) | copy-start | bytes 1156
  421.7 11.5 %copy-start.1 = (bf16[1024,1024]{1,0:T(8,128)(2,1)S(1)}, bf16[1024,1024]{1,0:T(8,128)(2,1)}, u32[]{:S(2)}) copy-start(bf16[1024,1024]{1,0:T(8,128)(2,1)} %copy-done) | copy-start | bytes 6291460
  421.7 10.7 %collective-permute-start.3 = (bf16[96,1024]{1,0:T(8,128)(2,1)S(1)}, bf16[96,1024]{1,0:T(8,128)(2,1)S(1)}, u32[]{:S(2)}, u32[]{:S(2)}) collective-permute-start(bf16[96,1024]{1,0:T(8,128)(2,1)S(1)} %add_convert_fusion.10), channel_id=1, source_target_pairs={{64,0},{65,1},{66,2},{67,3},{68,4},{69,5},{70,6},{71,7},{72,8},{73... | collective-permute-start | bytes 589832 | tf_op jit(solution)/shard_map/ppermute | solution.py:33
  437.5 11.7 %copy-start.15 = (f32[96,1024]{1,0:T(8,128)}, f32[96,1024]{1,0:T(8,128)S(1)}, u32[]{:S(2)}) copy-start(f32[96,1024]{1,0:T(8,128)S(1)} %get-tuple-element.1008) | copy-start | bytes 1179652 | tf_op jit(solution)/shard_map/cond
  489.5 16.8 %copy-start.3 = (f32[1024,1024]{0,1:T(8,128)}, f32[1024,1024]{0,1:T(8,128)S(1)}, u32[]{:S(2)}) copy-start(f32[1024,1024]{0,1:T(8,128)S(1)} %get-tuple-element.941) | copy-start | bytes 12582916
  489.6 16.8 %copy-start.69 = (bf16[1,96,1024]{2,1,0:T(8,128)(2,1)}, bf16[1,96,1024]{2,1,0:T(8,128)(2,1)S(1)}, u32[]{:S(2)}) copy-start(bf16[1,96,1024]{2,1,0:T(8,128)(2,1)S(1)} %get-tuple-element.691) | copy-start | bytes 589828
  489.6 16.7 %copy-start.136 = (f32[1024]{0:T(1024)}, f32[1024]{0:T(1024)S(1)}, u32[]{:S(2)}) copy-start(f32[1024]{0:T(1024)S(1)} %get-tuple-element.699) | copy-start | bytes 12292
  489.6 16.7 %copy-start.138 = (f32[1024]{0:T(1024)}, f32[1024]{0:T(1024)S(1)}, u32[]{:S(2)}) copy-start(f32[1024]{0:T(1024)S(1)} %get-tuple-element.701) | copy-start | bytes 12292
  515.9 199.8 %reduce-scatter.3.cloned.1.call-start = ((), (), s32[]{:S(2)}) async-start(), calls=%async_computation.4 | async-start | bytes 18104320 | tf_op jit(solution)/shard_map/reduce_scatter | solution.py:41
  545.9 17.0 %slice-start.4 = ((s8[16777216]{0:T(1024)(128)(4,1)}), s8[4194304]{0:T(1024)(128)(4,1)S(1)}, s32[]{:S(2)}) async-start(s8[16777216]{0:T(1024)(128)(4,1)} %bitcast.489), calls=%async_computation.11 | async-start | bytes 8388608
  545.9 17.0 %slice-start.5 = ((s8[16777216]{0:T(1024)(128)(4,1)}), s8[4194304]{0:T(1024)(128)(4,1)S(1)}, s32[]{:S(2)}) async-start(s8[16777216]{0:T(1024)(128)(4,1)} %bitcast.489), calls=%async_computation.12 | async-start | bytes 8388608
  545.9 18.6 %slice-start.6 = ((s8[16777216]{0:T(1024)(128)(4,1)}), s8[4194304]{0:T(1024)(128)(4,1)S(1)}, s32[]{:S(2)}) async-start(s8[16777216]{0:T(1024)(128)(4,1)} %bitcast.489), calls=%async_computation.13 | async-start | bytes 8388608
  545.9 19.9 %slice-start.7 = ((s8[16777216]{0:T(1024)(128)(4,1)}), s8[4194304]{0:T(1024)(128)(4,1)S(1)}, s32[]{:S(2)}) async-start(s8[16777216]{0:T(1024)(128)(4,1)} %bitcast.489), calls=%async_computation.14 | async-start | bytes 8388608
  616.3 155.5 %all-reduce.8.cloned.1.call-start = ((), (), s32[]{:S(2)}) async-start(), calls=%async_computation.6 | async-start | bytes 3145728 | tf_op jit(solution)/shard_map/psum | solution.py:412
  721.3 31.4 %copy-start.68 = (bf16[1,96,1024]{2,1,0:T(8,128)(2,1)S(1)}, bf16[1,96,1024]{2,1,0:T(8,128)(2,1)}, u32[]{:S(2)}) copy-start(bf16[1,96,1024]{2,1,0:T(8,128)(2,1)} %copy-done.67) | copy-start | bytes 589828
  721.3 31.4 %copy-start.70 = (bf16[1,96,1024]{2,1,0:T(8,128)(2,1)S(1)}, bf16[1,96,1024]{2,1,0:T(8,128)(2,1)}, u32[]{:S(2)}) copy-start(bf16[1,96,1024]{2,1,0:T(8,128)(2,1)} %copy-done.69) | copy-start | bytes 589828
  721.3 31.4 %copy-start.81 = (bf16[96,1024]{1,0:T(8,128)(2,1)S(1)}, bf16[96,1024]{1,0:T(8,128)(2,1)}, u32[]{:S(2)}) copy-start(bf16[96,1024]{1,0:T(8,128)(2,1)} %copy-done.80) | copy-start | bytes 589828
  (126 other events, 583.6 us)
Sparse Core Ops, SparseCore 0:
  10.5 59.7 all-gather.4
  72.0 93.5 all-gather.2
  516.0 74.3 reduce-scatter.4
  616.5 99.1 reduce-scatter.2
  721.5 50.2 all-reduce.7
where the time goes:
time: 798 us; the launch traced here: 784 us
  waiting for transfers between devices  261 us (33%)
  local copies, waits for them, and re-layouts  159 us (20%)
  matrix products  130 us (16%)
  other arithmetic  125 us (16%)
  blocking collectives  70.5 us (9%)
  between operations  17.1 us (2%)
  starting transfers between devices  10.8 us (1%)
  loops' own time  10 us (1%)
    all_gather x2, waiting for transfers between devices, sent_together(): filled = lax.all_gather(both, axis, axis=dim, tiled=True)  101 us
    reduce_scatter x2, waiting for transfers between devices, in_one_piece(): filled = lax.psum_scatter(both, axis, scatter_dimension=dim, tiled=True)  97.3 us
    ppermute x4, waiting for transfers between devices, shifted(): lax.ppermute(value, axis, [(source, source + steps) for source in range(l...  62.3 us
    dot_general x6, matrix products, dot_rows(): lax.dot_general(left, right, (((0,), (0,)), ((), ())), preferred_element_...  44.5 us
    dot_general x8, matrix products, dot_back(): lax.dot_general(left, right, (((1,), (1,)), ((), ())), preferred_element_...  41.7 us
    squeeze x4, local copies, waits for them, and re-layouts, on_device(): gathered = tuple((v[0] for v in fetched))  35.7 us
    concatenate x1, local copies, waits for them, and re-layouts, in_one_piece(): jnp.concatenate([a.reshape(*a.shape[:along], w) for a, w in zip(arrays, w...  34.7 us
    another operation x15, local copies, waits for them, and re-layouts  32.5 us
  transfers between devices with their start and end apart: 9, of which 7 were waited for; matrix products, arithmetic and copies ran while one was open for 18% of the time, Pallas kernels for 0%

commit v1 on v0

v1 whole, which is shorter than its diff:
```python
import functools

import jax
import jax.numpy as jnp
from jax import lax
from jax.sharding import PartitionSpec as P

HEADS = 16
SLOT = 96

norm_eps = 1e-05
masked_score = -1e30


def swap_section(value, steps):
    pairs = [(0, 1)] if steps > 0 else [(1, 0)]
    return lax.ppermute(value, "section", pairs)


def normalize(values, norm_gain, norm_bias):
    row_mean = jnp.mean(values, axis=-1, keepdims=True)
    centered = values - row_mean
    variance = jnp.mean(centered * centered, axis=-1, keepdims=True)
    return centered * lax.rsqrt(variance + norm_eps) * norm_gain + norm_bias


def dot(left, right):
    return jnp.dot(left, right, preferred_element_type=jnp.float32)


def dot_rows(left, right):
    return lax.dot_general(
        left, right, (((0,), (0,)), ((), ())), preferred_element_type=jnp.float32
    )


def dot_back(left, right):
    return lax.dot_general(
        left, right, (((1,), (1,)), ((), ())), preferred_element_type=jnp.float32
    )


def split_heads(values):
    return values.reshape(values.shape[0], HEADS, values.shape[1] // HEADS)


def allowed_pairs(segment):
    positions = jnp.arange(segment.shape[0])
    slot_of = positions // SLOT
    return (
        (segment[:, None] == segment[None, :])
        & (positions[None, :] <= positions[:, None])
        & (slot_of[:, None] == slot_of[None, :])
    )


def head_scores(queries, keys_part, allowed):
    score_scale = (queries.shape[1] // HEADS) ** (-0.5)
    raw_scores = (
        jnp.einsum(
            "qhd,khd->hqk",
            split_heads(queries),
            split_heads(keys_part),
            preferred_element_type=jnp.float32,
        )
        * score_scale
    )
    return jnp.where(allowed[None], raw_scores, masked_score)


def forward(rows_in, allowed, mats, vecs):
    w_qkv, w_out, w_up, w_down = mats
    width = rows_in.shape[1]
    inputs = rows_in.astype(jnp.float32)
    normed = normalize(inputs, vecs["ln1_gain"], vecs["ln1_bias"]).astype(jnp.bfloat16)
    projected = dot(normed, w_qkv)
    queries = (projected[:, :width] + vecs["b_query"]).astype(jnp.bfloat16)
    keys_part = projected[:, width : 2 * width].astype(jnp.bfloat16)
    values_part = (projected[:, 2 * width :] + vecs["b_value"]).astype(jnp.bfloat16)
    scores = head_scores(queries, keys_part, allowed)
    row_top = jnp.max(scores, axis=-1, keepdims=True)
    exponent = jnp.exp(scores - row_top)
    row_total = jnp.sum(exponent, axis=-1, keepdims=True)
    attn_probs = exponent / row_total
    row_lse = row_top + jnp.log(row_total)
    attended = (
        jnp.einsum(
            "hqk,khd->qhd",
            attn_probs.astype(jnp.bfloat16),
            split_heads(values_part),
            preferred_element_type=jnp.float32,
        )
        .reshape(rows_in.shape)
        .astype(jnp.bfloat16)
    )
    middle = inputs + dot(attended, w_out) + vecs["b_out"]
    second = normalize(middle, vecs["ln2_gain"], vecs["ln2_bias"]).astype(jnp.bfloat16)
    before = dot(second, w_up) + vecs["b_up"]
    hidden = jax.nn.gelu(before, approximate=True).astype(jnp.bfloat16)
    result = middle + dot(hidden, w_down) + vecs["b_down"]
    record = (inputs, normed, queries, keys_part, values_part, row_lse, attended, middle, second, before, hidden)
    return result.astype(jnp.bfloat16), record


def backward_rows(grad_out, record, allowed, mats, vecs):
    w_qkv, w_out, w_up, w_down = mats
    inputs, normed, queries, keys_part, values_part, row_lse, attended, middle, second, before, hidden = record
    width = inputs.shape[1]
    grad_update = grad_out.astype(jnp.bfloat16)
    grad_hidden = dot_back(grad_update, w_down)
    _, gelu_pull = jax.vjp(functools.partial(jax.nn.gelu, approximate=True), before)
    grad_before = gelu_pull(grad_hidden)[0].astype(jnp.bfloat16)
    grad_second = dot_back(grad_before, w_up)
    _, second_pull = jax.vjp(normalize, middle, vecs["ln2_gain"], vecs["ln2_bias"])
    grad_mid_norm, grad_gain_two, grad_bias_two = second_pull(grad_second)
    grad_middle = grad_out + grad_mid_norm
    grad_branch = grad_middle.astype(jnp.bfloat16)
    grad_attended = dot_back(grad_branch, w_out).astype(jnp.bfloat16)
    score_scale = (width // HEADS) ** (-0.5)
    attn_probs = jnp.exp(head_scores(queries, keys_part, allowed) - row_lse)
    grad_heads = split_heads(grad_attended)
    grad_probs = jnp.einsum(
        "qhd,khd->hqk", grad_heads, split_heads(values_part), preferred_element_type=jnp.float32
    )
    row_delta = jnp.sum(attn_probs * grad_probs, axis=-1, keepdims=True)
    grad_scores = (attn_probs * (grad_probs - row_delta)).astype(jnp.bfloat16)
    grad_query = (
        jnp.einsum("hqk,khd->qhd", grad_scores, split_heads(keys_part), preferred_element_type=jnp.float32)
        * score_scale
    )
    grad_key = (
        jnp.einsum("hqk,qhd->khd", grad_scores, split_heads(queries), preferred_element_type=jnp.float32)
        * score_scale
    )
    grad_value = jnp.einsum(
        "hqk,qhd->khd", attn_probs.astype(jnp.bfloat16), grad_heads, preferred_element_type=jnp.float32
    )
    grad_joined = jnp.concatenate(
        [v.reshape(inputs.shape) for v in (grad_query, grad_key, grad_value)], axis=1
    ).astype(jnp.bfloat16)
    _, first_pull = jax.vjp(normalize, inputs, vecs["ln1_gain"], vecs["ln1_bias"])
    grad_normed = dot_back(grad_joined, w_qkv)
    grad_in_norm, grad_gain_one, grad_bias_one = first_pull(grad_normed)
    grad_in = (grad_middle + grad_in_norm).astype(jnp.bfloat16)
    sides = (grad_update, grad_before, grad_branch, grad_joined)
    norm_sums = (grad_gain_one, grad_bias_one, grad_gain_two, grad_bias_two)
    return grad_in, sides, norm_sums


def column_sum(values):
    return jnp.sum(values.astype(jnp.float32), axis=0)


def on_device(
    ends, segment_ids, token_mask,
    ln1_gain, ln1_bias, w_qkv, b_query, b_value, w_out, b_out,
    ln2_gain, ln2_bias, w_up, b_up, w_down, b_down,
):
    names = ("ln1_gain", "ln1_bias", "b_query", "b_value", "b_out", "ln2_gain", "ln2_bias", "b_down", "b_up")
    shards = (ln1_gain, ln1_bias, b_query, b_value, b_out, ln2_gain, ln2_bias, b_down, b_up)
    packed = jnp.concatenate([v[0] for v in shards])
    everyone = lax.all_gather(packed, "shard", axis=0, tiled=False).astype(jnp.float32)
    vecs, at = {}, 0
    for name, v in zip(names, shards):
        vecs[name] = everyone[:, at : at + v.shape[1]].reshape(1, -1)
        at += v.shape[1]
    mats = tuple(lax.all_gather(w[0], "shard", axis=0, tiled=True) for w in (w_qkv, w_out, w_up, w_down))

    first_section = lax.axis_index("section") == 0
    local_rows = ends[0]
    allowed = allowed_pairs(segment_ids)

    early, _ = forward(local_rows, allowed, mats, vecs)
    arrived = swap_section(early, 1)
    own_rows = jnp.where(first_section, local_rows, arrived)
    section_out, record = forward(own_rows, allowed, mats, vecs)

    cotangent = local_rows.astype(jnp.float32) * token_mask[:, None].astype(jnp.float32)
    early_grad, _, _ = backward_rows(cotangent, record, allowed, mats, vecs)
    came_back = swap_section(early_grad, -1)
    grad_now = jnp.where(first_section, came_back.astype(jnp.float32), cotangent)
    section_grad, sides, norm_sums = backward_rows(grad_now, record, allowed, mats, vecs)

    grad_update, grad_before, grad_branch, grad_joined = sides
    inputs, normed, _, _, _, _, attended, _, second, _, hidden = record
    width = inputs.shape[1]
    partial = [
        dot_rows(left, right).astype(jnp.bfloat16)
        for left, right in (
            (hidden, grad_update), (second, grad_before), (attended, grad_branch), (normed, grad_joined)
        )
    ]
    summed = [lax.psum_scatter(p, "shard", scatter_dimension=0, tiled=True) for p in partial]
    summed = [lax.psum(s, "dp").astype(jnp.float32)[None] for s in summed]
    g_down, g_up, g_out, g_qkv = summed
    gain_one, bias_one, gain_two, bias_two = norm_sums
    vectors = [
        gain_one, bias_one, column_sum(grad_joined[:, :width])[None], column_sum(grad_joined[:, 2 * width :])[None],
        column_sum(grad_branch)[None], gain_two, bias_two, column_sum(grad_update)[None],
        column_sum(grad_before)[None],
    ]
    shard_count = lax.axis_size("shard")
    rows = jnp.concatenate([v.reshape(shard_count, -1) for v in vectors], axis=1)
    rows = lax.psum(rows, ("shard", "dp"))
    mine = lax.dynamic_slice_in_dim(rows, lax.axis_index("shard"), 1, 0)
    out, at = {}, 0
    for name, v in zip(names, shards):
        out[name] = mine[:, at : at + v.shape[1]]
        at += v.shape[1]
    return (
        section_out[None], section_grad[None], out["ln1_gain"], out["ln1_bias"], g_qkv, out["b_query"],
        out["b_value"], g_out, out["b_out"], out["ln2_gain"], out["ln2_bias"], g_up, out["b_up"], g_down,
        out["b_down"],
    )


def solution(mesh):
    vector, matrix = P("section", "shard"), P("section", "shard", None)
    rows, ids = P("section", ("dp", "shard"), None), P(("dp", "shard"))
    in_specs = (
        rows, ids, ids, vector, vector, matrix, vector, vector, matrix, vector, vector, vector, matrix,
        vector, matrix, vector,
    )
    out_specs = (
        rows, rows, vector, vector, matrix, vector, vector, matrix, vector, vector, vector, matrix, vector,
        matrix, vector,
    )
    return jax.shard_map(on_device, mesh=mesh, in_specs=in_specs, out_specs=out_specs, check_vma=False)
```

time: 798 us -> 905 us (1.13)
  blocking collectives: 70.5 us -> 298 us
  waiting for transfers between devices: 261 us -> 413 us
  local copies, waits for them, and re-layouts: 159 us -> 29.2 us
  other arithmetic: 125 us -> 24.3 us
  matrix products: 130 us -> 110 us
  loops' own time: 10 us -> 0 us
    psum x1, blocking collectives: 10.9 us -> 278 us  [on_device(): rows = lax.psum(rows, ('shard', 'dp'))]
    reduce_scatter x2 -> x4, waiting for transfers between devices: 97.3 us -> 244 us  [on_device(): lax.psum_scatter(p, 'shard', scatter_dimension=0, tiled=True)]
    convert_element_type x41 -> x6, other arithmetic: 60.1 us -> 3.06 us  [the longest x2 1.78 us: backward_rows(): grad_scores = (attn_probs * (grad_probs - row_delta)).astype(jnp.bfloat16)]
    all_gather x2 -> x4, waiting for transfers between devices: 101 us -> 146 us  [on_device(): lax.all_gather(w[0], 'shard', axis=0, tiled=True)]
    ppermute x4 -> x2, waiting for transfers between devices: 62.3 us -> 20.4 us  [swap_section(): return lax.ppermute(value, 'section', pairs)]
    squeeze x8 -> x0, local copies, waits for them, and re-layouts: 39.1 us -> none  [the longest x4 35.7 us: on_device(): gathered = tuple((v[0] for v in fetched))]
    another operation x25 -> x5, local copies, waits for them, and re-layouts: 36.4 us -> 1.68 us  [on_device(): v.reshape(shard_count, -1)]
    concatenate x2, local copies, waits for them, and re-layouts: 37.4 us -> 5.51 us  [the longest x1 5.42 us: on_device(): packed = jnp.concatenate([v[0] for v in shards])]
  transfers between devices with their start and end apart: 9 -> 11, of which waited for: 7 -> 10; matrix products, arithmetic and copies ran while one was open for 18% -> 8% of each run, Pallas kernels for 0% -> 0%
where the time goes in v1:
time: 905 us; the launch traced here: 897 us
  waiting for transfers between devices  413 us (46%)
  blocking collectives  298 us (33%)
  matrix products  110 us (12%)
  local copies, waits for them, and re-layouts  29.2 us (3%)
  other arithmetic  24.3 us (3%)
  between operations  15.3 us (2%)
    psum x1, blocking collectives, on_device(): rows = lax.psum(rows, ('shard', 'dp'))  278 us
    reduce_scatter x4, waiting for transfers between devices, on_device(): lax.psum_scatter(p, 'shard', scatter_dimension=0, tiled=True)  244 us
    all_gather x4, waiting for transfers between devices, on_device(): lax.all_gather(w[0], 'shard', axis=0, tiled=True)  146 us
    dot_general x7, matrix products, dot_back(): lax.dot_general(left, right, (((1,), (1,)), ((), ())), preferred_element_...  40.3 us
    dot_general x7, matrix products, dot(): return jnp.dot(left, right, preferred_element_type=jnp.float32)  32.5 us
    ppermute x2, waiting for transfers between devices, swap_section(): return lax.ppermute(value, 'section', pairs)  20.4 us
    all_gather x1, blocking collectives, on_device(): lax.all_gather(packed, 'shard', axis=0, tiled=False).astype(jnp.float32)  20.3 us
    dot_general x4, matrix products, dot_rows(): lax.dot_general(left, right, (((0,), (0,)), ((), ())), preferred_element_...  20.2 us
  transfers between devices with their start and end apart: 11, of which 10 were waited for; matrix products, arithmetic and copies ran while one was open for 8% of the time, Pallas kernels for 0%

profile of v1, /device:TPU:0, one launch (start us, length us, event | category | flops | bytes accessed | tf_op | source)
XLA Modules:
  0.0 897.4 jit_solution(12204455462339195669)
XLA Ops:
  10.7 5.4 concatenate.14
  16.1 20.3 %all-gather.5 = bf16[16,1,768]{2,1,0:T(2,128)(2,1)S(1)} all-gather(bf16[1,1,768]{2,1,0:T(2,128)(2,1)S(1)} %reshape.348), channel_id=2, replica_groups=mesh['section'=2,'dp'=4,'shard'=16] {'shard'}, dimensions={0}, use_global_device_ids=true | all-gather | bytes 26112 | tf_op jit(solution)/shard_map/all_gather | solution.py:162
  38.3 1.3 fusion.144
  40.4 14.2 %all-gather.11.cloned.1.call-done = bf16[1,1024,3072]{2,1,0:T(8,128)(2,1)} async-done(((bf16[1,64,3072]{2,1,0:T(8,128)(2,1)}), bf16[1,1024,3072]{2,1,0:T(8,128)(2,1)}) %all-gather.11.cloned.1.call-update) | async-done | bytes 6291472 | tf_op jit(solution)/shard_map/all_gather | solution.py:167
  54.6 4.4 fusion.23
  60.0 2.9 fusion.219
  62.9 2.4 fusion.77
  65.2 26.0 %all-gather.13.cloned.1.call-done = bf16[1,1024,1024]{2,1,0:T(8,128)(2,1)} async-done(((bf16[1,64,1024]{2,1,0:T(8,128)(2,1)}), bf16[1,1024,1024]{2,1,0:T(8,128)(2,1)}) %all-gather.13.cloned.1.call-update) | async-done | bytes 2097168 | tf_op jit(solution)/shard_map/all_gather | solution.py:167
  91.2 2.3 fusion.220
  93.8 51.3 %all-gather.17.cloned.1.call-done = bf16[1,4096,1024]{2,1,0:T(8,128)(2,1)} async-done(((bf16[1,256,1024]{2,1,0:T(8,128)(2,1)}), bf16[1,4096,1024]{2,1,0:T(8,128)(2,1)}) %all-gather.17.cloned.1.call-update) | async-done | bytes 8388624 | tf_op jit(solution)/shard_map/all_gather | solution.py:167
  145.1 54.6 %all-gather.15.cloned.1.call-done = bf16[1,1024,4096]{2,1,0:T(8,128)(2,1)} async-done(((bf16[1,64,4096]{2,1,0:T(8,128)(2,1)}), bf16[1,1024,4096]{2,1,0:T(8,128)(2,1)}) %all-gather.15.cloned.1.call-update) | async-done | bytes 8388624 | tf_op jit(solution)/shard_map/all_gather | solution.py:167
  199.7 9.8 %fusion.115 = bf16[192,1024]{1,0:T(8,128)(2,1)S(1)} fusion(f32[192,1024]{1,0:T(8,128)S(1)} %get-tuple-element.63, bf16[1,4096,1024]{2,1,0:T(8,128)(2,1)} %all-gather.17.cloned.1.call-done, bf16[1,1024,4096]{2,1,0:T(8,128)(2,1)} %all-gather.15.cloned.1.call-done, f32[4096]{0:T(1024)S(1)} %bitcast.242, f32[1024]{0:T(1024)S(1)} %add.260, f32[1024]{0:T(1024)S(1)} %add.251, ...), kind=kOutput, calls=%fused_computation.112 | convolution fusion | flops 3230662656 | bytes 17987072 | tf_op jit(solution)/shard_map/dot_general | solution.py:28
  209.5 5.3 collective-permute-start
  215.3 7.7 collective-permute-done
  224.7 4.3 fusion.21
  232.3 2.0 fusion.61
  234.3 1.7 fusion.51
  239.8 3.6 fusion.28
  243.4 13.1 %multiply_reduce_fusion.4 = (f32[192]{0:T(256)}, f32[192,1024]{1,0:T(8,128)}) fusion(f32[192,1024]{1,0:T(8,128)} %copy-done.2, f32[192]{0:T(256)} %copy-done.52, f32[1024]{0:T(1024)} %copy-done.39, bf16[1,1024,4096]{2,1,0:T(8,128)(2,1)} %all-gather.15.cloned.1.call-done, f32[192,4096]{1,0:T(8,128)} %fusion.28, ...), kind=kOutput, calls=%fused_computation.165 | convolution fusion | flops 3238330112 | bytes 21895424 | tf_op jit(solution)/shard_map/dot_general | solution.py:38
  256.4 1.3 multiply_multiply_fusion.6
  257.7 1.7 fusion.216
  260.3 3.2 fusion.109
  263.5 2.0 copy.79
  265.5 2.0 convolution_convert_fusion.5
  267.5 1.1 multiply_reduce_fusion.1
  271.0 2.3 fusion.149
  274.7 1.3 collective-permute-start.1
  276.0 12.7 %collective-permute-done.1 = bf16[192,1024]{1,0:T(8,128)(2,1)S(1)} collective-permute-done((bf16[192,1024]{1,0:T(8,128)(2,1)S(1)}, bf16[192,1024]{1,0:T(8,128)(2,1)S(1)}, u32[]{:S(2)}, u32[]{:S(2)}) %collective-permute-start.1) | collective-permute-done | bytes 393248 | tf_op jit(solution)/shard_map/ppermute | solution.py:17
  289.5 5.5 convert_reduce_fusion
  295.0 1.2 copy-done.30
  296.2 7.1 multiply_reduce_fusion.2
  305.4 2.0 convolution_convert_fusion.3
  307.5 3.4 fusion.112
  311.0 2.0 copy.83
  313.0 2.3 multiply_reduce_fusion
  319.1 4.8 convolution_convert_fusion.2
  325.6 5.7 convolution_convert_fusion.1
  332.3 7.6 convolution_convert_fusion
  340.7 7.4 fusion.121
  348.1 21.4 %reduce-scatter.7.cloned.1.call-done = bf16[64,1024]{1,0:T(8,128)(2,1)} async-done(((bf16[1024,1024]{1,0:T(8,128)(2,1)}), bf16[64,1024]{1,0:T(8,128)(2,1)}) %reduce-scatter.7.cloned.1.call-update) | async-done | bytes 131088 | tf_op jit(solution)/shard_map/reduce_scatter | solution.py:193
  369.5 71.6 %reduce-scatter.5.cloned.1.call-done = bf16[64,3072]{1,0:T(8,128)(2,1)} async-done(((bf16[1024,3072]{1,0:T(8,128)(2,1)}), bf16[64,3072]{1,0:T(8,128)(2,1)}) %reduce-scatter.5.cloned.1.call-update) | async-done | bytes 393232 | tf_op jit(solution)/shard_map/reduce_scatter | solution.py:193
  441.1 75.7 %reduce-scatter.9.cloned.1.call-done = bf16[64,4096]{1,0:T(8,128)(2,1)} async-done(((bf16[1024,4096]{1,0:T(8,128)(2,1)}), bf16[64,4096]{1,0:T(8,128)(2,1)}) %reduce-scatter.9.cloned.1.call-update) | async-done | bytes 524304 | tf_op jit(solution)/shard_map/reduce_scatter | solution.py:193
  516.8 75.6 %reduce-scatter.11.cloned.1.call-done = bf16[256,1024]{1,0:T(8,128)(2,1)} async-done(((bf16[4096,1024]{1,0:T(8,128)(2,1)}), bf16[256,1024]{1,0:T(8,128)(2,1)}) %reduce-scatter.11.cloned.1.call-update) | async-done | bytes 524304 | tf_op jit(solution)/shard_map/reduce_scatter | solution.py:193
  592.5 5.7 fusion.213
  603.2 278.2 %psum.35 = f32[16,768]{1,0:T(8,128)S(1)} all-reduce(f32[16,768]{1,0:T(8,128)S(1)} %concatenate.17), channel_id=1, replica_groups=mesh['section'=2,'dp'=4,'shard'=16] {'shard','dp'}, use_global_device_ids=true, to_apply=%region_31.32 | all-reduce | flops 12288 | bytes 98304 | tf_op jit(solution)/shard_map/psum | solution.py:204
  883.7 2.0 broadcast_in_dim.124
  885.6 1.6 broadcast_in_dim.126
  887.3 2.1 broadcast_in_dim.128
  (278 shorter events, 39.2 us)
Async XLA Ops:
  7.2 47.5 %all-gather.11.cloned.1.call-start = ((), (), s32[]{:S(2)}) async-start(), calls=%async_computation.8 | async-start | bytes 6684672 | tf_op jit(solution)/shard_map/all_gather | solution.py:167
  7.9 83.3 %all-gather.13.cloned.1.call-start = ((), (), s32[]{:S(2)}) async-start(), calls=%async_computation.9 | async-start | bytes 2228224 | tf_op jit(solution)/shard_map/all_gather | solution.py:167
  8.7 136.4 %all-gather.17.cloned.1.call-start = ((), (), s32[]{:S(2)}) async-start(), calls=%async_computation.11 | async-start | bytes 8912896 | tf_op jit(solution)/shard_map/all_gather | solution.py:167
  9.4 190.2 %all-gather.15.cloned.1.call-start = ((), (), s32[]{:S(2)}) async-start(), calls=%async_computation.10 | async-start | bytes 8912896 | tf_op jit(solution)/shard_map/all_gather | solution.py:167
  10.0 359.5 %reduce-scatter.7.cloned.1.call-start = ((), (), s32[]{:S(2)}) async-start(), calls=%async_computation.5 | async-start | bytes 2228224 | tf_op jit(solution)/shard_map/reduce_scatter | solution.py:193
  36.6 54.6 %copy-start.46 = (f32[1024]{0:T(1024)}, f32[1024]{0:T(1024)S(1)}, u32[]{:S(2)}) copy-start(f32[1024]{0:T(1024)S(1)} %add.247) | copy-start | bytes 12292
  36.7 187.4 %copy-start.77 = (f32[1024]{0:T(1024)}, f32[1024]{0:T(1024)S(1)}, u32[]{:S(2)}) copy-start(f32[1024]{0:T(1024)S(1)} %add.237) | copy-start | bytes 12292
  36.7 187.4 %copy-start.55 = (f32[1024]{0:T(1024)}, f32[1024]{0:T(1024)S(1)}, u32[]{:S(2)}) copy-start(f32[1024]{0:T(1024)S(1)} %mul.349) | copy-start | bytes 12292
  36.9 162.8 %copy-start.68 = (f32[2,2,8,128]{3,1,2,0:T(2,128)}, f32[2,2,8,128]{3,1,2,0:T(2,128)S(1)}, u32[]{:S(2)}) copy-start(f32[2,2,8,128]{3,1,2,0:T(2,128)S(1)} %copy.96) | copy-start | bytes 49156
  37.0 162.7 %copy-start.75 = (f32[1024]{0:T(1024)}, f32[1024]{0:T(1024)S(1)}, u32[]{:S(2)}) copy-start(f32[1024]{0:T(1024)S(1)} %add.260) | copy-start | bytes 12292
  37.0 162.6 %copy-start.43 = (f32[1024]{0:T(1024)}, f32[1024]{0:T(1024)S(1)}, u32[]{:S(2)}) copy-start(f32[1024]{0:T(1024)S(1)} %add.251) | copy-start | bytes 12292
  37.1 162.5 %copy-start.39 = (f32[1024]{0:T(1024)}, f32[1024]{0:T(1024)S(1)}, u32[]{:S(2)}) copy-start(f32[1024]{0:T(1024)S(1)} %mul.356) | copy-start | bytes 12292
  40.4 19.5 %copy-start.20 = (pred[192,192]{0,1:T(8,128)(4,1)}, pred[192,192]{0,1:T(8,128)(4,1)S(1)}, u32[]{:S(2)}) copy-start(pred[192,192]{0,1:T(8,128)(4,1)S(1)} %fusion.187) | copy-start | bytes 110596
  62.8 28.4 %copy-start.1 = (bf16[1,192,1024]{2,1,0:T(8,128)(2,1)S(1)}, bf16[1,192,1024]{2,1,0:T(8,128)(2,1)}, u32[]{:S(2)}) copy-start(bf16[1,192,1024]{2,1,0:T(8,128)(2,1)} %param.16) | copy-start | bytes 1179652
  199.7 15.1 %copy-start.81 = (s32[192]{0:T(256)S(1)}, s32[192]{0:T(256)}, u32[]{:S(2)}) copy-start(s32[192]{0:T(256)} %param.18) | copy-start | bytes 2308
  209.5 13.6 %collective-permute-start = (bf16[192,1024]{1,0:T(8,128)(2,1)S(1)}, bf16[192,1024]{1,0:T(8,128)(2,1)S(1)}, u32[]{:S(2)}, u32[]{:S(2)}) collective-permute-start(bf16[192,1024]{1,0:T(8,128)(2,1)S(1)} %fusion.115), channel_id=1, source_target_pairs={{0,64},{1,65},{2,66},{3,67},{4,68},{5,69},{6,70},{7,71},{8,72},{9,... | collective-permute-start | bytes 1179656 | tf_op jit(solution)/shard_map/ppermute | solution.py:17
  223.3 5.7 copy-start.5
  223.3 5.7 copy-start.48
  232.3 3.7 copy-start.18
  232.3 3.7 copy-start.21
  234.3 5.5 slice-start.2
  236.0 3.8 slice-start.3
  270.9 18.6 %slice-start = ((s8[8388608]{0:T(1024)(128)(4,1)}), s8[4194304]{0:T(1024)(128)(4,1)S(1)}, s32[]{:S(2)}) async-start(s8[8388608]{0:T(1024)(128)(4,1)} %bitcast.252), calls=%async_computation.13 | async-start | bytes 8388608
  271.0 18.5 %slice-start.1 = ((s8[8388608]{0:T(1024)(128)(4,1)}), s8[4194304]{0:T(1024)(128)(4,1)S(1)}, s32[]{:S(2)}) async-start(s8[8388608]{0:T(1024)(128)(4,1)} %bitcast.252), calls=%async_computation.14 | async-start | bytes 8388608
  273.3 16.2 %copy-start.82 = (f32[192,4096]{1,0:T(8,128)S(1)}, f32[192,4096]{1,0:T(8,128)}, u32[]{:S(2)}) copy-start(f32[192,4096]{1,0:T(8,128)} %fusion.28) | copy-start | bytes 9437188
  274.7 14.0 %collective-permute-start.1 = (bf16[192,1024]{1,0:T(8,128)(2,1)S(1)}, bf16[192,1024]{1,0:T(8,128)(2,1)S(1)}, u32[]{:S(2)}, u32[]{:S(2)}) collective-permute-start(bf16[192,1024]{1,0:T(8,128)(2,1)S(1)} %add_convert_fusion.3), channel_id=1, source_target_pairs={{64,0},{65,1},{66,2},{67,3},{68,4},{69,5},{70,6},{71,7},{72,8},{73... | collective-permute-start | bytes 1179656 | tf_op jit(solution)/shard_map/ppermute | solution.py:17
  289.5 5.5 copy-start.37
  289.5 6.7 copy-start.3
  289.5 6.7 copy-start.41
  289.5 6.7 copy-start.53
  289.5 6.7 copy-start.64
  296.2 7.1 copy-start.80
  307.5 5.5 copy-start.23
  307.5 133.6 %reduce-scatter.5.cloned.1.call-start = ((), (), s32[]{:S(2)}) async-start(), calls=%async_computation.4 | async-start | bytes 6684672 | tf_op jit(solution)/shard_map/reduce_scatter | solution.py:193
  324.0 192.8 %reduce-scatter.9.cloned.1.call-start = ((), (), s32[]{:S(2)}) async-start(), calls=%async_computation.6 | async-start | bytes 8912896 | tf_op jit(solution)/shard_map/reduce_scatter | solution.py:193
  331.4 261.0 %reduce-scatter.11.cloned.1.call-start = ((), (), s32[]{:S(2)}) async-start(), calls=%async_computation.7 | async-start | bytes 8912896 | tf_op jit(solution)/shard_map/reduce_scatter | solution.py:193
  340.0 543.7 %all-reduce.3.cloned.1.call-start = ((), (), s32[]{:S(2)}) async-start(), calls=%async_computation.12 | async-start | bytes 3145728 | tf_op jit(solution)/shard_map/psum | solution.py:194
  340.6 251.8 %copy-start.9 = (bf16[192,1024]{1,0:T(8,128)(2,1)S(1)}, bf16[192,1024]{1,0:T(8,128)(2,1)}, u32[]{:S(2)}) copy-start(bf16[192,1024]{1,0:T(8,128)(2,1)} %copy-done.5) | copy-start | bytes 1179652
  340.6 251.8 %copy-start.27 = (bf16[16,64,192]{2,1,0:T(8,128)(2,1)S(1)}, bf16[16,64,192]{2,1,0:T(8,128)(2,1)}, u32[]{:S(2)}) copy-start(bf16[16,64,192]{2,1,0:T(8,128)(2,1)} %copy-done.26) | copy-start | bytes 1179652
  340.6 251.8 %copy-start.33 = (bf16[16,64,192]{2,1,0:T(8,128)(2,1)S(1)}, bf16[16,64,192]{2,1,0:T(8,128)(2,1)}, u32[]{:S(2)}) copy-start(bf16[16,64,192]{2,1,0:T(8,128)(2,1)} %copy-done.32) | copy-start | bytes 1179652
  340.6 251.8 %copy-start.36 = (bf16[16,64,192]{2,1,0:T(8,128)(2,1)S(1)}, bf16[16,64,192]{2,1,0:T(8,128)(2,1)}, u32[]{:S(2)}) copy-start(bf16[16,64,192]{2,1,0:T(8,128)(2,1)} %copy-done.35) | copy-start | bytes 1179652
  340.6 251.8 %copy-start.51 = (f32[192]{0:T(256)S(1)}, f32[192]{0:T(256)}, u32[]{:S(2)}) copy-start(f32[192]{0:T(256)} %copy-done.48) | copy-start | bytes 2308
  340.6 251.8 %copy-start.58 = (f32[1024]{0:T(1024)S(1)}, f32[1024]{0:T(1024)}, u32[]{:S(2)}) copy-start(f32[1024]{0:T(1024)} %copy-done.55) | copy-start | bytes 12292
  592.5 5.7 copy-start.79
  592.5 5.7 copy-start.62
  592.5 9.8 %copy-start.67 = (f32[1024]{0:T(1024)S(1)}, f32[1024]{0:T(1024)}, u32[]{:S(2)}) copy-start(f32[1024]{0:T(1024)} %get-tuple-element.26) | copy-start | bytes 12292
  598.2 284.4 %copy-start.11 = (f32[192,1024]{1,0:T(8,128)S(1)}, f32[192,1024]{1,0:T(8,128)}, u32[]{:S(2)}) copy-start(f32[192,1024]{1,0:T(8,128)} %copy-done.10) | copy-start | bytes 2359300
  883.7 5.7 copy-start.34
  (52 other events, 85.5 us)
Sparse Core Ops, SparseCore 0:
  9.7 44.8 all-gather.10
  56.3 34.8 all-gather.12
  92.9 52.1 all-gather.16
  146.6 52.9 all-gather.14
  307.6 61.8 reduce-scatter.6
  371.7 69.3 reduce-scatter.4
  443.5 73.2 reduce-scatter.8
  519.2 73.1 reduce-scatter.10
  595.0 50.0 all-reduce.2

commit v2 on v1

--- a/solution.py
+++ b/solution.py
@@ -3,6 +3,8 @@
 import jax
 import jax.numpy as jnp
 from jax import lax
+from jax.experimental import pallas as pl
+from jax.experimental.pallas import tpu as pltpu
 from jax.sharding import PartitionSpec as P
 
 HEADS = 16
@@ -10,6 +12,137 @@
 
 norm_eps = 1e-05
 masked_score = -1e30
+MESH = pl.DeviceIdType.MESH
+RING_FIRST = (1, 3)
+
+
+def gather_kernel(count, *refs):
+    shards, fulls = refs[:count], refs[count : 2 * count]
+    own_sem, send_sem, recv_sem = refs[2 * count :]
+    me = lax.axis_index("shard")
+    core, x, y = me % 2, (me // 2) % 4, me // 8
+
+    def at(dy, dx):
+        return (((y + dy) % 2) * 4 + (x + dx) % 4) * 2 + core
+
+    sibling = me + 1 - 2 * core
+    right, left, pair = at(0, 1), at(0, 3), at(1, 0)
+    barrier = pltpu.get_barrier_semaphore()
+    for other in (sibling, right, left, pair):
+        pl.semaphore_signal(barrier, inc=1, device_id={"shard": other}, device_id_type=MESH)
+    pl.semaphore_wait(barrier, 4)
+
+    began = []
+
+    def send(which, dy, dx, target, half=None):
+        rows, width = shards[which].shape
+        mine = dy == 0 and dx == 0
+        spot = pl.ds(pl.multiple_of(at(dy, dx) * rows, 16), rows)
+        cut = pl.ds(0, width) if half is None else pl.ds(half * (width // 2), width // 2)
+        source = shards[which].at[:, cut] if mine else fulls[which].at[spot, cut]
+        copy = pltpu.make_async_remote_copy(
+            src_ref=source,
+            dst_ref=fulls[which].at[spot, cut],
+            send_sem=send_sem.at[len(began)],
+            recv_sem=recv_sem.at[len(began)],
+            device_id={"shard": target},
+            device_id_type=MESH,
+        )
+        copy.start()
+        began.append(copy)
+        return copy
+
+    pair_first = [k for k in range(count) if k not in RING_FIRST]
+    ring_first = [k for k in range(count) if k in RING_FIRST]
+    kept = []
+    for k in range(count):
+        rows = shards[k].shape[0]
+        spot = pl.ds(pl.multiple_of(me * rows, 16), rows)
+        copy = pltpu.make_async_copy(shards[k], fulls[k].at[spot, :], own_sem.at[k])
+        copy.start()
+        kept.append(copy)
+    to_pair, to_right, to_left, shared = {}, {}, {}, []
+    for k in pair_first:
+        to_pair[k] = send(k, 0, 0, pair)
+    for k in ring_first + pair_first:
+        to_right[k] = send(k, 0, 0, right)
+        to_left[k] = send(k, 0, 0, left)
+    for k in ring_first:
+        to_pair[k] = send(k, 0, 0, pair)
+    for k in range(count):
+        shared.append(send(k, 0, 0, sibling))
+    pair_right, pair_left = {}, {}
+    for k in pair_first:
+        to_pair[k].wait_recv()
+        pair_right[k] = send(k, 1, 0, right)
+        pair_left[k] = send(k, 1, 0, left)
+        shared.append(send(k, 1, 0, sibling))
+    far, ring_pair = {}, {}
+    for k in ring_first + pair_first:
+        to_right[k].wait_recv()
+        far[k, 0] = send(k, 0, 3, right, 0)
+        if k in ring_first:
+            ring_pair[k, 3] = send(k, 0, 3, pair)
+        shared.append(send(k, 0, 3, sibling))
+        to_left[k].wait_recv()
+        far[k, 1] = send(k, 0, 1, left, 1)
+        if k in ring_first:
+            ring_pair[k, 1] = send(k, 0, 1, pair)
+        shared.append(send(k, 0, 1, sibling))
+    for k in ring_first:
+        to_pair[k].wait_recv()
+        shared.append(send(k, 1, 0, sibling))
+    for k in ring_first:
+        far[k, 0].wait_recv()
+        far[k, 1].wait_recv()
+        ring_pair[k, 2] = send(k, 0, 2, pair)
+        shared.append(send(k, 0, 2, sibling))
+    far_pair = {}
+    for k in pair_first:
+        pair_right[k].wait_recv()
+        far_pair[k, 0] = send(k, 1, 3, right, 0)
+        shared.append(send(k, 1, 3, sibling))
+        pair_left[k].wait_recv()
+        far_pair[k, 1] = send(k, 1, 1, left, 1)
+        shared.append(send(k, 1, 1, sibling))
+    for k in pair_first:
+        far[k, 0].wait_recv()
+        far[k, 1].wait_recv()
+        shared.append(send(k, 0, 2, sibling))
+    for k in ring_first:
+        for dx in (3, 1):
+            ring_pair[k, dx].wait_recv()
+            shared.append(send(k, 1, dx, sibling))
+    for k in pair_first:
+        far_pair[k, 0].wait_recv()
+        far_pair[k, 1].wait_recv()
+        shared.append(send(k, 1, 2, sibling))
+    for k in ring_first:
+        ring_pair[k, 2].wait_recv()
+        shared.append(send(k, 1, 2, sibling))
+    for copy in shared:
+        copy.wait_recv()
+    for copy in began:
+        copy.wait_send()
+    for copy in kept:
+        copy.wait()
+
+
+def gather_all(arrays):
+    count = len(arrays)
+    copies = sum(16 if k in RING_FIRST else 17 for k in range(count))
+    return pl.pallas_call(
+        functools.partial(gather_kernel, count),
+        out_shape=[jax.ShapeDtypeStruct((16 * a.shape[0], a.shape[1]), a.dtype) for a in arrays],
+        in_specs=[pl.BlockSpec(memory_space=pl.ANY)] * count,
+        out_specs=[pl.BlockSpec(memory_space=pl.ANY)] * count,
+        scratch_shapes=[
+            pltpu.SemaphoreType.DMA((count,)),
+            pltpu.SemaphoreType.DMA((copies,)),
+            pltpu.SemaphoreType.DMA((copies,)),
+        ],
+        compiler_params=pltpu.CompilerParams(collective_id=0, has_side_effects=True),
+    )(*arrays)
 
 
 def swap_section(value, steps):
@@ -159,12 +292,13 @@
     names = ("ln1_gain", "ln1_bias", "b_query", "b_value", "b_out", "ln2_gain", "ln2_bias", "b_down", "b_up")
     shards = (ln1_gain, ln1_bias, b_query, b_value, b_out, ln2_gain, ln2_bias, b_down, b_up)
     packed = jnp.concatenate([v[0] for v in shards])
-    everyone = lax.all_gather(packed, "shard", axis=0, tiled=False).astype(jnp.float32)
+    tall = jnp.broadcast_to(packed[None], (16, packed.shape[0]))
+    *mats, everyone = gather_all((w_qkv[0], w_out[0], w_up[0], w_down[0], tall))
+    everyone = everyone.reshape(-1, *tall.shape)[:, 0].astype(jnp.float32)
     vecs, at = {}, 0
     for name, v in zip(names, shards):
         vecs[name] = everyone[:, at : at + v.shape[1]].reshape(1, -1)
         at += v.shape[1]
-    mats = tuple(lax.all_gather(w[0], "shard", axis=0, tiled=True) for w in (w_qkv, w_out, w_up, w_down))
 
     first_section = lax.axis_index("section") == 0
     local_rows = ends[0]
@@ -201,7 +335,7 @@
     ]
     shard_count = lax.axis_size("shard")
     rows = jnp.concatenate([v.reshape(shard_count, -1) for v in vectors], axis=1)
-    rows = lax.psum(rows, ("shard", "dp"))
+    rows = lax.psum(lax.psum(rows, "shard"), "dp")
     mine = lax.dynamic_slice_in_dim(rows, lax.axis_index("shard"), 1, 0)
     out, at = {}, 0
     for name, v in zip(names, shards):

time: 905 us -> 621 us (0.69)
  blocking collectives: 298 us -> 71.2 us
  waiting for transfers between devices: 413 us -> 265 us
  Pallas kernels: 0 us -> 91 us
    psum x1 -> x2, blocking collectives: 278 us -> 71.2 us  [on_device(): rows = lax.psum(lax.psum(rows, 'shard'), 'dp')]
    all_gather x4 -> x0, waiting for transfers between devices: 146 us -> none  [on_device(): lax.all_gather(w[0], 'shard', axis=0, tiled=True)]
    pallas_call x0 -> x1, Pallas kernels: none -> 91 us  [gather_all(): pl.pallas_call(functools.partial(gather_kernel, count), out_shape=[jax.Sh...]
    all_gather x1 -> x0, blocking collectives: 20.3 us -> none  [on_device(): lax.all_gather(packed, 'shard', axis=0, tiled=False).astype(jnp.float32)]
  transfers between devices with their start and end apart: 11 -> 7, of which waited for: 10 -> 6; matrix products, arithmetic and copies ran while one was open for 8% -> 8% of each run, Pallas kernels for 0% -> 0%
where the time goes in v2:
time: 621 us; the launch traced here: 612 us
  waiting for transfers between devices  265 us (43%)
  matrix products  108 us (17%)
  Pallas kernels  91 us (15%)
  blocking collectives  71.2 us (11%)
  local copies, waits for them, and re-layouts  29.9 us (5%)
  other arithmetic  24.5 us (4%)
  between operations  15.3 us (2%)
  starting transfers between devices  7.06 us (1%)
    reduce_scatter x4, waiting for transfers between devices, on_device(): lax.psum_scatter(p, 'shard', scatter_dimension=0, tiled=True)  244 us
    pallas_call x1, Pallas kernels, gather_all(): pl.pallas_call(functools.partial(gather_kernel, count), out_shape=[jax.Sh...  91 us
    psum x2, blocking collectives, on_device(): rows = lax.psum(lax.psum(rows, 'shard'), 'dp')  71.2 us
    dot_general x7, matrix products, dot_back(): lax.dot_general(left, right, (((1,), (1,)), ((), ())), preferred_element_...  40.3 us
    dot_general x7, matrix products, dot(): return jnp.dot(left, right, preferred_element_type=jnp.float32)  30.9 us
    ppermute x2, waiting for transfers between devices, swap_section(): return lax.ppermute(value, 'section', pairs)  20.8 us
    dot_general x4, matrix products, dot_rows(): lax.dot_general(left, right, (((0,), (0,)), ((), ())), preferred_element_...  20.1 us
  transfers between devices with their start and end apart: 7, of which 6 were waited for; matrix products, arithmetic and copies ran while one was open for 8% of the time, Pallas kernels for 0%

profile of v2, /device:TPU:0, one launch (start us, length us, event | category | flops | bytes accessed | tf_op | source)
XLA Modules:
  0.0 612.3 jit_solution(17327992733831539642)
XLA Ops:
  7.9 5.4 concatenate.14
  14.0 91.0 %shard_map.271 = (bf16[1024,3072]{1,0:T(8,128)(2,1)}, bf16[1024,1024]{1,0:T(8,128)(2,1)}, bf16[1024,4096]{1,0:T(8,128)(2,1)}, bf16[4096,1024]{1,0:T(8,128)(2,1)}, bf16[256,768]{1,0:T(8,128)(2,1)}) custom-call(bf16[64,3072]{1,0:T(8,128)(2,1)} %bitcast.163, bf16[64,1024]{1,0:T(8,128)(2,1)} %bitcast.167, bf16[64,4096]{1,0:T(8,128)(2,1)} %bitcast.149, ...), custom_call_target="tpu_custom_call" | custom-call | tf_op jit(solution)/shard_map/pallas_call | solution.py:134
  106.3 1.1 convert_reduce_fusion.1
  107.4 1.2 fusion.61
  108.8 4.4 fusion.79
  114.5 2.9 fusion.143
  117.4 2.5 fusion.33
  121.0 9.8 %fusion.43 = bf16[192,1024]{1,0:T(8,128)(2,1)S(1)} fusion(f32[192,1024]{1,0:T(8,128)S(1)} %get-tuple-element.75, bf16[4096,1024]{1,0:T(8,128)(2,1)} %get-tuple-element.24, bf16[1024,4096]{1,0:T(8,128)(2,1)} %get-tuple-element.23, f32[4096]{0:T(1024)S(1)} %bitcast.169, f32[1024]{0:T(1024)S(1)} %add.262, f32[1024]{0:T(1024)S(1)} %add.253, ...), kind=kOutput, calls=%fused_computation.83 | convolution fusion | flops 3230662656 | bytes 17987072 | tf_op jit(solution)/shard_map/dot_general | solution.py:161
  130.8 5.3 collective-permute-start
  136.7 7.9 %collective-permute-done = bf16[192,1024]{1,0:T(8,128)(2,1)S(1)} collective-permute-done((bf16[192,1024]{1,0:T(8,128)(2,1)S(1)}, bf16[192,1024]{1,0:T(8,128)(2,1)S(1)}, u32[]{:S(2)}, u32[]{:S(2)}) %collective-permute-start) | collective-permute-done | bytes 393248 | tf_op jit(solution)/shard_map/ppermute | solution.py:150
  146.3 4.3 fusion.134
  151.8 1.0 copy.60
  153.8 2.0 fusion.15
  155.8 1.7 fusion.13
  161.4 3.6 convolution_add_fusion
  164.9 13.1 %multiply_reduce_fusion.4 = (f32[192]{0:T(256)}, f32[192,1024]{1,0:T(8,128)}) fusion(f32[192,1024]{1,0:T(8,128)} %copy-done.3, f32[192]{0:T(256)} %copy-done.53, f32[1024]{0:T(1024)} %copy-done.40, bf16[1024,4096]{1,0:T(8,128)(2,1)} %get-tuple-element.23, f32[192,4096]{1,0:T(8,128)} %convolution_add_fusion, bf16[4096,1024]{1,0:T(8,128)(2,1)} %get-tuple-element.24, ...), kind=kOutput, calls=%fused_computation.135 | convolution fusion | flops 3238330112 | bytes 21895424 | tf_op jit(solution)/shard_map/dot_general | solution.py:171
  178.0 1.3 multiply_multiply_fusion.6
  179.3 1.7 fusion.140
  181.9 3.2 convolution_convert_fusion.7
  185.1 2.0 copy.63
  187.1 2.0 convolution_convert_fusion.5
  189.1 1.1 multiply_reduce_fusion.1
  192.6 2.3 fusion.66
  196.3 1.3 collective-permute-start.1
  197.6 12.9 %collective-permute-done.1 = bf16[192,1024]{1,0:T(8,128)(2,1)S(1)} collective-permute-done((bf16[192,1024]{1,0:T(8,128)(2,1)S(1)}, bf16[192,1024]{1,0:T(8,128)(2,1)S(1)}, u32[]{:S(2)}, u32[]{:S(2)}) %collective-permute-start.1) | collective-permute-done | bytes 393248 | tf_op jit(solution)/shard_map/ppermute | solution.py:150
  211.3 5.5 convert_reduce_fusion
  216.8 1.2 copy-done.31
  218.0 7.1 %multiply_reduce_fusion.2 = (f32[1024]{0:T(1024)}, f32[192]{0:T(256)S(1)}, f32[1024]{0:T(1024)}, f32[192,1024]{1,0:T(8,128)S(1)}) fusion(f32[192,1024]{1,0:T(8,128)S(1)} %copy-done.4, f32[192]{0:T(256)S(1)} %copy-done.65, f32[192]{0:T(256)S(1)} %copy-done.54, f32[1024]{0:T(1024)S(1)} %copy-done.42, bf16[192,4096]{1,0:T(8,128)(2,1)S(1)} %get-tuple-element.37, ...), kind=kOutput, calls=%fused_computation.127 | convolution fusion | flops 1612183296 | bytes 11548928 | tf_op jit(solution)/shard_map/dot_general | solution.py:171
  227.2 2.0 convolution_convert_fusion.3
  229.3 3.4 convolution_convert_fusion.6
  232.7 2.0 copy.67
  234.7 2.3 multiply_reduce_fusion
  240.9 4.8 convolution_convert_fusion.2
  247.4 5.7 convolution_convert_fusion.1
  254.1 7.6 %convolution_convert_fusion = bf16[4096,1024]{1,0:T(8,128)(2,1)} fusion(bf16[192,1024]{1,0:T(8,128)(2,1)S(1)} %copy-done.39, f32[192,4096]{1,0:T(8,128)} %convolution_add_fusion), kind=kOutput, calls=%fused_computation.1 | convolution fusion | flops 1621884928 | bytes 11927552 | tf_op jit(solution)/shard_map/dot_general | solution.py:165
  262.4 7.4 %fusion.44 = bf16[1,192,1024]{2,1,0:T(8,128)(2,1)} fusion(f32[192,1024]{1,0:T(8,128)S(1)} %copy-done.5, bf16[4096,1024]{1,0:T(8,128)(2,1)} %get-tuple-element.24, f32[1024]{0:T(1024)S(1)} %copy-done.77, f32[192,4096]{1,0:T(8,128)} %convolution_add_fusion), kind=kOutput, calls=%fused_computation.84 | convolution fusion | flops 1618280448 | bytes 12718080 | tf_op jit(solution)/shard_map/dot_general | solution.py:161
  269.8 21.8 %reduce-scatter.7.cloned.1.call-done = bf16[64,1024]{1,0:T(8,128)(2,1)} async-done(((bf16[1024,1024]{1,0:T(8,128)(2,1)}), bf16[64,1024]{1,0:T(8,128)(2,1)}) %reduce-scatter.7.cloned.1.call-update) | async-done | bytes 131088 | tf_op jit(solution)/shard_map/reduce_scatter | solution.py:327
  291.6 71.7 %reduce-scatter.5.cloned.1.call-done = bf16[64,3072]{1,0:T(8,128)(2,1)} async-done(((bf16[1024,3072]{1,0:T(8,128)(2,1)}), bf16[64,3072]{1,0:T(8,128)(2,1)}) %reduce-scatter.5.cloned.1.call-update) | async-done | bytes 393232 | tf_op jit(solution)/shard_map/reduce_scatter | solution.py:327
  363.3 75.6 %reduce-scatter.9.cloned.1.call-done = bf16[64,4096]{1,0:T(8,128)(2,1)} async-done(((bf16[1024,4096]{1,0:T(8,128)(2,1)}), bf16[64,4096]{1,0:T(8,128)(2,1)}) %reduce-scatter.9.cloned.1.call-update) | async-done | bytes 524304 | tf_op jit(solution)/shard_map/reduce_scatter | solution.py:327
  438.9 75.4 %reduce-scatter.11.cloned.1.call-done = bf16[256,1024]{1,0:T(8,128)(2,1)} async-done(((bf16[4096,1024]{1,0:T(8,128)(2,1)}), bf16[256,1024]{1,0:T(8,128)(2,1)}) %reduce-scatter.11.cloned.1.call-update) | async-done | bytes 524304 | tf_op jit(solution)/shard_map/reduce_scatter | solution.py:327
  514.4 5.7 fusion.137
  525.0 53.6 %psum.42 = f32[16,768]{1,0:T(8,128)S(1)} all-reduce(f32[16,768]{1,0:T(8,128)S(1)} %concatenate.17), channel_id=1, replica_groups=mesh['section'=2,'dp'=4,'shard'=16] {'shard'}, use_global_device_ids=true, to_apply=%region_31.32 | all-reduce | flops 12288 | bytes 98304 | tf_op jit(solution)/shard_map/psum | solution.py:338
  578.6 17.6 %psum.43 = f32[16,768]{1,0:T(8,128)S(1)} all-reduce(f32[16,768]{1,0:T(8,128)S(1)} %psum.42), channel_id=1, replica_groups=mesh['section'=2,'dp'=4,'shard'=16] {'dp'}, use_global_device_ids=true, to_apply=%region_32.33 | all-reduce | flops 12288 | bytes 98304 | tf_op jit(solution)/shard_map/psum | solution.py:338
  597.5 1.1 fusion.78
  598.5 2.0 broadcast_in_dim.131
  600.5 1.6 broadcast_in_dim.133
  602.2 2.1 broadcast_in_dim.135
  604.2 1.1 broadcast_in_dim.137
  (272 shorter events, 33.8 us)
Async XLA Ops:
  7.2 284.4 %reduce-scatter.7.cloned.1.call-start = ((), (), s32[]{:S(2)}) async-start(), calls=%async_computation.5 | async-start | bytes 2228224 | tf_op jit(solution)/shard_map/reduce_scatter | solution.py:327
  106.1 13.8 %copy-start.47 = (f32[1024]{0:T(1024)}, f32[1024]{0:T(1024)S(1)}, u32[]{:S(2)}) copy-start(f32[1024]{0:T(1024)S(1)} %add.249) | copy-start | bytes 12292
  106.2 38.9 %copy-start.78 = (f32[1024]{0:T(1024)}, f32[1024]{0:T(1024)S(1)}, u32[]{:S(2)}) copy-start(f32[1024]{0:T(1024)S(1)} %add.239) | copy-start | bytes 12292
  106.3 38.9 %copy-start.56 = (f32[1024]{0:T(1024)}, f32[1024]{0:T(1024)S(1)}, u32[]{:S(2)}) copy-start(f32[1024]{0:T(1024)S(1)} %mul.349) | copy-start | bytes 12292
  114.2 6.8 %copy-start.69 = (f32[2,2,8,128]{3,1,2,0:T(2,128)}, f32[2,2,8,128]{3,1,2,0:T(2,128)S(1)}, u32[]{:S(2)}) copy-start(f32[2,2,8,128]{3,1,2,0:T(2,128)S(1)} %copy.80) | copy-start | bytes 49156
  114.2 6.7 %copy-start.76 = (f32[1024]{0:T(1024)}, f32[1024]{0:T(1024)S(1)}, u32[]{:S(2)}) copy-start(f32[1024]{0:T(1024)S(1)} %add.262) | copy-start | bytes 12292
  114.3 6.7 %copy-start.44 = (f32[1024]{0:T(1024)}, f32[1024]{0:T(1024)S(1)}, u32[]{:S(2)}) copy-start(f32[1024]{0:T(1024)S(1)} %add.253) | copy-start | bytes 12292
  114.4 6.6 %copy-start.40 = (f32[1024]{0:T(1024)}, f32[1024]{0:T(1024)S(1)}, u32[]{:S(2)}) copy-start(f32[1024]{0:T(1024)S(1)} %mul.356) | copy-start | bytes 12292
  114.5 2.9 copy-start.21
  121.0 15.1 %copy-start.83 = (s32[192]{0:T(256)S(1)}, s32[192]{0:T(256)}, u32[]{:S(2)}) copy-start(s32[192]{0:T(256)} %param.18) | copy-start | bytes 2308
  130.8 13.8 %collective-permute-start = (bf16[192,1024]{1,0:T(8,128)(2,1)S(1)}, bf16[192,1024]{1,0:T(8,128)(2,1)S(1)}, u32[]{:S(2)}, u32[]{:S(2)}) collective-permute-start(bf16[192,1024]{1,0:T(8,128)(2,1)S(1)} %fusion.43), channel_id=1, source_target_pairs={{0,64},{1,65},{2,66},{3,67},{4,68},{5,69},{6,70},{7,71},{8,72},{9,... | collective-permute-start | bytes 1179656 | tf_op jit(solution)/shard_map/ppermute | solution.py:150
  144.8 5.7 copy-start.6
  144.8 5.7 copy-start.49
  153.8 3.7 copy-start.19
  153.8 3.7 copy-start.22
  155.8 5.5 slice-start.2
  157.6 3.8 slice-start.3
  189.1 3.4 slice-start.4
  192.5 18.8 %slice-start = ((s8[8388608]{0:T(1024)(128)(4,1)}), s8[4194304]{0:T(1024)(128)(4,1)S(1)}, s32[]{:S(2)}) async-start(s8[8388608]{0:T(1024)(128)(4,1)} %bitcast.180), calls=%async_computation.9 | async-start | bytes 8388608
  192.6 2.9 copy-start.61
  192.6 3.3 copy-start.18
  192.6 3.3 copy-start.67
  192.6 3.3 copy-start.72
  192.6 18.7 %slice-start.1 = ((s8[8388608]{0:T(1024)(128)(4,1)}), s8[4194304]{0:T(1024)(128)(4,1)S(1)}, s32[]{:S(2)}) async-start(s8[8388608]{0:T(1024)(128)(4,1)} %bitcast.180), calls=%async_computation.10 | async-start | bytes 8388608
  194.9 16.4 %copy-start.84 = (f32[192,4096]{1,0:T(8,128)S(1)}, f32[192,4096]{1,0:T(8,128)}, u32[]{:S(2)}) copy-start(f32[192,4096]{1,0:T(8,128)} %convolution_add_fusion) | copy-start | bytes 9437188
  196.3 14.2 %collective-permute-start.1 = (bf16[192,1024]{1,0:T(8,128)(2,1)S(1)}, bf16[192,1024]{1,0:T(8,128)(2,1)S(1)}, u32[]{:S(2)}, u32[]{:S(2)}) collective-permute-start(bf16[192,1024]{1,0:T(8,128)(2,1)S(1)} %add_convert_fusion.6), channel_id=1, source_target_pairs={{64,0},{65,1},{66,2},{67,3},{68,4},{69,5},{70,6},{71,7},{72,8},{73... | collective-permute-start | bytes 1179656 | tf_op jit(solution)/shard_map/ppermute | solution.py:150
  211.3 5.5 copy-start.38
  211.3 6.7 %copy-start.4 = (f32[192,1024]{1,0:T(8,128)S(1)}, f32[192,1024]{1,0:T(8,128)}, u32[]{:S(2)}) copy-start(f32[192,1024]{1,0:T(8,128)} %copy-done.3) | copy-start | bytes 2359300
  211.3 6.7 %copy-start.42 = (f32[1024]{0:T(1024)S(1)}, f32[1024]{0:T(1024)}, u32[]{:S(2)}) copy-start(f32[1024]{0:T(1024)} %copy-done.40) | copy-start | bytes 12292
  211.3 6.7 %copy-start.54 = (f32[192]{0:T(256)S(1)}, f32[192]{0:T(256)}, u32[]{:S(2)}) copy-start(f32[192]{0:T(256)} %copy-done.53) | copy-start | bytes 2308
  211.3 6.7 %copy-start.65 = (f32[192]{0:T(256)S(1)}, f32[192]{0:T(256)}, u32[]{:S(2)}) copy-start(f32[192]{0:T(256)} %copy-done.64) | copy-start | bytes 2308
  218.0 7.1 %copy-start.81 = (f32[192]{0:T(256)S(1)}, f32[192]{0:T(256)}, u32[]{:S(2)}) copy-start(f32[192]{0:T(256)} %get-tuple-element.49) | copy-start | bytes 2308
  229.2 5.5 copy-start.24
  229.3 134.0 %reduce-scatter.5.cloned.1.call-start = ((), (), s32[]{:S(2)}) async-start(), calls=%async_computation.4 | async-start | bytes 6684672 | tf_op jit(solution)/shard_map/reduce_scatter | solution.py:327
  245.8 193.1 %reduce-scatter.9.cloned.1.call-start = ((), (), s32[]{:S(2)}) async-start(), calls=%async_computation.6 | async-start | bytes 8912896 | tf_op jit(solution)/shard_map/reduce_scatter | solution.py:327
  253.1 261.2 %reduce-scatter.11.cloned.1.call-start = ((), (), s32[]{:S(2)}) async-start(), calls=%async_computation.7 | async-start | bytes 8912896 | tf_op jit(solution)/shard_map/reduce_scatter | solution.py:327
  261.7 336.8 %all-reduce.3.cloned.1.call-start = ((), (), s32[]{:S(2)}) async-start(), calls=%async_computation.8 | async-start | bytes 3145728 | tf_op jit(solution)/shard_map/psum | solution.py:328
  262.4 251.9 %copy-start.10 = (bf16[192,1024]{1,0:T(8,128)(2,1)S(1)}, bf16[192,1024]{1,0:T(8,128)(2,1)}, u32[]{:S(2)}) copy-start(bf16[192,1024]{1,0:T(8,128)(2,1)} %copy-done.6) | copy-start | bytes 1179652
  262.4 251.9 %copy-start.28 = (bf16[16,64,192]{2,1,0:T(8,128)(2,1)S(1)}, bf16[16,64,192]{2,1,0:T(8,128)(2,1)}, u32[]{:S(2)}) copy-start(bf16[16,64,192]{2,1,0:T(8,128)(2,1)} %copy-done.27) | copy-start | bytes 1179652
  262.4 251.9 %copy-start.34 = (bf16[16,64,192]{2,1,0:T(8,128)(2,1)S(1)}, bf16[16,64,192]{2,1,0:T(8,128)(2,1)}, u32[]{:S(2)}) copy-start(bf16[16,64,192]{2,1,0:T(8,128)(2,1)} %copy-done.33) | copy-start | bytes 1179652
  262.4 252.0 %copy-start.37 = (bf16[16,64,192]{2,1,0:T(8,128)(2,1)S(1)}, bf16[16,64,192]{2,1,0:T(8,128)(2,1)}, u32[]{:S(2)}) copy-start(bf16[16,64,192]{2,1,0:T(8,128)(2,1)} %copy-done.36) | copy-start | bytes 1179652
  262.4 252.0 %copy-start.52 = (f32[192]{0:T(256)S(1)}, f32[192]{0:T(256)}, u32[]{:S(2)}) copy-start(f32[192]{0:T(256)} %copy-done.49) | copy-start | bytes 2308
  262.4 252.0 %copy-start.59 = (f32[1024]{0:T(1024)S(1)}, f32[1024]{0:T(1024)}, u32[]{:S(2)}) copy-start(f32[1024]{0:T(1024)} %copy-done.56) | copy-start | bytes 12292
  514.3 5.7 copy-start.80
  514.4 5.7 copy-start.63
  514.4 9.8 %copy-start.68 = (f32[1024]{0:T(1024)S(1)}, f32[1024]{0:T(1024)}, u32[]{:S(2)}) copy-start(f32[1024]{0:T(1024)} %get-tuple-element.38) | copy-start | bytes 12292
  520.0 77.4 %copy-start.12 = (f32[192,1024]{1,0:T(8,128)S(1)}, f32[192,1024]{1,0:T(8,128)}, u32[]{:S(2)}) copy-start(f32[192,1024]{1,0:T(8,128)} %copy-done.11) | copy-start | bytes 2359300
  598.5 5.7 copy-start.35
  (50 other events, 75.8 us)
Sparse Core Ops, SparseCore 0:
  229.4 62.1 reduce-scatter.6
  294.0 69.2 reduce-scatter.4
  365.7 73.1 reduce-scatter.8
  441.1 73.0 reduce-scatter.10
  516.7 49.7 all-reduce.2

commit v3 on v2

v3 whole, which is shorter than its diff:
```python
import collections
import functools
import math

import jax
import jax.numpy as jnp
from jax import lax
from jax.experimental import pallas as pl
from jax.experimental.pallas import tpu as pltpu
from jax.sharding import PartitionSpec as P

HEADS = 16
SLOT = 96
GELU_A = math.sqrt(2.0 / math.pi)
GELU_B = 0.044715

norm_eps = 1e-05
masked_score = -1e30
MESH = pl.DeviceIdType.MESH
RING_FIRST = (1, 3)


def dot(left, right):
    return jnp.dot(left, right, preferred_element_type=jnp.float32)


def dot_rows(left, right):
    return lax.dot_general(
        left, right, (((0,), (0,)), ((), ())), preferred_element_type=jnp.float32
    )


def dot_back(left, right):
    return lax.dot_general(
        left, right, (((1,), (1,)), ((), ())), preferred_element_type=jnp.float32
    )


def gather_kernel(count, *refs):
    shards, fulls = refs[:count], refs[count : 2 * count]
    own_sem, send_sem, recv_sem = refs[2 * count :]
    me = lax.axis_index("shard")
    core, x, y = me % 2, (me // 2) % 4, me // 8

    def at(dy, dx):
        return (((y + dy) % 2) * 4 + (x + dx) % 4) * 2 + core

    sibling = me + 1 - 2 * core
    right, left, pair = at(0, 1), at(0, 3), at(1, 0)
    barrier = pltpu.get_barrier_semaphore()
    for other in (sibling, right, left, pair):
        pl.semaphore_signal(barrier, inc=1, device_id={"shard": other}, device_id_type=MESH)
    pl.semaphore_wait(barrier, 4)

    began = []

    def send(which, dy, dx, target, half=None):
        rows, width = shards[which].shape
        mine = dy == 0 and dx == 0
        spot = pl.ds(pl.multiple_of(at(dy, dx) * rows, 16), rows)
        cut = pl.ds(0, width) if half is None else pl.ds(half * (width // 2), width // 2)
        source = shards[which].at[:, cut] if mine else fulls[which].at[spot, cut]
        copy = pltpu.make_async_remote_copy(
            src_ref=source,
            dst_ref=fulls[which].at[spot, cut],
            send_sem=send_sem.at[len(began)],
            recv_sem=recv_sem.at[len(began)],
            device_id={"shard": target},
            device_id_type=MESH,
        )
        copy.start()
        began.append(copy)
        return copy

    pair_first = [k for k in range(count) if k not in RING_FIRST]
    ring_first = [k for k in range(count) if k in RING_FIRST]
    kept = []
    for k in range(count):
        rows = shards[k].shape[0]
        spot = pl.ds(pl.multiple_of(me * rows, 16), rows)
        copy = pltpu.make_async_copy(shards[k], fulls[k].at[spot, :], own_sem.at[k])
        copy.start()
        kept.append(copy)
    to_pair, to_right, to_left, shared = {}, {}, {}, []
    for k in pair_first:
        to_pair[k] = send(k, 0, 0, pair)
    for k in ring_first + pair_first:
        to_right[k] = send(k, 0, 0, right)
        to_left[k] = send(k, 0, 0, left)
    for k in ring_first:
        to_pair[k] = send(k, 0, 0, pair)
    for k in range(count):
        shared.append(send(k, 0, 0, sibling))
    pair_right, pair_left = {}, {}
    for k in pair_first:
        to_pair[k].wait_recv()
        pair_right[k] = send(k, 1, 0, right)
        pair_left[k] = send(k, 1, 0, left)
        shared.append(send(k, 1, 0, sibling))
    far, ring_pair = {}, {}
    for k in ring_first + pair_first:
        to_right[k].wait_recv()
        far[k, 0] = send(k, 0, 3, right, 0)
        if k in ring_first:
            ring_pair[k, 3] = send(k, 0, 3, pair)
        shared.append(send(k, 0, 3, sibling))
        to_left[k].wait_recv()
        far[k, 1] = send(k, 0, 1, left, 1)
        if k in ring_first:
            ring_pair[k, 1] = send(k, 0, 1, pair)
        shared.append(send(k, 0, 1, sibling))
    for k in ring_first:
        to_pair[k].wait_recv()
        shared.append(send(k, 1, 0, sibling))
    for k in ring_first:
        far[k, 0].wait_recv()
        far[k, 1].wait_recv()
        ring_pair[k, 2] = send(k, 0, 2, pair)
        shared.append(send(k, 0, 2, sibling))
    far_pair = {}
    for k in pair_first:
        pair_right[k].wait_recv()
        far_pair[k, 0] = send(k, 1, 3, right, 0)
        shared.append(send(k, 1, 3, sibling))
        pair_left[k].wait_recv()
        far_pair[k, 1] = send(k, 1, 1, left, 1)
        shared.append(send(k, 1, 1, sibling))
    for k in pair_first:
        far[k, 0].wait_recv()
        far[k, 1].wait_recv()
        shared.append(send(k, 0, 2, sibling))
    for k in ring_first:
        for dx in (3, 1):
            ring_pair[k, dx].wait_recv()
            shared.append(send(k, 1, dx, sibling))
    for k in pair_first:
        far_pair[k, 0].wait_recv()
        far_pair[k, 1].wait_recv()
        shared.append(send(k, 1, 2, sibling))
    for k in ring_first:
        ring_pair[k, 2].wait_recv()
        shared.append(send(k, 1, 2, sibling))
    for copy in shared:
        copy.wait_recv()
    for copy in began:
        copy.wait_send()
    for copy in kept:
        copy.wait()


def gather_all(arrays):
    count = len(arrays)
    copies = sum(16 if k in RING_FIRST else 17 for k in range(count))
    return pl.pallas_call(
        functools.partial(gather_kernel, count),
        out_shape=[jax.ShapeDtypeStruct((16 * a.shape[0], a.shape[1]), a.dtype) for a in arrays],
        in_specs=[pl.BlockSpec(memory_space=pl.ANY)] * count,
        out_specs=[pl.BlockSpec(memory_space=pl.ANY)] * count,
        scratch_shapes=[
            pltpu.SemaphoreType.DMA((count,)),
            pltpu.SemaphoreType.DMA((copies,)),
            pltpu.SemaphoreType.DMA((copies,)),
        ],
        compiler_params=pltpu.CompilerParams(collective_id=0, has_side_effects=True),
    )(*arrays)


def reduce_kernel(plans, *refs):
    count = len(plans)
    refs = list(refs)

    def take(number):
        taken = refs[:number]
        del refs[:number]
        return taken

    lefts, rights = take(count), take(count)
    outs = take(count)
    sums, from_sibling, to_sibling = take(count), take(count), take(count)
    half_left, half_right, full_left, full_right, from_pair = (take(count) for _ in range(5))
    quarters, merged, spread = take(count), take(count), take(count)
    send_sem, recv_sem = refs

    me, plane = lax.axis_index("shard"), lax.axis_index("dp")
    core, x, y = me % 2, (me // 2) % 4, me // 8

    def chip(dy, dx):
        return ((y + dy) % 2) * 4 + (x + dx) % 4

    sibling = me + 1 - 2 * core
    right, left, pair = (chip(0, 1) * 2 + core, chip(0, 3) * 2 + core, chip(1, 0) * 2 + core)
    barrier = pltpu.get_barrier_semaphore()
    neighbours = [{"shard": d} for d in (sibling, right, left, pair)]
    neighbours += [{"dp": (plane + k) % 4} for k in (1, 2, 3)]
    for other in neighbours:
        pl.semaphore_signal(barrier, inc=1, device_id=other, device_id_type=MESH)
    pl.semaphore_wait(barrier, len(neighbours))

    began = []

    def send(source, target, device):
        copy = pltpu.make_async_remote_copy(
            src_ref=source,
            dst_ref=target,
            send_sem=send_sem.at[len(began)],
            recv_sem=recv_sem.at[len(began)],
            device_id=device,
            device_id_type=MESH,
        )
        copy.start()
        began.append(copy)
        return copy

    def tiles(width, body, tile=512):
        tile = min(tile, width)

        @pl.loop(0, width // tile)
        def _(step):
            body(pl.ds(pl.multiple_of(step * tile, 128), tile))

    def add(where, *others):
        def body(cut):
            total = where[:, cut].astype(jnp.float32)
            for other in others:
                total = total + other[:, cut].astype(jnp.float32)
            where[:, cut] = total.astype(where.dtype)

        tiles(where.shape[1], body)

    width = [p.width for p in plans]
    lower = [pl.ds(0, w // 2) for w in width]
    upper = [pl.ds(w // 2, w // 2) for w in width]
    shared, waiting, slots = {}, [], [[] for _ in range(count)]
    halves, fulls, paired = {}, {}, {}

    def produce(k, dy, dx):
        rows, spot = plans[k].rows, dy * 4 + dx
        place = chip(dy, dx) * 2
        own = pl.ds(pl.multiple_of((place + core) * rows, rows), rows)
        others = pl.ds(pl.multiple_of((place + 1 - core) * rows, rows), rows)
        slot = len(slots[k]) % SLOTS
        if len(slots[k]) >= SLOTS:
            slots[k][-SLOTS].wait_send()
        if plans[k].product:
            both = jnp.concatenate([lefts[k][own, :], lefts[k][others, :]], axis=0)

            def body(cut):
                block = dot(both, rights[k][:, cut])
                sums[k][spot, :, cut] = block[:rows].astype(sums[k].dtype)
                to_sibling[k][slot, :, cut] = block[rows:].astype(sums[k].dtype)

            tiles(width[k], body, 256 if rows > 64 else 512)
        else:
            sums[k][spot] = lefts[k][own, :]
            to_sibling[k][slot] = lefts[k][others, :]
        copy = send(to_sibling[k].at[slot], from_sibling[k].at[spot], {"shard": sibling})
        shared[k, dy, dx] = copy
        slots[k].append(copy)
        waiting.append((k, dy, dx))
        if len(waiting) > 2:
            settle(*waiting[0])

    def send_halves(k, dy):
        part = dy if plans[k].ring_first else 0
        halves[k, dy, 0] = send(
            sums[k].at[dy * 4 + 2, :, lower[k]], half_left[k].at[part], {"shard": right}
        )
        halves[k, dy, 1] = send(
            sums[k].at[dy * 4 + 2, :, upper[k]], half_right[k].at[part], {"shard": left}
        )

    def settle(k, dy, dx):
        if (k, dy, dx) not in waiting:
            return
        waiting.remove((k, dy, dx))
        spot = dy * 4 + dx
        shared[k, dy, dx].wait_recv()
        add(sums[k].at[spot], from_sibling[k].at[spot])
        if plans[k].ring_first:
            if dx == 2:
                send_halves(k, dy)
        elif dy == 1:
            paired[k, dx] = send(sums[k].at[spot], from_pair[k].at[dx], {"shard": pair})

    def forward(k, dy):
        part = dy if plans[k].ring_first else 0
        settle(k, dy, 1)
        halves[k, dy, 0].wait_recv()
        add(sums[k].at[dy * 4 + 1, :, lower[k]], half_left[k].at[part])
        fulls[k, dy, 0] = send(sums[k].at[dy * 4 + 1], full_left[k].at[part], {"shard": right})
        settle(k, dy, 3)
        halves[k, dy, 1].wait_recv()
        add(sums[k].at[dy * 4 + 3, :, upper[k]], half_right[k].at[part])
        fulls[k, dy, 1] = send(sums[k].at[dy * 4 + 3], full_right[k].at[part], {"shard": left})

    def meet(k, dx):
        settle(k, 0, dx)
        paired[k, dx].wait_recv()
        add(sums[k].at[dx], from_pair[k].at[dx])

    def ring_end(k, dy):
        part = dy if plans[k].ring_first else 0
        settle(k, dy, 0)
        fulls[k, dy, 0].wait_recv()
        fulls[k, dy, 1].wait_recv()
        add(sums[k].at[dy * 4], full_left[k].at[part], full_right[k].at[part])

    def cut_of(k, which):
        quarter = width[k] // 4
        return pl.ds(pl.multiple_of(which * quarter, 128), quarter)

    scattered, returned = {}, {}

    def scatter_planes(k):
        for hop in (2, 1, 3):
            there = (plane + hop) % 4
            scattered[k, hop] = send(sums[k].at[0, :, cut_of(k, there)], quarters[k].at[hop - 1], {"dp": there})

    def return_planes(k):
        for hop in (1, 2, 3):
            scattered[k, hop].wait_recv()
        total = sums[k][0, :, cut_of(k, plane)].astype(jnp.float32)
        for hop in range(3):
            total = total + quarters[k][hop].astype(jnp.float32)
        merged[k][...] = total.astype(merged[k].dtype)
        spread[k][:, cut_of(k, plane)] = merged[k][...]
        for hop in (2, 1, 3):
            there = (plane + hop) % 4
            returned[k, hop] = send(merged[k], spread[k].at[:, cut_of(k, plane)], {"dp": there})

    def finish(k):
        for hop in (1, 2, 3):
            returned[k, hop].wait_recv()

        def body(cut):
            outs[k][:, cut] = spread[k][:, cut].astype(jnp.float32)

        tiles(width[k], body)

    down, up, out, joint, vectors = range(5)
    for k, dy, dx in (
        (up, 1, 2), (up, 0, 2), (down, 1, 2), (joint, 1, 2), (joint, 0, 2), (down, 1, 1), (down, 1, 3),
        (down, 1, 0), (vectors, 1, 2), (vectors, 0, 2),
    ):
        produce(k, dy, dx)
    for dy in (1, 0):
        produce(up, dy, 1)
        produce(up, dy, 3)
        forward(up, dy)
    for dx in (2, 1, 3, 0):
        produce(out, 1, dx)
    for dy in (1, 0):
        produce(joint, dy, 1)
        produce(joint, dy, 3)
        forward(joint, dy)
    produce(down, 0, 2)
    meet(down, 2)
    send_halves(down, 0)
    for dy in (1, 0):
        produce(vectors, dy, 1)
        produce(vectors, dy, 3)
        forward(vectors, dy)
    produce(out, 0, 2)
    meet(out, 2)
    send_halves(out, 0)
    produce(up, 1, 0)
    ring_end(up, 1)
    paired[up, 0] = send(sums[up].at[4], from_pair[up].at[0], {"shard": pair})
    for k in (down, out):
        produce(k, 0, 1)
        produce(k, 0, 3)
        meet(k, 1)
        meet(k, 3)
        forward(k, 0)
    for k in (joint, vectors):
        produce(k, 1, 0)
        ring_end(k, 1)
        paired[k, 0] = send(sums[k].at[4], from_pair[k].at[0], {"shard": pair})
    for k in (up, joint, vectors):
        produce(k, 0, 0)
        ring_end(k, 0)
        paired[k, 0].wait_recv()
        add(sums[k].at[0], from_pair[k].at[0])
        scatter_planes(k)
    return_planes(up)
    for k in (down, out):
        produce(k, 0, 0)
        meet(k, 0)
        ring_end(k, 0)
        scatter_planes(k)
    for k in (joint, vectors, down, out):
        return_planes(k)
    for k in (up, joint, vectors, down, out):
        finish(k)
    kept_back = {id(c) for per in slots for c in per[:-SLOTS]}
    for copy in began:
        if id(copy) not in kept_back:
            copy.wait_send()


Plan = collections.namedtuple("Plan", ("rows", "width", "product", "ring_first", "dtype"))
SLOTS = 3


def reduce_all(pairs, vectors):
    plans = [
        Plan(left.shape[0] // 16, right.shape[1], True, k in (1, 3), jnp.bfloat16)
        for k, (left, right) in enumerate(pairs)
    ]
    plans.append(Plan(vectors.shape[0] // 16, vectors.shape[1], False, True, jnp.float32))
    lefts = [left for left, _ in pairs] + [vectors]
    rights = [right for _, right in pairs] + [jnp.zeros((8, 128), jnp.float32)]

    def room(depth, part=1):
        return [
            pltpu.VMEM((depth(p) if callable(depth) else depth, p.rows, p.width // part), p.dtype) for p in plans
        ]

    ring_parts = lambda p: 2 if p.ring_first else 1
    scratch = room(8) + room(8) + room(SLOTS)
    scratch += room(ring_parts, 2) + room(ring_parts, 2) + room(ring_parts) + room(ring_parts)
    scratch += room(lambda p: 1 if p.ring_first else 4)
    scratch += room(3, 4)
    scratch += [pltpu.VMEM((p.rows, p.width // 4), p.dtype) for p in plans]
    scratch += [pltpu.VMEM((p.rows, p.width), p.dtype) for p in plans]
    copies = sum(8 + (9 if p.ring_first else 8) + 6 for p in plans)
    return pl.pallas_call(
        functools.partial(reduce_kernel, plans),
        out_shape=[jax.ShapeDtypeStruct((p.rows, p.width), jnp.float32) for p in plans],
        in_specs=[pl.BlockSpec(memory_space=pltpu.VMEM)] * (2 * len(plans)),
        out_specs=[pl.BlockSpec(memory_space=pltpu.VMEM)] * len(plans),
        scratch_shapes=scratch
        + [pltpu.SemaphoreType.DMA((copies,)), pltpu.SemaphoreType.DMA((copies,))],
        compiler_params=pltpu.CompilerParams(
            collective_id=1, has_side_effects=True, vmem_limit_bytes=62 * 1024 * 1024
        ),
    )(*lefts, *rights)


def relay_kernel(
    rows, cotangent, allowed, vec, bias_qkv, bias_up, hbm_qkv, hbm_out, hbm_up, hbm_down,
    section_out, section_grad, hidden_t, second_t, attended_t, normed_t, du, dbefore, db, dprojected, sums, sum_up,
    w_qkv, w_out, w_up, w_down, x, hat_one, scale_one, normed, qkv, probs, attended, middle, hat_two, scale_two,
    second, slope, hidden, wide, dmiddle, dattended, ship_out, ship_grad, land_out, land_grad,
    load_sem, send_sem, recv_sem,
):
    section = lax.axis_index("section")
    first = section == 0
    loads = [
        pltpu.make_async_copy(source, target, load_sem.at[k])
        for k, (source, target) in enumerate(
            ((hbm_qkv, w_qkv), (hbm_out, w_out), (hbm_up, w_up), (hbm_down, w_down))
        )
    ]
    for load in loads:
        load.start()
    barrier = pltpu.get_barrier_semaphore()
    pl.semaphore_signal(barrier, inc=1, device_id={"section": 1 - section}, device_id_type=MESH)
    pl.semaphore_wait(barrier, 1)

    def hop(source, target, k):
        return pltpu.make_async_remote_copy(
            src_ref=source, dst_ref=target, send_sem=send_sem.at[k], recv_sem=recv_sem.at[k],
            device_id={"section": 1 - section}, device_id_type=MESH,
        )

    def tiles(width, body, tile=512):
        @pl.loop(0, width // tile)
        def _(step):
            body(pl.ds(pl.multiple_of(step * tile, 128), tile))

    ln1_gain, ln1_bias, _, _, b_out, ln2_gain, ln2_bias, b_down = (vec[k : k + 1, :] for k in range(8))
    lane = lax.broadcasted_iota(jnp.int32, (SLOT, 128), 1)
    low_half = lane < 64
    halves = (low_half, jnp.logical_not(low_half))

    def standard(values):
        centered = values - jnp.mean(values, axis=-1, keepdims=True)
        scale = lax.rsqrt(jnp.mean(centered * centered, axis=-1, keepdims=True) + norm_eps)
        return centered * scale, scale

    def only(which, values):
        return jnp.where(halves[which], values, jnp.zeros_like(values))

    def forward(result, before_use):
        hat, scale = standard(x[...].astype(jnp.float32))
        hat_one[...] = hat
        scale_one[...] = scale
        normed[...] = (hat * ln1_gain + ln1_bias).astype(jnp.bfloat16)
        before_use(0)

        def project(cut):
            qkv[:, cut] = (dot(normed[...], w_qkv[:, cut]) + bias_qkv[:, cut]).astype(jnp.bfloat16)

        tiles(3072, project)

        @pl.loop(0, HEADS // 2)
        def _(couple):
            cuts = [pl.ds(pl.multiple_of(couple * 128 + 1024 * k, 128), 128) for k in range(3)]
            for slot in range(2):
                spot = pl.ds(slot * SLOT, SLOT)
                query, key, value = (qkv[spot, cut] for cut in cuts)
                mixed = []
                for which in range(2):
                    scores = dot_back(query, only(which, key)) * 0.125
                    scores = jnp.where(allowed[slot] > 0, scores, masked_score)
                    exponent = jnp.exp(scores - jnp.max(scores, axis=-1, keepdims=True))
                    prob = exponent / jnp.sum(exponent, axis=-1, keepdims=True)
                    probs[couple * 4 + slot * 2 + which] = prob
                    mixed.append(dot(prob.astype(jnp.bfloat16), value))
                attended[spot, cuts[0]] = jnp.where(low_half, *mixed).astype(jnp.bfloat16)

        before_use(1)

        def mix(cut):
            branch = dot(attended[...], w_out[:, cut]) + vec[4:5, cut]
            middle[:, cut] = x[:, cut].astype(jnp.float32) + branch

        tiles(1024, mix)
        hat, scale = standard(middle[...])
        hat_two[...] = hat
        scale_two[...] = scale
        second[...] = (hat * ln2_gain + ln2_bias).astype(jnp.bfloat16)
        before_use(2)

        def grow(cut):
            before = dot(second[...], w_up[:, cut]) + bias_up[:, cut]
            square = before * before
            bend = jnp.tanh(GELU_A * (before + GELU_B * before * square))
            half = 0.5 * (1.0 + bend)
            hidden[:, cut] = (before * half).astype(jnp.bfloat16)
            slope[:, cut] = half + (0.5 * GELU_A) * before * (1.0 - bend * bend) * (1.0 + (3.0 * GELU_B) * square)

        tiles(4096, grow, 256)
        before_use(3)

        def shrink(cut):
            result[:, cut] = (middle[:, cut] + dot(hidden[...], w_down[:, cut]) + vec[7:8, cut]).astype(jnp.bfloat16)

        tiles(1024, shrink)

    def norm_back(hat, scale, grad, gain):
        inner = grad * gain
        return scale * (
            inner
            - jnp.mean(inner, axis=-1, keepdims=True)
            - hat * jnp.mean(inner * hat, axis=-1, keepdims=True)
        )

    def total(values):
        return jnp.sum(values.astype(jnp.float32), axis=0, keepdims=True)

    def backward(result, last):
        def grow_back(cut):
            grad = dot_back(du[...], w_down[cut, :]) * slope[:, cut]
            dbefore[:, cut] = grad.astype(jnp.bfloat16)
            if last:
                sum_up[:, cut] = total(dbefore[:, cut])

        tiles(4096, grow_back)

        def second_back(cut):
            wide[:, cut] = dot_back(dbefore[...], w_up[cut, :])

        tiles(1024, second_back)
        grad = wide[...]
        if last:
            sums[5:6, :] = jnp.sum(grad * hat_two[...], axis=0, keepdims=True)
            sums[6:7, :] = total(grad)
            sums[7:8, :] = total(du[...])
        dmiddle[...] = du[...].astype(jnp.float32) + norm_back(hat_two[...], scale_two[...], grad, ln2_gain)
        db[...] = dmiddle[...].astype(jnp.bfloat16)

        def mix_back(cut):
            dattended[:, cut] = dot_back(db[...], w_out[cut, :]).astype(jnp.bfloat16)

        tiles(1024, mix_back)

        @pl.loop(0, HEADS // 2)
        def _(couple):
            cuts = [pl.ds(pl.multiple_of(couple * 128 + 1024 * k, 128), 128) for k in range(3)]
            for slot in range(2):
                spot = pl.ds(slot * SLOT, SLOT)
                query, key, value = (qkv[spot, cut] for cut in cuts)
                grad = dattended[spot, cuts[0]]
                parts = ([], [], [])
                for which in range(2):
                    prob = probs[couple * 4 + slot * 2 + which]
                    dprob = dot_back(only(which, grad), value)
                    delta = jnp.sum(prob * dprob, axis=-1, keepdims=True)
                    dscore = (prob * (dprob - delta)).astype(jnp.bfloat16)
                    parts[0].append(dot(dscore, key) * 0.125)
                    parts[1].append(dot_rows(dscore, query) * 0.125)
                    parts[2].append(dot_rows(prob.astype(jnp.bfloat16), grad))
                for cut, part in zip(cuts, parts):
                    dprojected[spot, cut] = jnp.where(low_half, *part).astype(jnp.bfloat16)

        def normed_back(cut):
            wide[:, cut] = dot_back(dprojected[...], w_qkv[cut, :])

        tiles(1024, normed_back)
        grad = wide[...]
        result[...] = (dmiddle[...] + norm_back(hat_one[...], scale_one[...], grad, ln1_gain)).astype(jnp.bfloat16)
        if last:
            sums[0:1, :] = jnp.sum(grad * hat_one[...], axis=0, keepdims=True)
            sums[1:2, :] = total(grad)
            sums[2:3, :] = total(dprojected[:, :1024])
            sums[3:4, :] = total(dprojected[:, 2048:])
            sums[4:5, :] = total(db[...])

    x[...] = rows[...]
    forward(ship_out, lambda k: loads[k].wait())
    there = hop(ship_out, land_out, 0)
    there.start()
    there.wait()
    x[...] = jnp.where(first, rows[...], land_out[...])
    forward(section_out, lambda k: None)
    du[...] = cotangent[...]
    backward(ship_grad, False)
    back = hop(ship_grad, land_grad, 1)
    back.start()

    def flip(source, target):
        def body(cut):
            target[cut, :] = source[:, cut].T

        tiles(source.shape[1], body, 256)

    for source, target in ((hidden, hidden_t), (second, second_t), (attended, attended_t), (normed, normed_t)):
        flip(source, target)
    back.wait()
    du[...] = jnp.where(first, land_grad[...], cotangent[...])
    backward(section_grad, True)


def relay(rows, cotangent, allowed, vec, bias_qkv, bias_up, mats):
    tall, width, wide = rows.shape[0], rows.shape[1], mats[2].shape[1]
    low, full = jnp.bfloat16, jnp.float32
    outs = [
        ((tall, width), low), ((tall, width), low), ((wide, tall), low), ((width, tall), low), ((width, tall), low),
        ((width, tall), low), ((tall, width), low), ((tall, wide), low), ((tall, width), low),
        ((tall, 3 * width), low), ((8, width), full), ((1, wide), full),
    ]
    scratch = [(m.shape, low) for m in mats] + [
        ((tall, width), low), ((tall, width), full), ((tall, 1), full), ((tall, width), low),
        ((tall, 3 * width), low), ((2 * HEADS, SLOT, SLOT), full), ((tall, width), low), ((tall, width), full),
        ((tall, width), full), ((tall, 1), full), ((tall, width), low), ((tall, wide), full), ((tall, wide), low),
        ((tall, width), full), ((tall, width), full), ((tall, width), low),
    ] + [((tall, width), low)] * 4
    in_vmem, anywhere = pl.BlockSpec(memory_space=pltpu.VMEM), pl.BlockSpec(memory_space=pl.ANY)
    return pl.pallas_call(
        relay_kernel,
        out_shape=[jax.ShapeDtypeStruct(*o) for o in outs],
        in_specs=[in_vmem] * 6 + [anywhere] * 4,
        out_specs=[in_vmem] * len(outs),
        scratch_shapes=[pltpu.VMEM(*s) for s in scratch]
        + [pltpu.SemaphoreType.DMA((n,)) for n in (4, 2, 2)],
        compiler_params=pltpu.CompilerParams(
            collective_id=2, has_side_effects=True, vmem_limit_bytes=62 * 1024 * 1024
        ),
    )(rows, cotangent, allowed, vec, bias_qkv, bias_up, *mats)


def allowed_pairs(segment):
    by_slot = segment.reshape(-1, SLOT)
    positions = jnp.arange(SLOT)
    allowed = (by_slot[:, :, None] == by_slot[:, None, :]) & (positions[None, :] <= positions[:, None])
    return allowed.astype(jnp.float32)


def on_device(
    ends, segment_ids, token_mask,
    ln1_gain, ln1_bias, w_qkv, b_query, b_value, w_out, b_out,
    ln2_gain, ln2_bias, w_up, b_up, w_down, b_down,
):
    width = ends.shape[2]
    shard_count = lax.axis_size("shard")
    packed = jnp.concatenate([ln1_gain, ln1_bias, b_query, b_value, b_out, ln2_gain, ln2_bias, b_down, b_up], axis=1)
    tall = jnp.broadcast_to(packed, (16, packed.shape[1]))
    *mats, everyone = gather_all((w_qkv[0], w_out[0], w_up[0], w_down[0], tall))
    everyone = everyone.reshape(shard_count, *tall.shape)[:, 0].astype(jnp.float32)
    piece = width // shard_count
    vec = everyone[:, : 8 * piece].reshape(shard_count, 8, piece).transpose(1, 0, 2).reshape(8, width)
    bias_up = everyone[:, 8 * piece :].reshape(1, -1)
    bias_qkv = jnp.concatenate([vec[2:3], jnp.zeros((1, width), jnp.float32), vec[3:4]], axis=1)

    local_rows = ends[0]
    cotangent = local_rows * token_mask[:, None].astype(jnp.bfloat16)
    (
        section_out, section_grad, hidden_t, second_t, attended_t, normed_t, du, dbefore, db, dprojected, sums, sum_up,
    ) = relay(local_rows, cotangent, allowed_pairs(segment_ids), vec, bias_qkv, bias_up, mats)

    rows = jnp.concatenate(
        [
            sums.reshape(8, shard_count, piece).transpose(1, 0, 2).reshape(shard_count, 8 * piece),
            sum_up.reshape(shard_count, -1),
        ],
        axis=1,
    )
    spread = jnp.pad(rows[:, None], ((0, 0), (0, 7), (0, 1024 - rows.shape[1])))
    g_down, g_up, g_out, g_qkv, mine = reduce_all(
        ((hidden_t, du), (second_t, dbefore), (attended_t, db), (normed_t, dprojected)), spread.reshape(-1, 1024)
    )
    out = [mine[:1, k * piece : (k + 1) * piece] for k in range(8)]
    g_ln1_gain, g_ln1_bias, g_query, g_value, g_b_out, g_ln2_gain, g_ln2_bias, g_b_down = out
    g_b_up = mine[:1, 8 * piece : 8 * piece + b_up.shape[1]]
    return (
        section_out[None], section_grad[None], g_ln1_gain, g_ln1_bias, g_qkv[None], g_query, g_value, g_out[None],
        g_b_out, g_ln2_gain, g_ln2_bias, g_up[None], g_b_up, g_down[None], g_b_down,
    )


def solution(mesh):
    vector, matrix = P("section", "shard"), P("section", "shard", None)
    rows, ids = P("section", ("dp", "shard"), None), P(("dp", "shard"))
    in_specs = (
        rows, ids, ids, vector, vector, matrix, vector, vector, matrix, vector, vector, vector, matrix,
        vector, matrix, vector,
    )
    out_specs = (
        rows, rows, vector, vector, matrix, vector, vector, matrix, vector, vector, vector, matrix, vector,
        matrix, vector,
    )
    return jax.shard_map(on_device, mesh=mesh, in_specs=in_specs, out_specs=out_specs, check_vma=False)
```

time: 621 us -> 360 us (0.58); the launches traced: 612 us -> 359 us
  waiting for transfers between devices: 265 us -> 0 us
  Pallas kernels: 91 us -> 338 us
  matrix products: 108 us -> 0 us
  blocking collectives: 71.2 us -> 0 us
  other arithmetic: 24.5 us -> 3.65 us
  between operations: 15.3 us -> 0.81 us
  local copies, waits for them, and re-layouts: 29.9 us -> 16.1 us
  starting transfers between devices: 7.06 us -> 0 us
    pallas_call x0 -> x2, Pallas kernels: none -> 247 us  [the longest x1 131 us: reduce_all(): pl.pallas_call(functools.partial(reduce_kernel, plans), out_shape=[jax.Sh...]
    reduce_scatter x4 -> x0, waiting for transfers between devices: 244 us -> none  [on_device(): lax.psum_scatter(p, 'shard', scatter_dimension=0, tiled=True)]
    dot_general x29 -> x0, matrix products: 105 us -> none  [the longest x7 40.3 us: dot_back(): lax.dot_general(left, right, (((1,), (1,)), ((), ())), preferred_element_...]
    psum x2 -> x0, blocking collectives: 71.2 us -> none  [on_device(): rows = lax.psum(lax.psum(rows, 'shard'), 'dp')]
    ppermute x2 -> x0, waiting for transfers between devices: 20.8 us -> none  [swap_section(): return lax.ppermute(value, 'section', pairs)]
    reduce_sum x15 -> x0, other arithmetic: 9.86 us -> none  [the longest x3 2.38 us: normalize(): centered = values - row_mean]
    broadcast_in_dim x5 -> x0, other arithmetic: 7.83 us -> none  [the longest x4 6.78 us: on_device(): summed = [lax.psum(s, 'dp').astype(jnp.float32)[None] for s in summed]]
    ppermute x2 -> x0, starting transfers between devices: 6.6 us -> none  [swap_section(): return lax.ppermute(value, 'section', pairs)]
  transfers between devices with their start and end apart: 7 -> 0, of which waited for: 6 -> 0; matrix products, arithmetic and copies ran while one was open for 8% -> 0% of each run, Pallas kernels for 0% -> 0%
where the time goes in v3:
time: 360 us; the launch traced here: 359 us
  Pallas kernels  338 us (94%)
  local copies, waits for them, and re-layouts  16.1 us (4%)
  other arithmetic  3.65 us (1%)
    pallas_call x1, Pallas kernels, reduce_all(): pl.pallas_call(functools.partial(reduce_kernel, plans), out_shape=[jax.Sh...  131 us
    pallas_call x1, Pallas kernels, relay(): pl.pallas_call(relay_kernel, out_shape=[jax.ShapeDtypeStruct(*o) for o in...  116 us
    pallas_call x1, Pallas kernels, gather_all(): pl.pallas_call(functools.partial(gather_kernel, count), out_shape=[jax.Sh...  91 us

profile of v3, /device:TPU:0, one launch (start us, length us, event | category | flops | bytes accessed | tf_op | source)
XLA Modules:
  0.0 358.9 jit_solution(10978974515204069103)
XLA Ops:
  0.6 0.0 copy-start.7
  0.7 0.0 copy-start
  0.7 0.0 copy-start.6
  0.7 0.9 concatenate.9
  1.6 0.6 broadcast_in_dim.39.refs_4_
  2.2 91.0 %shard_map.271 = (bf16[1024,3072]{1,0:T(8,128)(2,1)}, bf16[1024,1024]{1,0:T(8,128)(2,1)}, bf16[1024,4096]{1,0:T(8,128)(2,1)}, bf16[4096,1024]{1,0:T(8,128)(2,1)}, bf16[256,768]{1,0:T(8,128)(2,1)}) custom-call(bf16[64,3072]{1,0:T(8,128)(2,1)} %bitcast.37, bf16[64,1024]{1,0:T(8,128)(2,1)} %bitcast.42, bf16[64,4096]{1,0:T(8,128)(2,1)} %bitcast.33, ...), custom_call_target="tpu_custom_call" | custom-call | tf_op jit(solution)/shard_map/pallas_call | solution.py:154
  93.3 1.0 slice.64
  94.3 0.1 reshape.75
  94.4 0.1 slice.51
  94.5 0.1 slice.53
  94.5 0.6 pad_maximum_fusion.1.bias_qkv
  95.2 0.7 reshape.76.vec
  95.9 0.6 copy.35
  96.5 0.0 copy-done.7
  96.5 0.0 copy-done
  96.5 0.8 broadcast_multiply_fusion.cotangent
  97.3 0.0 copy-done.6
  97.4 0.1 eq.15
  97.4 0.7 and_convert_fusion.allowed
  98.2 116.4 %shard_map.272 = (bf16[192,1024]{1,0:T(8,128)(2,1)}, bf16[192,1024]{1,0:T(8,128)(2,1)}, bf16[4096,192]{1,0:T(8,128)(2,1)}, bf16[1024,192]{1,0:T(8,128)(2,1)}, bf...) custom-call(bf16[192,1024]{1,0:T(8,128)(2,1)} %bitcast.29, ...), custom_call_target="tpu_custom_call" | custom-call | tf_op jit(solution)/shard_map/pallas_call | solution.py:651
  214.5 0.8 reshape.78
  215.4 0.1 reshape.79
  215.5 0.5 broadcast.13
  216.0 1.4 reduce.4
  217.5 0.8 pad_bitcast_fusion.refs_4_
  218.3 0.6 broadcast_in_dim.44.refs_9_
  218.9 0.0 copy-start.4
  218.9 0.0 copy-start.3
  218.9 131.0 %shard_map.273 = (f32[256,1024]{1,0:T(8,128)}, f32[64,4096]{1,0:T(8,128)}, f32[64,1024]{1,0:T(8,128)}, f32[64,3072]{1,0:T(8,128)}, f32[8,1024]{1,0:T(8,128)}) custom-call(bf16[4096,192]{1,0:T(8,128)(2,1)} %get-tuple-element.44.refs_0_, bf16[1024,192]{1,0:T(8,128)(2,1)} %get-tuple-element.45.refs_1_, bf16[1024,192]{1,0:T(8,128)(2,1)} %get-tuple-element.46.refs_2_, ...), custom_call_target="tpu_custom_call" | custom-call | tf_op jit(solution)/shard_map/pallas_call | solution.py:427
  349.9 0.0 copy-start.5
  350.0 0.0 copy-start.2
  350.0 1.4 fusion.2
  351.4 1.3 slice.62
  352.6 0.0 copy-done.4
  352.6 0.7 copy.47
  353.4 0.0 copy-done.3
  353.4 0.7 copy.48
  354.1 0.0 copy-start.1
  354.1 2.2 copy.49
  356.3 0.0 copy-done.5
  356.3 0.7 copy.50
  357.0 0.0 copy-done.2
  357.0 1.0 copy.51
  358.0 0.0 copy-done.1
  358.0 1.0 copy.52
  (14 shorter events, 0.2 us)
Async XLA Ops:
  0.6 95.8 %copy-start.7 = (s32[192]{0:T(256)S(1)}, s32[192]{0:T(256)}, u32[]{:S(2)}) copy-start(s32[192]{0:T(256)} %param.18) | copy-start | bytes 2308
  0.7 95.8 %copy-start = (bf16[1,192,1024]{2,1,0:T(8,128)(2,1)S(1)}, bf16[1,192,1024]{2,1,0:T(8,128)(2,1)}, u32[]{:S(2)}) copy-start(bf16[1,192,1024]{2,1,0:T(8,128)(2,1)} %param.16) | copy-start | bytes 1179652
  0.7 96.7 %copy-start.6 = (s32[192]{0:T(256)S(1)}, s32[192]{0:T(256)}, u32[]{:S(2)}) copy-start(s32[192]{0:T(256)} %param.17) | copy-start | bytes 2308
  218.9 133.7 %copy-start.4 = (bf16[192,1024]{1,0:T(8,128)(2,1)S(1)}, bf16[192,1024]{1,0:T(8,128)(2,1)}, u32[]{:S(2)}) copy-start(bf16[192,1024]{1,0:T(8,128)(2,1)} %get-tuple-element.42) | copy-start | bytes 1179652
  218.9 134.5 %copy-start.3 = (bf16[192,1024]{1,0:T(8,128)(2,1)S(1)}, bf16[192,1024]{1,0:T(8,128)(2,1)}, u32[]{:S(2)}) copy-start(bf16[192,1024]{1,0:T(8,128)(2,1)} %get-tuple-element.43) | copy-start | bytes 1179652
  349.9 6.3 %copy-start.5 = (f32[64,1024]{1,0:T(8,128)S(1)}, f32[64,1024]{1,0:T(8,128)}, u32[]{:S(2)}) copy-start(f32[64,1024]{1,0:T(8,128)} %get-tuple-element.56) | copy-start | bytes 786436
  350.0 7.0 %copy-start.2 = (f32[64,4096]{1,0:T(8,128)S(1)}, f32[64,4096]{1,0:T(8,128)}, u32[]{:S(2)}) copy-start(f32[64,4096]{1,0:T(8,128)} %get-tuple-element.57) | copy-start | bytes 3145732
  354.1 3.8 %copy-start.1 = (f32[256,1024]{1,0:T(8,128)S(1)}, f32[256,1024]{1,0:T(8,128)}, u32[]{:S(2)}) copy-start(f32[256,1024]{1,0:T(8,128)} %get-tuple-element.58) | copy-start | bytes 3145732

commit v4 on v3

--- a/solution.py
+++ b/solution.py
@@ -4,6 +4,7 @@
 
 import jax
 import jax.numpy as jnp
+import numpy as np
 from jax import lax
 from jax.experimental import pallas as pl
 from jax.experimental.pallas import tpu as pltpu
@@ -17,7 +18,10 @@
 norm_eps = 1e-05
 masked_score = -1e30
 MESH = pl.DeviceIdType.MESH
-RING_FIRST = (1, 3)
+SCALE = np.array(0.125, jnp.bfloat16)
+RING_FIRST = (3,)
+SPREAD = 2
+FIRST_USED = (2, 4, 0, 1, 3)
 
 
 def dot(left, right):
@@ -39,7 +43,7 @@
 def gather_kernel(count, *refs):
     shards, fulls = refs[:count], refs[count : 2 * count]
     own_sem, send_sem, recv_sem = refs[2 * count :]
-    me = lax.axis_index("shard")
+    me, plane = lax.axis_index("shard"), lax.axis_index("dp")
     core, x, y = me % 2, (me // 2) % 4, me // 8
 
     def at(dy, dx):
@@ -48,32 +52,49 @@
     sibling = me + 1 - 2 * core
     right, left, pair = at(0, 1), at(0, 3), at(1, 0)
     barrier = pltpu.get_barrier_semaphore()
-    for other in (sibling, right, left, pair):
-        pl.semaphore_signal(barrier, inc=1, device_id={"shard": other}, device_id_type=MESH)
-    pl.semaphore_wait(barrier, 4)
+    neighbours = [{"shard": d} for d in (sibling, right, left, pair)]
+    neighbours += [{"dp": (plane + k) % 4} for k in (1, 2, 3)]
+    for other in neighbours:
+        pl.semaphore_signal(barrier, inc=1, device_id=other, device_id_type=MESH)
+    pl.semaphore_wait(barrier, len(neighbours))
 
     began = []
 
-    def send(which, dy, dx, target, half=None):
+    def send(which, dy, dx, target, half=None, whole=False):
         rows, width = shards[which].shape
         mine = dy == 0 and dx == 0
         spot = pl.ds(pl.multiple_of(at(dy, dx) * rows, 16), rows)
-        cut = pl.ds(0, width) if half is None else pl.ds(half * (width // 2), width // 2)
+        start = 0
+        if which == SPREAD and not whole:
+            width = width // 4
+            start = pl.multiple_of(plane * width, 128)
+        cut = pl.ds(start, width)
+        if half is not None:
+            cut = pl.ds(start + half * (width // 2), width // 2)
         source = shards[which].at[:, cut] if mine else fulls[which].at[spot, cut]
         copy = pltpu.make_async_remote_copy(
             src_ref=source,
             dst_ref=fulls[which].at[spot, cut],
             send_sem=send_sem.at[len(began)],
             recv_sem=recv_sem.at[len(began)],
-            device_id={"shard": target},
+            device_id=target if isinstance(target, dict) else {"shard": target},
             device_id_type=MESH,
         )
         copy.start()
         began.append(copy)
         return copy
 
-    pair_first = [k for k in range(count) if k not in RING_FIRST]
-    ring_first = [k for k in range(count) if k in RING_FIRST]
+    spreads = []
+
+    def share(which, dy, dx):
+        if which == SPREAD and (dy, dx) != (0, 0):
+            copies = [send(which, dy, dx, {"dp": (plane + k) % 4}) for k in (2, 1, 3)]
+            spreads.append((dy, dx, copies))
+        else:
+            shared.append(send(which, dy, dx, sibling, whole=True))
+
+    pair_first = [k for k in FIRST_USED if k not in RING_FIRST]
+    ring_first = [k for k in FIRST_USED if k in RING_FIRST]
     kept = []
     for k in range(count):
         rows = shards[k].shape[0]
@@ -90,56 +111,60 @@
     for k in ring_first:
         to_pair[k] = send(k, 0, 0, pair)
     for k in range(count):
-        shared.append(send(k, 0, 0, sibling))
+        share(k, 0, 0)
     pair_right, pair_left = {}, {}
     for k in pair_first:
         to_pair[k].wait_recv()
         pair_right[k] = send(k, 1, 0, right)
         pair_left[k] = send(k, 1, 0, left)
-        shared.append(send(k, 1, 0, sibling))
+        share(k, 1, 0)
     far, ring_pair = {}, {}
     for k in ring_first + pair_first:
         to_right[k].wait_recv()
         far[k, 0] = send(k, 0, 3, right, 0)
         if k in ring_first:
             ring_pair[k, 3] = send(k, 0, 3, pair)
-        shared.append(send(k, 0, 3, sibling))
+        share(k, 0, 3)
         to_left[k].wait_recv()
         far[k, 1] = send(k, 0, 1, left, 1)
         if k in ring_first:
             ring_pair[k, 1] = send(k, 0, 1, pair)
-        shared.append(send(k, 0, 1, sibling))
+        share(k, 0, 1)
     for k in ring_first:
         to_pair[k].wait_recv()
-        shared.append(send(k, 1, 0, sibling))
+        share(k, 1, 0)
     for k in ring_first:
         far[k, 0].wait_recv()
         far[k, 1].wait_recv()
         ring_pair[k, 2] = send(k, 0, 2, pair)
-        shared.append(send(k, 0, 2, sibling))
+        share(k, 0, 2)
     far_pair = {}
     for k in pair_first:
         pair_right[k].wait_recv()
         far_pair[k, 0] = send(k, 1, 3, right, 0)
-        shared.append(send(k, 1, 3, sibling))
+        share(k, 1, 3)
         pair_left[k].wait_recv()
         far_pair[k, 1] = send(k, 1, 1, left, 1)
-        shared.append(send(k, 1, 1, sibling))
+        share(k, 1, 1)
     for k in pair_first:
         far[k, 0].wait_recv()
         far[k, 1].wait_recv()
-        shared.append(send(k, 0, 2, sibling))
+        share(k, 0, 2)
     for k in ring_first:
         for dx in (3, 1):
             ring_pair[k, dx].wait_recv()
-            shared.append(send(k, 1, dx, sibling))
+            share(k, 1, dx)
     for k in pair_first:
         far_pair[k, 0].wait_recv()
         far_pair[k, 1].wait_recv()
-        shared.append(send(k, 1, 2, sibling))
+        share(k, 1, 2)
     for k in ring_first:
         ring_pair[k, 2].wait_recv()
-        shared.append(send(k, 1, 2, sibling))
+        share(k, 1, 2)
+    for dy, dx, copies in spreads:
+        for copy in copies:
+            copy.wait_recv()
+        shared.append(send(SPREAD, dy, dx, sibling, whole=True))
     for copy in shared:
         copy.wait_recv()
     for copy in began:
@@ -150,7 +175,7 @@
 
 def gather_all(arrays):
     count = len(arrays)
-    copies = sum(16 if k in RING_FIRST else 17 for k in range(count))
+    copies = sum(16 if k in RING_FIRST else 17 for k in range(count)) + 21
     return pl.pallas_call(
         functools.partial(gather_kernel, count),
         out_shape=[jax.ShapeDtypeStruct((16 * a.shape[0], a.shape[1]), a.dtype) for a in arrays],
@@ -441,7 +466,7 @@
     rows, cotangent, allowed, vec, bias_qkv, bias_up, hbm_qkv, hbm_out, hbm_up, hbm_down,
     section_out, section_grad, hidden_t, second_t, attended_t, normed_t, du, dbefore, db, dprojected, sums, sum_up,
     w_qkv, w_out, w_up, w_down, x, hat_one, scale_one, normed, qkv, probs, attended, middle, hat_two, scale_two,
-    second, slope, hidden, wide, dmiddle, dattended, ship_out, ship_grad, land_out, land_grad,
+    second, slope, hidden, wide, dmiddle, dattended, ship_out, ship_grad, land_out, land_grad, between,
     load_sem, send_sem, recv_sem,
 ):
     section = lax.axis_index("section")
@@ -454,15 +479,51 @@
     ]
     for load in loads:
         load.start()
+    shard = lax.axis_index("shard")
+    height = section * 2 + shard // 8
+
+    def beside(step):
+        there = (height + step) % 4
+        return {"section": there // 2, "shard": (there % 2) * 8 + shard % 8}
+
     barrier = pltpu.get_barrier_semaphore()
-    pl.semaphore_signal(barrier, inc=1, device_id={"section": 1 - section}, device_id_type=MESH)
-    pl.semaphore_wait(barrier, 1)
-
-    def hop(source, target, k):
-        return pltpu.make_async_remote_copy(
-            src_ref=source, dst_ref=target, send_sem=send_sem.at[k], recv_sem=recv_sem.at[k],
-            device_id={"section": 1 - section}, device_id_type=MESH,
-        )
+    for step in (1, 3):
+        pl.semaphore_signal(barrier, inc=1, device_id=beside(step), device_id_type=MESH)
+    pl.semaphore_wait(barrier, 2)
+
+    def hop(source, land, which):
+        begun = []
+
+        def send(start, target, part, far, way):
+            k = ((which * 2 + part) * 2 + far) * 2 + way
+            copy = pltpu.make_async_remote_copy(
+                src_ref=start, dst_ref=target, send_sem=send_sem.at[k], recv_sem=recv_sem.at[k],
+                device_id=beside((1, 3)[way]), device_id_type=MESH,
+            )
+            copy.start()
+            begun.append(copy)
+            return copy
+
+        def view(ref, part, way):
+            return ref.at[pl.ds(way * SLOT, SLOT), pl.ds(part * 512, 512)]
+
+        near, far = {}, {}
+
+        def begin(part):
+            for way in range(2):
+                near[part, way] = send(view(source, part, way), view(between.at[which], part, way), part, 0, way)
+
+        def end():
+            for part in range(2):
+                for way in range(2):
+                    near[part, way].wait_recv()
+                    far[part, way] = send(view(between.at[which], part, way), view(land, part, way), part, 1, way)
+            for copy in far.values():
+                copy.wait_recv()
+            for copy in begun:
+                copy.wait_send()
+
+        return begin, end
 
     def tiles(width, body, tile=512):
         @pl.loop(0, width // tile)
@@ -470,19 +531,21 @@
             body(pl.ds(pl.multiple_of(step * tile, 128), tile))
 
     ln1_gain, ln1_bias, _, _, b_out, ln2_gain, ln2_bias, b_down = (vec[k : k + 1, :] for k in range(8))
-    lane = lax.broadcasted_iota(jnp.int32, (SLOT, 128), 1)
-    low_half = lane < 64
-    halves = (low_half, jnp.logical_not(low_half))
+    low_half = lax.broadcasted_iota(jnp.int32, (SLOT, 128), 1) < 64
+
+    def stacked(values):
+        none = jnp.zeros_like(values)
+        return jnp.concatenate([jnp.where(low_half, values, none), jnp.where(low_half, none, values)], axis=0)
+
+    def unstacked(values):
+        return jnp.where(low_half, values[:SLOT], values[SLOT:])
 
     def standard(values):
         centered = values - jnp.mean(values, axis=-1, keepdims=True)
         scale = lax.rsqrt(jnp.mean(centered * centered, axis=-1, keepdims=True) + norm_eps)
         return centered * scale, scale
 
-    def only(which, values):
-        return jnp.where(halves[which], values, jnp.zeros_like(values))
-
-    def forward(result, before_use):
+    def forward(result, before_use, made=None):
         hat, scale = standard(x[...].astype(jnp.float32))
         hat_one[...] = hat
         scale_one[...] = scale
@@ -500,15 +563,13 @@
             for slot in range(2):
                 spot = pl.ds(slot * SLOT, SLOT)
                 query, key, value = (qkv[spot, cut] for cut in cuts)
-                mixed = []
-                for which in range(2):
-                    scores = dot_back(query, only(which, key)) * 0.125
-                    scores = jnp.where(allowed[slot] > 0, scores, masked_score)
-                    exponent = jnp.exp(scores - jnp.max(scores, axis=-1, keepdims=True))
-                    prob = exponent / jnp.sum(exponent, axis=-1, keepdims=True)
-                    probs[couple * 4 + slot * 2 + which] = prob
-                    mixed.append(dot(prob.astype(jnp.bfloat16), value))
-                attended[spot, cuts[0]] = jnp.where(low_half, *mixed).astype(jnp.bfloat16)
+                scores = dot_back(stacked(query * SCALE), key)
+                scores = jnp.where(allowed[slot] > 0, scores, masked_score)
+                exponent = jnp.exp(scores - jnp.max(scores, axis=-1, keepdims=True))
+                prob = exponent / jnp.sum(exponent, axis=-1, keepdims=True)
+                probs[couple * 2 + slot] = prob
+                mixed = dot(prob.astype(jnp.bfloat16), value)
+                attended[spot, cuts[0]] = unstacked(mixed).astype(jnp.bfloat16)
 
         before_use(1)
 
@@ -537,7 +598,12 @@
         def shrink(cut):
             result[:, cut] = (middle[:, cut] + dot(hidden[...], w_down[:, cut]) + vec[7:8, cut]).astype(jnp.bfloat16)
 
-        tiles(1024, shrink)
+        if made is None:
+            tiles(1024, shrink)
+        else:
+            for part in range(2):
+                shrink(pl.ds(part * 512, 512))
+                made(part)
 
     def norm_back(hat, scale, grad, gain):
         inner = grad * gain
@@ -583,17 +649,14 @@
                 spot = pl.ds(slot * SLOT, SLOT)
                 query, key, value = (qkv[spot, cut] for cut in cuts)
                 grad = dattended[spot, cuts[0]]
-                parts = ([], [], [])
-                for which in range(2):
-                    prob = probs[couple * 4 + slot * 2 + which]
-                    dprob = dot_back(only(which, grad), value)
-                    delta = jnp.sum(prob * dprob, axis=-1, keepdims=True)
-                    dscore = (prob * (dprob - delta)).astype(jnp.bfloat16)
-                    parts[0].append(dot(dscore, key) * 0.125)
-                    parts[1].append(dot_rows(dscore, query) * 0.125)
-                    parts[2].append(dot_rows(prob.astype(jnp.bfloat16), grad))
-                for cut, part in zip(cuts, parts):
-                    dprojected[spot, cut] = jnp.where(low_half, *part).astype(jnp.bfloat16)
+                grads = stacked(grad)
+                prob = probs[couple * 2 + slot]
+                dprob = dot_back(grads, value)
+                delta = jnp.sum(prob * dprob, axis=-1, keepdims=True)
+                dscore = (prob * (dprob - delta)).astype(jnp.bfloat16)
+                dprojected[spot, cuts[0]] = (unstacked(dot(dscore, key)) * 0.125).astype(jnp.bfloat16)
+                dprojected[spot, cuts[1]] = dot_rows(dscore, stacked(query * SCALE)).astype(jnp.bfloat16)
+                dprojected[spot, cuts[2]] = dot_rows(prob.astype(jnp.bfloat16), grads).astype(jnp.bfloat16)
 
         def normed_back(cut):
             wide[:, cut] = dot_back(dprojected[...], w_qkv[cut, :])
@@ -609,16 +672,16 @@
             sums[4:5, :] = total(db[...])
 
     x[...] = rows[...]
-    forward(ship_out, lambda k: loads[k].wait())
-    there = hop(ship_out, land_out, 0)
-    there.start()
-    there.wait()
+    begin, end = hop(ship_out, land_out, 0)
+    forward(ship_out, lambda k: loads[k].wait(), begin)
+    end()
     x[...] = jnp.where(first, rows[...], land_out[...])
     forward(section_out, lambda k: None)
     du[...] = cotangent[...]
     backward(ship_grad, False)
-    back = hop(ship_grad, land_grad, 1)
-    back.start()
+    begin, end = hop(ship_grad, land_grad, 1)
+    begin(0)
+    begin(1)
 
     def flip(source, target):
         def body(cut):
@@ -628,7 +691,7 @@
 
     for source, target in ((hidden, hidden_t), (second, second_t), (attended, attended_t), (normed, normed_t)):
         flip(source, target)
-    back.wait()
+    end()
     du[...] = jnp.where(first, land_grad[...], cotangent[...])
     backward(section_grad, True)
 
@@ -643,10 +706,10 @@
     ]
     scratch = [(m.shape, low) for m in mats] + [
         ((tall, width), low), ((tall, width), full), ((tall, 1), full), ((tall, width), low),
-        ((tall, 3 * width), low), ((2 * HEADS, SLOT, SLOT), full), ((tall, width), low), ((tall, width), full),
+        ((tall, 3 * width), low), ((HEADS, 2 * SLOT, SLOT), full), ((tall, width), low), ((tall, width), full),
         ((tall, width), full), ((tall, 1), full), ((tall, width), low), ((tall, wide), full), ((tall, wide), low),
         ((tall, width), full), ((tall, width), full), ((tall, width), low),
-    ] + [((tall, width), low)] * 4
+    ] + [((tall, width), low)] * 4 + [((2, tall, width), low)]
     in_vmem, anywhere = pl.BlockSpec(memory_space=pltpu.VMEM), pl.BlockSpec(memory_space=pl.ANY)
     return pl.pallas_call(
         relay_kernel,
@@ -654,7 +717,7 @@
         in_specs=[in_vmem] * 6 + [anywhere] * 4,
         out_specs=[in_vmem] * len(outs),
         scratch_shapes=[pltpu.VMEM(*s) for s in scratch]
-        + [pltpu.SemaphoreType.DMA((n,)) for n in (4, 2, 2)],
+        + [pltpu.SemaphoreType.DMA((n,)) for n in (4, 16, 16)],
         compiler_params=pltpu.CompilerParams(
             collective_id=2, has_side_effects=True, vmem_limit_bytes=62 * 1024 * 1024
         ),
@@ -665,7 +728,7 @@
     by_slot = segment.reshape(-1, SLOT)
     positions = jnp.arange(SLOT)
     allowed = (by_slot[:, :, None] == by_slot[:, None, :]) & (positions[None, :] <= positions[:, None])
-    return allowed.astype(jnp.float32)
+    return jnp.concatenate([allowed, allowed], axis=1).astype(jnp.float32)
 
 
 def on_device(

time: 360 us -> 332 us (0.922)
  Pallas kernels: 338 us -> 310 us
    pallas_call x1, Pallas kernels: 116 us -> 98.1 us  [relay(): pl.pallas_call(relay_kernel, out_shape=[jax.ShapeDtypeStruct(*o) for o in...]
    pallas_call x1, Pallas kernels: 91 us -> 81.5 us  [gather_all(): pl.pallas_call(functools.partial(gather_kernel, count), out_shape=[jax.Sh...]
where the time goes in v4:
time: 332 us; the launch traced here: 330 us
  Pallas kernels  310 us (93%)
  local copies, waits for them, and re-layouts  16.1 us (5%)
  other arithmetic  3.7 us (1%)
    pallas_call x1, Pallas kernels, reduce_all(): pl.pallas_call(functools.partial(reduce_kernel, plans), out_shape=[jax.Sh...  130 us
    pallas_call x1, Pallas kernels, relay(): pl.pallas_call(relay_kernel, out_shape=[jax.ShapeDtypeStruct(*o) for o in...  98.1 us
    pallas_call x1, Pallas kernels, gather_all(): pl.pallas_call(functools.partial(gather_kernel, count), out_shape=[jax.Sh...  81.5 us
    unnamed x24, local copies, waits for them, and re-layouts  6.95 us

profile of v4, /device:TPU:0, one launch (start us, length us, event | category | flops | bytes accessed | tf_op | source)
XLA Modules:
  0.0 330.5 jit_solution(11941814527681148806)
XLA Ops:
  0.6 0.0 copy-start.7
  0.7 0.0 copy-start
  0.7 0.0 copy-start.6
  0.7 0.9 concatenate.13
  1.6 0.6 broadcast_in_dim.39.refs_4_
  2.2 81.5 %shard_map.271 = (bf16[1024,3072]{1,0:T(8,128)(2,1)}, bf16[1024,1024]{1,0:T(8,128)(2,1)}, bf16[1024,4096]{1,0:T(8,128)(2,1)}, bf16[4096,1024]{1,0:T(8,128)(2,1)}, bf16[256,768]{1,0:T(8,128)(2,1)}) custom-call(bf16[64,3072]{1,0:T(8,128)(2,1)} %bitcast.37, bf16[64,1024]{1,0:T(8,128)(2,1)} %bitcast.42, bf16[64,4096]{1,0:T(8,128)(2,1)} %bitcast.33, ...), custom_call_target="tpu_custom_call" | custom-call | tf_op jit(solution)/shard_map/pallas_call | solution.py:179
  83.8 1.0 slice.64
  84.7 0.1 reshape.75
  84.9 0.1 slice.51
  84.9 0.1 slice.53
  85.0 0.6 pad_maximum_fusion.1.bias_qkv
  85.6 0.7 reshape.76.vec
  86.3 0.6 copy.35
  87.0 0.0 copy-done.7
  87.0 0.0 copy-done
  87.0 0.8 broadcast_multiply_fusion.cotangent
  87.8 0.0 copy-done.6
  87.8 0.1 eq.15
  87.9 0.1 compare_and_fusion
  88.0 0.7 add_convert_fusion.allowed
  88.7 98.1 %shard_map.272 = (bf16[192,1024]{1,0:T(8,128)(2,1)}, bf16[192,1024]{1,0:T(8,128)(2,1)}, bf16[4096,192]{1,0:T(8,128)(2,1)}, bf16[1024,192]{1,0:T(8,128)(2,1)}, bf...) custom-call(bf16[192,1024]{1,0:T(8,128)(2,1)} %bitcast.29, ...), custom_call_target="tpu_custom_call" | custom-call | tf_op jit(solution)/shard_map/pallas_call | solution.py:714
  186.9 0.8 reshape.78
  187.7 0.1 reshape.79
  187.8 0.5 broadcast.13
  188.3 1.4 reduce.4
  189.8 0.8 pad_bitcast_fusion.refs_4_
  190.6 0.6 broadcast_in_dim.44.refs_9_
  191.2 0.0 copy-start.4
  191.2 0.0 copy-start.3
  191.2 130.3 %shard_map.273 = (f32[256,1024]{1,0:T(8,128)}, f32[64,4096]{1,0:T(8,128)}, f32[64,1024]{1,0:T(8,128)}, f32[64,3072]{1,0:T(8,128)}, f32[8,1024]{1,0:T(8,128)}) custom-call(bf16[4096,192]{1,0:T(8,128)(2,1)} %get-tuple-element.44.refs_0_, bf16[1024,192]{1,0:T(8,128)(2,1)} %get-tuple-element.45.refs_1_, bf16[1024,192]{1,0:T(8,128)(2,1)} %get-tuple-element.46.refs_2_, ...), custom_call_target="tpu_custom_call" | custom-call | tf_op jit(solution)/shard_map/pallas_call | solution.py:452
  321.5 0.0 copy-start.5
  321.5 0.0 copy-start.2
  321.5 1.4 fusion.2
  322.9 1.3 slice.62
  324.2 0.0 copy-done.4
  324.2 0.7 copy.47
  324.9 0.0 copy-done.3
  324.9 0.7 copy.48
  325.7 0.0 copy-start.1
  325.7 2.2 copy.49
  327.8 0.0 copy-done.5
  327.9 0.7 copy.50
  328.6 0.0 copy-done.2
  328.6 1.0 copy.51
  329.5 0.0 copy-done.1
  329.5 1.0 copy.52
  (14 shorter events, 0.2 us)
Async XLA Ops:
  0.6 86.3 %copy-start.7 = (s32[192]{0:T(256)S(1)}, s32[192]{0:T(256)}, u32[]{:S(2)}) copy-start(s32[192]{0:T(256)} %param.18) | copy-start | bytes 2308
  0.7 86.3 %copy-start = (bf16[1,192,1024]{2,1,0:T(8,128)(2,1)S(1)}, bf16[1,192,1024]{2,1,0:T(8,128)(2,1)}, u32[]{:S(2)}) copy-start(bf16[1,192,1024]{2,1,0:T(8,128)(2,1)} %param.16) | copy-start | bytes 1179652
  0.7 87.2 %copy-start.6 = (s32[192]{0:T(256)S(1)}, s32[192]{0:T(256)}, u32[]{:S(2)}) copy-start(s32[192]{0:T(256)} %param.17) | copy-start | bytes 2308
  191.2 133.0 %copy-start.4 = (bf16[192,1024]{1,0:T(8,128)(2,1)S(1)}, bf16[192,1024]{1,0:T(8,128)(2,1)}, u32[]{:S(2)}) copy-start(bf16[192,1024]{1,0:T(8,128)(2,1)} %get-tuple-element.42) | copy-start | bytes 1179652
  191.2 133.7 %copy-start.3 = (bf16[192,1024]{1,0:T(8,128)(2,1)S(1)}, bf16[192,1024]{1,0:T(8,128)(2,1)}, u32[]{:S(2)}) copy-start(bf16[192,1024]{1,0:T(8,128)(2,1)} %get-tuple-element.43) | copy-start | bytes 1179652
  321.5 6.3 %copy-start.5 = (f32[64,1024]{1,0:T(8,128)S(1)}, f32[64,1024]{1,0:T(8,128)}, u32[]{:S(2)}) copy-start(f32[64,1024]{1,0:T(8,128)} %get-tuple-element.56) | copy-start | bytes 786436
  321.5 7.0 %copy-start.2 = (f32[64,4096]{1,0:T(8,128)S(1)}, f32[64,4096]{1,0:T(8,128)}, u32[]{:S(2)}) copy-start(f32[64,4096]{1,0:T(8,128)} %get-tuple-element.57) | copy-start | bytes 3145732
  325.7 3.8 %copy-start.1 = (f32[256,1024]{1,0:T(8,128)S(1)}, f32[256,1024]{1,0:T(8,128)}, u32[]{:S(2)}) copy-start(f32[256,1024]{1,0:T(8,128)} %get-tuple-element.58) | copy-start | bytes 3145732

commit v5 on v4

--- a/solution.py
+++ b/solution.py
@@ -191,7 +191,7 @@
 
 
 def reduce_kernel(plans, *refs):
-    count = len(plans)
+    count, given = len(plans), len({p.source for p in plans})
     refs = list(refs)
 
     def take(number):
@@ -199,8 +199,9 @@
         del refs[:number]
         return taken
 
-    lefts, rights = take(count), take(count)
-    outs = take(count)
+    lefts, rights = take(given), take(given)
+    outs = take(given)
+    lefts, rights = ([group[p.source] for p in plans] for group in (lefts, rights))
     sums, from_sibling, to_sibling = take(count), take(count), take(count)
     half_left, half_right, full_left, full_right, from_pair = (take(count) for _ in range(5))
     quarters, merged, spread = take(count), take(count), take(count)
@@ -237,7 +238,7 @@
         return copy
 
     def tiles(width, body, tile=512):
-        tile = min(tile, width)
+        tile = min(tile, width) if width % tile == 0 or width < tile else 256
 
         @pl.loop(0, width // tile)
         def _(step):
@@ -270,7 +271,7 @@
             both = jnp.concatenate([lefts[k][own, :], lefts[k][others, :]], axis=0)
 
             def body(cut):
-                block = dot(both, rights[k][:, cut])
+                block = dot(both, rights[k][:, pl.ds(pl.multiple_of(plans[k].start + cut.start, 128), cut.size)])
                 sums[k][spot, :, cut] = block[:rows].astype(sums[k].dtype)
                 to_sibling[k][slot, :, cut] = block[rows:].astype(sums[k].dtype)
 
@@ -357,65 +358,99 @@
         for hop in (1, 2, 3):
             returned[k, hop].wait_recv()
 
+        result = outs[plans[k].source].at[:, pl.ds(plans[k].start, width[k])]
+
         def body(cut):
-            outs[k][:, cut] = spread[k][:, cut].astype(jnp.float32)
+            result[:, cut] = spread[k][:, cut].astype(jnp.float32)
 
         tiles(width[k], body)
 
-    down, up, out, joint, vectors = range(5)
-    for k, dy, dx in (
-        (up, 1, 2), (up, 0, 2), (down, 1, 2), (joint, 1, 2), (joint, 0, 2), (down, 1, 1), (down, 1, 3),
-        (down, 1, 0), (vectors, 1, 2), (vectors, 0, 2),
-    ):
-        produce(k, dy, dx)
-    for dy in (1, 0):
-        produce(up, dy, 1)
-        produce(up, dy, 3)
-        forward(up, dy)
-    for dx in (2, 1, 3, 0):
-        produce(out, 1, dx)
-    for dy in (1, 0):
-        produce(joint, dy, 1)
-        produce(joint, dy, 3)
-        forward(joint, dy)
-    produce(down, 0, 2)
-    meet(down, 2)
-    send_halves(down, 0)
-    for dy in (1, 0):
-        produce(vectors, dy, 1)
-        produce(vectors, dy, 3)
-        forward(vectors, dy)
-    produce(out, 0, 2)
-    meet(out, 2)
-    send_halves(out, 0)
-    produce(up, 1, 0)
-    ring_end(up, 1)
-    paired[up, 0] = send(sums[up].at[4], from_pair[up].at[0], {"shard": pair})
-    for k in (down, out):
+    def start_ring(k):
+        produce(k, 1, 2)
+        produce(k, 0, 2)
+
+    def turn_ring(k):
+        for dy in (1, 0):
+            produce(k, dy, 1)
+            produce(k, dy, 3)
+            forward(k, dy)
+
+    def to_pair(k):
+        if plans[k].ring_first:
+            produce(k, 1, 0)
+            ring_end(k, 1)
+            paired[k, 0] = send(sums[k].at[4], from_pair[k].at[0], {"shard": pair})
+        else:
+            for dx in (2, 1, 3, 0):
+                produce(k, 1, dx)
+
+    def late_start(k):
+        produce(k, 0, 2)
+        meet(k, 2)
+        send_halves(k, 0)
+
+    def late_turn(k):
         produce(k, 0, 1)
         produce(k, 0, 3)
         meet(k, 1)
         meet(k, 3)
         forward(k, 0)
-    for k in (joint, vectors):
-        produce(k, 1, 0)
-        ring_end(k, 1)
-        paired[k, 0] = send(sums[k].at[4], from_pair[k].at[0], {"shard": pair})
-    for k in (up, joint, vectors):
+
+    def conclude(k):
         produce(k, 0, 0)
-        ring_end(k, 0)
-        paired[k, 0].wait_recv()
-        add(sums[k].at[0], from_pair[k].at[0])
+        if plans[k].ring_first:
+            ring_end(k, 0)
+            paired[k, 0].wait_recv()
+            add(sums[k].at[0], from_pair[k].at[0])
+        else:
+            meet(k, 0)
+            ring_end(k, 0)
         scatter_planes(k)
-    return_planes(up)
-    for k in (down, out):
-        produce(k, 0, 0)
-        meet(k, 0)
-        ring_end(k, 0)
-        scatter_planes(k)
-    for k in (joint, vectors, down, out):
-        return_planes(k)
-    for k in (up, joint, vectors, down, out):
+
+    down_a, down_b, up_a, up_b, out, joint_a, joint_b, vectors = range(8)
+    start_ring(up_a)
+    produce(down_a, 1, 2)
+    start_ring(up_b)
+    for dx in (1, 3, 0):
+        produce(down_a, 1, dx)
+    turn_ring(up_a)
+    start_ring(joint_a)
+    to_pair(down_b)
+    turn_ring(up_b)
+    start_ring(vectors)
+    late_start(down_a)
+    to_pair(up_a)
+    start_ring(joint_b)
+    turn_ring(joint_a)
+    to_pair(out)
+    late_turn(down_a)
+    to_pair(up_b)
+    conclude(up_a)
+    late_start(down_b)
+    turn_ring(joint_b)
+    turn_ring(vectors)
+    to_pair(joint_a)
+    conclude(down_a)
+    conclude(up_b)
+    return_planes(up_a)
+    late_start(out)
+    late_turn(down_b)
+    to_pair(joint_b)
+    to_pair(vectors)
+    conclude(joint_a)
+    return_planes(down_a)
+    return_planes(up_b)
+    late_turn(out)
+    conclude(joint_b)
+    conclude(vectors)
+    return_planes(joint_a)
+    conclude(down_b)
+    return_planes(joint_b)
+    return_planes(vectors)
+    conclude(out)
+    return_planes(down_b)
+    return_planes(out)
+    for k in (up_a, down_a, up_b, joint_a, joint_b, vectors, down_b, out):
         finish(k)
     kept_back = {id(c) for per in slots for c in per[:-SLOTS]}
     for copy in began:
@@ -423,16 +458,18 @@
             copy.wait_send()
 
 
-Plan = collections.namedtuple("Plan", ("rows", "width", "product", "ring_first", "dtype"))
+Plan = collections.namedtuple("Plan", ("source", "start", "rows", "width", "product", "ring_first", "dtype"))
 SLOTS = 3
 
 
 def reduce_all(pairs, vectors):
-    plans = [
-        Plan(left.shape[0] // 16, right.shape[1], True, k in (1, 3), jnp.bfloat16)
-        for k, (left, right) in enumerate(pairs)
-    ]
-    plans.append(Plan(vectors.shape[0] // 16, vectors.shape[1], False, True, jnp.float32))
+    plans = []
+    for k, (left, right) in enumerate(pairs):
+        parts = 1 if right.shape[1] == left.shape[0] else 2
+        width = right.shape[1] // parts
+        for part in range(parts):
+            plans.append(Plan(k, part * width, left.shape[0] // 16, width, True, k in (1, 3), jnp.bfloat16))
+    plans.append(Plan(len(pairs), 0, vectors.shape[0] // 16, vectors.shape[1], False, True, jnp.float32))
     lefts = [left for left, _ in pairs] + [vectors]
     rights = [right for _, right in pairs] + [jnp.zeros((8, 128), jnp.float32)]
 
@@ -451,9 +488,12 @@
     copies = sum(8 + (9 if p.ring_first else 8) + 6 for p in plans)
     return pl.pallas_call(
         functools.partial(reduce_kernel, plans),
-        out_shape=[jax.ShapeDtypeStruct((p.rows, p.width), jnp.float32) for p in plans],
-        in_specs=[pl.BlockSpec(memory_space=pltpu.VMEM)] * (2 * len(plans)),
-        out_specs=[pl.BlockSpec(memory_space=pltpu.VMEM)] * len(plans),
+        out_shape=[
+            jax.ShapeDtypeStruct((left.shape[0] // 16, right.shape[1]), jnp.float32) for left, right in pairs
+        ]
+        + [jax.ShapeDtypeStruct((vectors.shape[0] // 16, vectors.shape[1]), jnp.float32)],
+        in_specs=[pl.BlockSpec(memory_space=pltpu.VMEM)] * (2 * len(lefts)),
+        out_specs=[pl.BlockSpec(memory_space=pltpu.VMEM)] * len(lefts),
         scratch_shapes=scratch
         + [pltpu.SemaphoreType.DMA((copies,)), pltpu.SemaphoreType.DMA((copies,))],
         compiler_params=pltpu.CompilerParams(

time: 332 us -> 321 us (0.967)
  Pallas kernels: 310 us -> 299 us
    pallas_call x1, Pallas kernels: 130 us -> 120 us  [reduce_all(): pl.pallas_call(functools.partial(reduce_kernel, plans), out_shape=[jax.Sh...]
where the time goes in v5:
time: 321 us; the launch traced here: 320 us
  Pallas kernels  299 us (93%)
  local copies, waits for them, and re-layouts  16.1 us (5%)
  other arithmetic  3.7 us (1%)
    pallas_call x1, Pallas kernels, reduce_all(): pl.pallas_call(functools.partial(reduce_kernel, plans), out_shape=[jax.Sh...  120 us
    pallas_call x1, Pallas kernels, relay(): pl.pallas_call(relay_kernel, out_shape=[jax.ShapeDtypeStruct(*o) for o in...  98.1 us
    pallas_call x1, Pallas kernels, gather_all(): pl.pallas_call(functools.partial(gather_kernel, count), out_shape=[jax.Sh...  81.5 us
    unnamed x24, local copies, waits for them, and re-layouts  6.95 us

profile of v5, /device:TPU:0, one launch (start us, length us, event | category | flops | bytes accessed | tf_op | source)
XLA Modules:
  0.0 319.8 jit_solution(12811175552111843576)
XLA Ops:
  0.6 0.0 copy-start.7
  0.7 0.0 copy-start
  0.7 0.0 copy-start.6
  0.7 0.9 concatenate.13
  1.6 0.6 broadcast_in_dim.39.refs_4_
  2.2 81.5 %shard_map.271 = (bf16[1024,3072]{1,0:T(8,128)(2,1)}, bf16[1024,1024]{1,0:T(8,128)(2,1)}, bf16[1024,4096]{1,0:T(8,128)(2,1)}, bf16[4096,1024]{1,0:T(8,128)(2,1)}, bf16[256,768]{1,0:T(8,128)(2,1)}) custom-call(bf16[64,3072]{1,0:T(8,128)(2,1)} %bitcast.37, bf16[64,1024]{1,0:T(8,128)(2,1)} %bitcast.42, bf16[64,4096]{1,0:T(8,128)(2,1)} %bitcast.33, ...), custom_call_target="tpu_custom_call" | custom-call | tf_op jit(solution)/shard_map/pallas_call | solution.py:179
  83.8 1.0 slice.64
  84.7 0.1 reshape.75
  84.9 0.1 slice.51
  84.9 0.1 slice.53
  85.0 0.6 pad_maximum_fusion.1.bias_qkv
  85.6 0.7 reshape.76.vec
  86.3 0.6 copy.35
  87.0 0.0 copy-done.7
  87.0 0.0 copy-done
  87.0 0.8 broadcast_multiply_fusion.cotangent
  87.8 0.0 copy-done.6
  87.8 0.1 eq.15
  87.9 0.1 compare_and_fusion
  88.0 0.7 add_convert_fusion.allowed
  88.7 98.1 %shard_map.272 = (bf16[192,1024]{1,0:T(8,128)(2,1)}, bf16[192,1024]{1,0:T(8,128)(2,1)}, bf16[4096,192]{1,0:T(8,128)(2,1)}, bf16[1024,192]{1,0:T(8,128)(2,1)}, bf...) custom-call(bf16[192,1024]{1,0:T(8,128)(2,1)} %bitcast.29, ...), custom_call_target="tpu_custom_call" | custom-call | tf_op jit(solution)/shard_map/pallas_call | solution.py:754
  186.9 0.8 reshape.78
  187.7 0.1 reshape.79
  187.8 0.5 broadcast.13
  188.3 1.4 reduce.4
  189.8 0.8 pad_bitcast_fusion.refs_4_
  190.6 0.6 broadcast_in_dim.44.refs_9_
  191.2 0.0 copy-start.4
  191.2 0.0 copy-start.3
  191.2 119.6 %shard_map.273 = (f32[256,1024]{1,0:T(8,128)}, f32[64,4096]{1,0:T(8,128)}, f32[64,1024]{1,0:T(8,128)}, f32[64,3072]{1,0:T(8,128)}, f32[8,1024]{1,0:T(8,128)}) custom-call(bf16[4096,192]{1,0:T(8,128)(2,1)} %get-tuple-element.44.refs_0_, bf16[1024,192]{1,0:T(8,128)(2,1)} %get-tuple-element.45.refs_1_, bf16[1024,192]{1,0:T(8,128)(2,1)} %get-tuple-element.46.refs_2_, ...), custom_call_target="tpu_custom_call" | custom-call | tf_op jit(solution)/shard_map/pallas_call | solution.py:489
  310.8 0.0 copy-start.5
  310.8 0.0 copy-start.2
  310.8 1.4 fusion.2
  312.2 1.3 slice.62
  313.5 0.0 copy-done.4
  313.5 0.7 copy.47
  314.2 0.0 copy-done.3
  314.2 0.7 copy.48
  315.0 0.0 copy-start.1
  315.0 2.2 copy.49
  317.1 0.0 copy-done.5
  317.1 0.7 copy.50
  317.8 0.0 copy-done.2
  317.9 1.0 copy.51
  318.8 0.0 copy-done.1
  318.8 1.0 copy.52
  (14 shorter events, 0.2 us)
Async XLA Ops:
  0.6 86.3 %copy-start.7 = (s32[192]{0:T(256)S(1)}, s32[192]{0:T(256)}, u32[]{:S(2)}) copy-start(s32[192]{0:T(256)} %param.18) | copy-start | bytes 2308
  0.7 86.3 %copy-start = (bf16[1,192,1024]{2,1,0:T(8,128)(2,1)S(1)}, bf16[1,192,1024]{2,1,0:T(8,128)(2,1)}, u32[]{:S(2)}) copy-start(bf16[1,192,1024]{2,1,0:T(8,128)(2,1)} %param.16) | copy-start | bytes 1179652
  0.7 87.2 %copy-start.6 = (s32[192]{0:T(256)S(1)}, s32[192]{0:T(256)}, u32[]{:S(2)}) copy-start(s32[192]{0:T(256)} %param.17) | copy-start | bytes 2308
  191.2 122.3 %copy-start.4 = (bf16[192,1024]{1,0:T(8,128)(2,1)S(1)}, bf16[192,1024]{1,0:T(8,128)(2,1)}, u32[]{:S(2)}) copy-start(bf16[192,1024]{1,0:T(8,128)(2,1)} %get-tuple-element.42) | copy-start | bytes 1179652
  191.2 123.0 %copy-start.3 = (bf16[192,1024]{1,0:T(8,128)(2,1)S(1)}, bf16[192,1024]{1,0:T(8,128)(2,1)}, u32[]{:S(2)}) copy-start(bf16[192,1024]{1,0:T(8,128)(2,1)} %get-tuple-element.43) | copy-start | bytes 1179652
  310.8 6.3 %copy-start.5 = (f32[64,1024]{1,0:T(8,128)S(1)}, f32[64,1024]{1,0:T(8,128)}, u32[]{:S(2)}) copy-start(f32[64,1024]{1,0:T(8,128)} %get-tuple-element.56) | copy-start | bytes 786436
  310.8 7.0 %copy-start.2 = (f32[64,4096]{1,0:T(8,128)S(1)}, f32[64,4096]{1,0:T(8,128)}, u32[]{:S(2)}) copy-start(f32[64,4096]{1,0:T(8,128)} %get-tuple-element.57) | copy-start | bytes 3145732
  315.0 3.8 %copy-start.1 = (f32[256,1024]{1,0:T(8,128)S(1)}, f32[256,1024]{1,0:T(8,128)}, u32[]{:S(2)}) copy-start(f32[256,1024]{1,0:T(8,128)} %get-tuple-element.58) | copy-start | bytes 3145732

commit v6 on v5

--- a/solution.py
+++ b/solution.py
@@ -597,7 +597,7 @@
 
         tiles(3072, project)
 
-        @pl.loop(0, HEADS // 2)
+        @pl.loop(0, HEADS // 2, unroll=4)
         def _(couple):
             cuts = [pl.ds(pl.multiple_of(couple * 128 + 1024 * k, 128), 128) for k in range(3)]
             for slot in range(2):
@@ -632,7 +632,7 @@
             hidden[:, cut] = (before * half).astype(jnp.bfloat16)
             slope[:, cut] = half + (0.5 * GELU_A) * before * (1.0 - bend * bend) * (1.0 + (3.0 * GELU_B) * square)
 
-        tiles(4096, grow, 256)
+        tiles(4096, grow, 512)
         before_use(3)
 
         def shrink(cut):
@@ -682,7 +682,7 @@
 
         tiles(1024, mix_back)
 
-        @pl.loop(0, HEADS // 2)
+        @pl.loop(0, HEADS // 2, unroll=4)
         def _(couple):
             cuts = [pl.ds(pl.multiple_of(couple * 128 + 1024 * k, 128), 128) for k in range(3)]
             for slot in range(2):

time: 321 us -> 309 us (0.963)
  Pallas kernels: 299 us -> 287 us
    pallas_call x1, Pallas kernels: 98.1 us -> 85.9 us  [relay(): pl.pallas_call(relay_kernel, out_shape=[jax.ShapeDtypeStruct(*o) for o in...]
where the time goes in v6:
time: 309 us; the launch traced here: 308 us
  Pallas kernels  287 us (93%)
  local copies, waits for them, and re-layouts  16.1 us (5%)
  other arithmetic  3.7 us (1%)
    pallas_call x1, Pallas kernels, reduce_all(): pl.pallas_call(functools.partial(reduce_kernel, plans), out_shape=[jax.Sh...  120 us
    pallas_call x1, Pallas kernels, relay(): pl.pallas_call(relay_kernel, out_shape=[jax.ShapeDtypeStruct(*o) for o in...  85.9 us
    pallas_call x1, Pallas kernels, gather_all(): pl.pallas_call(functools.partial(gather_kernel, count), out_shape=[jax.Sh...  81.5 us
    unnamed x24, local copies, waits for them, and re-layouts  6.95 us

profile of v6, /device:TPU:0, one launch (start us, length us, event | category | flops | bytes accessed | tf_op | source)
XLA Modules:
  0.0 307.8 jit_solution(13632550163921748153)
XLA Ops:
  0.6 0.0 copy-start.7
  0.7 0.0 copy-start
  0.7 0.0 copy-start.6
  0.7 0.9 concatenate.13
  1.6 0.6 broadcast_in_dim.39.refs_4_
  2.2 81.5 %shard_map.271 = (bf16[1024,3072]{1,0:T(8,128)(2,1)}, bf16[1024,1024]{1,0:T(8,128)(2,1)}, bf16[1024,4096]{1,0:T(8,128)(2,1)}, bf16[4096,1024]{1,0:T(8,128)(2,1)}, bf16[256,768]{1,0:T(8,128)(2,1)}) custom-call(bf16[64,3072]{1,0:T(8,128)(2,1)} %bitcast.37, bf16[64,1024]{1,0:T(8,128)(2,1)} %bitcast.42, bf16[64,4096]{1,0:T(8,128)(2,1)} %bitcast.33, ...), custom_call_target="tpu_custom_call" | custom-call | tf_op jit(solution)/shard_map/pallas_call | solution.py:179
  83.8 1.0 slice.64
  84.7 0.1 reshape.75
  84.9 0.1 slice.51
  84.9 0.1 slice.53
  85.0 0.6 pad_maximum_fusion.1.bias_qkv
  85.6 0.7 reshape.76.vec
  86.3 0.6 copy.35
  87.0 0.0 copy-done.7
  87.0 0.0 copy-done
  87.0 0.8 broadcast_multiply_fusion.cotangent
  87.8 0.0 copy-done.6
  87.8 0.1 eq.15
  87.9 0.1 compare_and_fusion
  88.0 0.7 add_convert_fusion.allowed
  88.7 85.9 %shard_map.272 = (bf16[192,1024]{1,0:T(8,128)(2,1)}, bf16[192,1024]{1,0:T(8,128)(2,1)}, bf16[4096,192]{1,0:T(8,128)(2,1)}, bf16[1024,192]{1,0:T(8,128)(2,1)}, bf...) custom-call(bf16[192,1024]{1,0:T(8,128)(2,1)} %bitcast.29, ...), custom_call_target="tpu_custom_call" | custom-call | tf_op jit(solution)/shard_map/pallas_call | solution.py:754
  174.6 0.8 reshape.78
  175.4 0.1 reshape.79
  175.5 0.5 broadcast.13
  176.0 1.4 reduce.4
  177.5 0.8 pad_bitcast_fusion.refs_4_
  178.4 0.6 broadcast_in_dim.44.refs_9_
  178.9 0.0 copy-start.4
  178.9 0.0 copy-start.3
  178.9 119.8 %shard_map.273 = (f32[256,1024]{1,0:T(8,128)}, f32[64,4096]{1,0:T(8,128)}, f32[64,1024]{1,0:T(8,128)}, f32[64,3072]{1,0:T(8,128)}, f32[8,1024]{1,0:T(8,128)}) custom-call(bf16[4096,192]{1,0:T(8,128)(2,1)} %get-tuple-element.44.refs_0_, bf16[1024,192]{1,0:T(8,128)(2,1)} %get-tuple-element.45.refs_1_, bf16[1024,192]{1,0:T(8,128)(2,1)} %get-tuple-element.46.refs_2_, ...), custom_call_target="tpu_custom_call" | custom-call | tf_op jit(solution)/shard_map/pallas_call | solution.py:489
  298.8 0.0 copy-start.5
  298.8 0.0 copy-start.2
  298.8 1.4 fusion.2
  300.2 1.3 slice.62
  301.5 0.0 copy-done.4
  301.5 0.7 copy.47
  302.2 0.0 copy-done.3
  302.2 0.7 copy.48
  303.0 0.0 copy-start.1
  303.0 2.2 copy.49
  305.1 0.0 copy-done.5
  305.2 0.7 copy.50
  305.9 0.0 copy-done.2
  305.9 1.0 copy.51
  306.8 0.0 copy-done.1
  306.8 1.0 copy.52
  (14 shorter events, 0.2 us)
Async XLA Ops:
  0.6 86.3 %copy-start.7 = (s32[192]{0:T(256)S(1)}, s32[192]{0:T(256)}, u32[]{:S(2)}) copy-start(s32[192]{0:T(256)} %param.18) | copy-start | bytes 2308
  0.7 86.3 %copy-start = (bf16[1,192,1024]{2,1,0:T(8,128)(2,1)S(1)}, bf16[1,192,1024]{2,1,0:T(8,128)(2,1)}, u32[]{:S(2)}) copy-start(bf16[1,192,1024]{2,1,0:T(8,128)(2,1)} %param.16) | copy-start | bytes 1179652
  0.7 87.2 %copy-start.6 = (s32[192]{0:T(256)S(1)}, s32[192]{0:T(256)}, u32[]{:S(2)}) copy-start(s32[192]{0:T(256)} %param.17) | copy-start | bytes 2308
  178.9 122.5 %copy-start.4 = (bf16[192,1024]{1,0:T(8,128)(2,1)S(1)}, bf16[192,1024]{1,0:T(8,128)(2,1)}, u32[]{:S(2)}) copy-start(bf16[192,1024]{1,0:T(8,128)(2,1)} %get-tuple-element.42) | copy-start | bytes 1179652
  178.9 123.3 %copy-start.3 = (bf16[192,1024]{1,0:T(8,128)(2,1)S(1)}, bf16[192,1024]{1,0:T(8,128)(2,1)}, u32[]{:S(2)}) copy-start(bf16[192,1024]{1,0:T(8,128)(2,1)} %get-tuple-element.43) | copy-start | bytes 1179652
  298.8 6.3 %copy-start.5 = (f32[64,1024]{1,0:T(8,128)S(1)}, f32[64,1024]{1,0:T(8,128)}, u32[]{:S(2)}) copy-start(f32[64,1024]{1,0:T(8,128)} %get-tuple-element.56) | copy-start | bytes 786436
  298.8 7.0 %copy-start.2 = (f32[64,4096]{1,0:T(8,128)S(1)}, f32[64,4096]{1,0:T(8,128)}, u32[]{:S(2)}) copy-start(f32[64,4096]{1,0:T(8,128)} %get-tuple-element.57) | copy-start | bytes 3145732
  303.0 3.8 %copy-start.1 = (f32[256,1024]{1,0:T(8,128)S(1)}, f32[256,1024]{1,0:T(8,128)}, u32[]{:S(2)}) copy-start(f32[256,1024]{1,0:T(8,128)} %get-tuple-element.58) | copy-start | bytes 3145732
